TPU v7x, 128 devices: a whole 4x4x4 slice. The times are simulated.
128 devices in a mesh: tm: 16 (over y, x_lo, core), tile: 8 (over x_hi, z).
Axes of the slice: x: 4 (x_hi: 2, x_lo: 2; x = x_hi * 2 + x_lo), y: 4, z: 4, core: 2. Of those that a mesh axis runs over, the one named last changes fastest.
Arguments:
- adjoint: bfloat16 [5120, 131072], P('tm', 'tile'), may hold values from -6 to 6
- emission: bfloat16 [5120, 131072], P('tm', 'tile'), may hold values from 0.29882812 to 3
- step_weights: float32 [5120], P('tm'), may hold values from 0.0041926275 to 0.041926276
- tile_list: int32 [4096, 2], P('tile'), may hold values from 0 to 1023, as said below
- counts: int32 [8], P('tile'), may hold values from 256 to 512, as said below
Outputs:
- coupling_grad: float32 [8, 512, 128, 128], P('tile', 'tm')
Inputs may be any that keep to these rules, and one draw needn't show every extreme that they name: Slot k of owner o is tile_list[o * 512 + k]; its row block lies in owner o's range o * 128 to (o + 1) * 128 - 1. For every owner and every other owner, the live slots of the first name exactly 4 distinct column blocks in the range of the second. The live slots of owner o are its first counts[o] slots; some owner has all 512 slots live.
All inputs are finite; a program needn't handle non-finite values.
Results may differ from a plain program's by a relative error of at most 0.009.
Values may be sent and summed in bfloat16 or wider, within the bound.
No kernel may reach another device: no remote copies, remote signals or barrier semaphores. Data moves between devices by JAX's collectives and lax.ppermute only.
A program may use at most 256 MiB of HBM per device.

v0:
```python
import functools

import jax
import jax.numpy as jnp
from jax import lax
from jax.experimental import pallas as pl
from jax.experimental.pallas import tpu as pltpu
from jax.sharding import PartitionSpec as P

BLK = 128
CAP = 4
GRP = 32
KA = 384
F32 = jnp.float32
BF16 = jnp.bfloat16
I32 = jnp.int32


def iota(shape, dim):
    return lax.broadcasted_iota(I32, shape, dim)


def in_hbm(a):
    return pltpu.with_memory_space_constraint(a, pltpu.HBM)


def plan_kernel(early, own_ref, count_ref, tiles_ref, request_ref, table_ref):
    slots = tiles_ref.shape[0]
    own = own_ref[0]
    r = tiles_ref[:, 0:1]
    c = tiles_ref[:, 1:2]
    k = iota((slots, 1), 0)
    src = c >> 7
    within = c & (BLK - 1)
    row = r & (BLK - 1)
    remote = (k < count_ref[0]) & (src != own)
    lane = iota((slots, BLK), 1)
    by_src = jnp.where((lane == src) & remote, 1.0, 0.0).astype(F32)
    by_block = jnp.where(lane == within, 1.0, 0.0).astype(F32)
    named = jnp.dot(by_src.T.astype(BF16), by_block.astype(BF16), preferred_element_type=F32)
    hit = jnp.where(named > 0.0, 1.0, 0.0).astype(F32)
    upper = jnp.where(iota((BLK, BLK), 0) <= iota((BLK, BLK), 1), 1.0, 0.0).astype(BF16)
    rank = jnp.dot(hit.astype(BF16), upper, preferred_element_type=F32) * hit
    slot_rank = jnp.sum(
        jnp.dot(by_src.astype(BF16), rank.astype(BF16), preferred_element_type=F32) * by_block,
        axis=1,
        keepdims=True,
    )
    slot_rank = jnp.clip(slot_rank.astype(I32) - 1, 0, CAP - 1)
    col = jnp.where(remote, BLK + src * CAP + slot_rank, within)

    jj = iota((slots, slots), 1)
    kk = iota((slots, slots), 0)
    same = (jj >> 5) == (kk >> 5)
    remote_f = jnp.broadcast_to(jnp.where(remote, 1.0, 0.0), (slots, BLK)).astype(BF16)
    ahead = jnp.where(same & (jj < kk), 1.0, 0.0).astype(BF16)
    ahead = jnp.dot(ahead, remote_f, preferred_element_type=F32)[:, 0:1].astype(I32)
    total = jnp.where(same, 1.0, 0.0).astype(BF16)
    total = jnp.dot(total, remote_f, preferred_element_type=F32)[:, 0:1].astype(I32)
    s = k & (GRP - 1)
    pos = jnp.where(remote, GRP - total + ahead, s - ahead)
    value = jnp.where(lane < GRP, row, jnp.where(lane < 2 * GRP, col, s))
    value = jnp.where((lane & (GRP - 1)) == pos, value, 0)
    value = jnp.where(lane < 3 * GRP, value, 0).astype(F32).astype(BF16)
    groups = slots // GRP
    pick = jnp.where((iota((groups, slots), 1) >> 5) == iota((groups, slots), 0), 1.0, 0.0)
    table_ref[...] = jnp.dot(pick.astype(BF16), value, preferred_element_type=F32).astype(I32)

    late = jnp.max(jnp.where(total > GRP - early, 1, 0), axis=0, keepdims=True)
    owners = request_ref.shape[0]
    hit8 = hit[0:owners, :]
    rank8 = rank[0:owners, :]
    lane8 = iota((owners, BLK), 1)
    request = jnp.where(lane8 == CAP, jnp.broadcast_to(late, (owners, BLK)), 0)
    for q in range(CAP):
        block = jnp.sum(
            jnp.where((rank8 == q + 1.0) & (hit8 > 0.0), lane8, 0), axis=1, keepdims=True
        )
        request = jnp.where(lane8 == q, block, request)
    request_ref[...] = request


def plan(own, counts, tile_list, owners, early):
    slots = tile_list.shape[0]
    smem = pl.BlockSpec(memory_space=pltpu.SMEM)
    vmem = pl.BlockSpec(memory_space=pltpu.VMEM)
    return pl.pallas_call(
        functools.partial(plan_kernel, early),
        in_specs=[smem, smem, vmem],
        out_specs=[vmem, vmem],
        out_shape=[
            jax.ShapeDtypeStruct((owners, BLK), I32),
            jax.ShapeDtypeStruct((slots // GRP, BLK), I32),
        ],
        compiler_params=pltpu.CompilerParams(vmem_limit_bytes=16 * 2**20),
        name="plan",
    )(own, counts, tile_list)


STEP = 16
DEPTH = 3


def prep_kernel(with_far, weights_ref, adj_ref, em_ref, *refs):
    if with_far:
        far_ref, refs = refs[0], refs[1:]
        refs, fsem = refs[:-1], refs[-1]
    wt_ref, e_ref, abuf, ebuf, wide, asem, esem = refs
    steps = adj_ref.shape[0]
    blocks = wt_ref.shape[0]
    chunks = blocks // STEP
    wide[...] = jnp.broadcast_to(weights_ref[...], wide.shape)

    def copies(j):
        slot = lax.rem(j, DEPTH)
        cols = pl.ds(pl.multiple_of(j * (STEP * BLK), STEP * BLK), STEP * BLK)
        return (
            pltpu.make_async_copy(adj_ref.at[:, cols], abuf.at[slot], asem.at[slot]),
            pltpu.make_async_copy(em_ref.at[:, cols], ebuf.at[slot], esem.at[slot]),
        )

    for j in range(DEPTH - 1):
        for copy in copies(j):
            copy.start()
    if with_far:
        rest = pl.ds(blocks, e_ref.shape[0] - blocks)
        far_copy = pltpu.make_async_copy(far_ref, e_ref.at[rest, pl.ds(0, steps)], fsem)
        far_copy.start()
    ones = jnp.where(iota((KA - steps, BLK), 0) < 2, 1.0, 0.0).astype(BF16)
    rows = iota((KA - steps, BLK), 0)

    def chunk(j, carry):
        slot = lax.rem(j, DEPTH)

        @pl.when(j + DEPTH - 1 < chunks)
        def _():
            for copy in copies(j + DEPTH - 1):
                copy.start()

        for copy in copies(j):
            copy.wait()
        for b in range(STEP):
            at = j * STEP + b
            w = (wide[...] * abuf[slot, :, b * BLK : (b + 1) * BLK].astype(F32)).astype(BF16)
            e = ebuf[slot, :, b * BLK : (b + 1) * BLK]
            sums = -jnp.sum(w.astype(F32) * e.astype(F32), axis=0, keepdims=True)
            high = sums.astype(BF16).astype(F32)
            low = sums - high
            tail = jnp.where(rows == 0, high, jnp.where(rows == 1, low, 0.0)).astype(BF16)
            wt_ref[at] = jnp.concatenate([w, tail], axis=0).T
            e_ref[at, 0:steps, :] = e
            e_ref[at, steps:KA, :] = ones
        return carry

    lax.fori_loop(0, chunks, chunk, 0)
    if with_far:
        for i in range(blocks, e_ref.shape[0]):
            e_ref[i, steps:KA, :] = ones
        far_copy.wait()


def prep(weights, adjoint, emission, far=None):
    steps, nodes = adjoint.shape
    blocks = nodes // BLK
    anyspace = pl.BlockSpec(memory_space=pl.ANY)
    vmem = pl.BlockSpec(memory_space=pltpu.VMEM)
    with_far = far is not None
    columns = blocks + (far.shape[0] if with_far else 0)
    wt, e_blocks = pl.pallas_call(
        functools.partial(prep_kernel, with_far),
        in_specs=[vmem] + [anyspace] * (3 if with_far else 2),
        out_specs=[vmem, vmem],
        out_shape=[
            pltpu.VMEM((blocks, BLK, KA), BF16),
            pltpu.VMEM((columns, KA, BLK), BF16),
        ],
        scratch_shapes=[
            pltpu.VMEM((DEPTH, steps, STEP * BLK), BF16),
            pltpu.VMEM((DEPTH, steps, STEP * BLK), BF16),
            pltpu.VMEM((steps, BLK), F32),
            pltpu.SemaphoreType.DMA((DEPTH,)),
            pltpu.SemaphoreType.DMA((DEPTH,)),
        ]
        + ([pltpu.SemaphoreType.DMA] if with_far else []),
        compiler_params=pltpu.CompilerParams(vmem_limit_bytes=14 * 2**20),
        name="prep",
    )(weights, in_hbm(adjoint), in_hbm(emission), *([in_hbm(far)] if with_far else []))
    return (
        pltpu.with_memory_space_constraint(wt, pltpu.VMEM),
        pltpu.with_memory_space_constraint(e_blocks, pltpu.VMEM),
    )


def pack_kernel(asked_ref, em_ref, out_ref, sems):
    count = out_ref.shape[0]

    def copy(i):
        block = asked_ref[i >> 2, i & (CAP - 1)] & (BLK - 1)
        cols = pl.ds(pl.multiple_of(block * BLK, BLK), BLK)
        return pltpu.make_async_copy(em_ref.at[:, cols], out_ref.at[i], sems.at[i])

    for i in range(count):
        copy(i).start()
    for i in range(count):
        copy(i).wait()


def pack(asked, emission):
    owners = asked.shape[0]
    return pl.pallas_call(
        pack_kernel,
        in_specs=[pl.BlockSpec(memory_space=pltpu.SMEM), pl.BlockSpec(memory_space=pl.ANY)],
        out_specs=pl.BlockSpec(memory_space=pltpu.VMEM),
        out_shape=jax.ShapeDtypeStruct((owners * CAP, emission.shape[0], BLK), BF16),
        scratch_shapes=[pltpu.SemaphoreType.DMA((owners * CAP,))],
        compiler_params=pltpu.CompilerParams(vmem_limit_bytes=8 * 2**20),
        name="pack",
    )(asked, in_hbm(emission))


def tiles_kernel(first, per, with_add, *refs):
    groups_ref, places_ref, table_ref, wt_ref, e_ref = refs[:5]
    outs = refs[6:] if with_add else refs[5:]
    last = e_ref.shape[0] - 1
    n = 0
    for out_ref in outs:
        for j in range(out_ref.shape[0] // per):
            g = groups_ref[n]
            for q in range(per):
                row = table_ref[g, first + q]
                col = jnp.minimum(table_ref[g, GRP + first + q], last)
                acc = jnp.dot(wt_ref[row], e_ref[col], preferred_element_type=F32)
                if with_add:
                    acc = acc + refs[5][places_ref[n] * per + q].astype(F32)
                out_ref[j * per + q] = acc.astype(BF16)
            n += 1


def tiles(groups, places, table, wt, e_blocks, first, per, outs, add=None):
    smem = pl.BlockSpec(memory_space=pltpu.SMEM)
    vmem = pl.BlockSpec(memory_space=pltpu.VMEM)
    count = groups.shape[0] * per
    with_add = add is not None
    return pl.pallas_call(
        functools.partial(tiles_kernel, first, per, with_add),
        in_specs=[smem, smem, smem, vmem, vmem] + ([vmem] if with_add else []),
        out_specs=[vmem] * outs,
        out_shape=[jax.ShapeDtypeStruct((count // outs, BLK, BLK), BF16)] * outs,
        compiler_params=pltpu.CompilerParams(vmem_limit_bytes=10 * 2**20),
        name="tiles",
    )(groups, places, table, wt, e_blocks, *([add] if with_add else []))


def add_kernel(n, *refs):
    for i in range(n):
        mine, came = refs[2 * i], refs[2 * i + 1]
        sent, kept = refs[2 * n + 2 * i], refs[2 * n + 2 * i + 1]
        half = sent.shape[0]

        def one(j, carry, mine=mine, came=came, sent=sent, kept=kept, half=half):
            sent[j] = (mine[j].astype(F32) + came[j].astype(F32)).astype(BF16)
            kept[j] = (mine[half + j].astype(F32) + came[half + j].astype(F32)).astype(BF16)
            return carry

        lax.fori_loop(0, half, one, 0, unroll=2)


def add_pairs(pairs):
    vmem = pl.BlockSpec(memory_space=pltpu.VMEM)
    shapes = []
    for mine, _ in pairs:
        shapes += [jax.ShapeDtypeStruct((mine.shape[0] // 2, BLK, BLK), BF16)] * 2
    flat = [a for pair in pairs for a in pair]
    return pl.pallas_call(
        functools.partial(add_kernel, len(pairs)),
        in_specs=[vmem] * len(flat),
        out_specs=[vmem] * len(shapes),
        out_shape=shapes,
        compiler_params=pltpu.CompilerParams(vmem_limit_bytes=20 * 2**20),
        name="add_pairs",
    )(*flat)


def finish_kernel(firsts, me_ref, count_ref, table_ref, *refs):
    me = me_ref[0]
    out_ref, stage, sem = refs[-3:]
    for i, first in enumerate(firsts):
        mine, came = refs[2 * i], refs[2 * i + 1]
        for j in range(mine.shape[0]):
            s = table_ref[me, 2 * GRP + first + j]
            live = jnp.where(me * GRP + s < count_ref[0], 1.0, 0.0).astype(F32)
            stage[first + j] = (mine[j].astype(F32) + came[j].astype(F32)) * live
            pltpu.make_async_copy(stage.at[first + j], out_ref.at[s], sem).start()
    pltpu.make_async_copy(stage, out_ref, sem).wait()


def finish(me, counts, table, pairs, firsts):
    smem = pl.BlockSpec(memory_space=pltpu.SMEM)
    vmem = pl.BlockSpec(memory_space=pltpu.VMEM)
    flat = [a for pair in pairs for a in pair]
    return pl.pallas_call(
        functools.partial(finish_kernel, firsts),
        in_specs=[smem, smem, smem] + [vmem] * len(flat),
        out_specs=pl.BlockSpec(memory_space=pltpu.HBM),
        out_shape=pltpu.HBM((GRP, BLK, BLK), F32),
        scratch_shapes=[pltpu.VMEM((GRP, BLK, BLK), F32), pltpu.SemaphoreType.DMA],
        compiler_params=pltpu.CompilerParams(vmem_limit_bytes=16 * 2**20),
        name="finish",
    )(me, counts, table, *flat)


CORE, ALONG_X, UP_Y, DOWN_Y = 1, 2, 4, 12
ORDERS = (
    (ALONG_X, UP_Y, DOWN_Y),
    (UP_Y, DOWN_Y, ALONG_X),
    (DOWN_Y, ALONG_X, UP_Y),
)


def swap(a, mask):
    n = lax.axis_size("tm")
    return lax.ppermute(a, "tm", [(i, i ^ mask) for i in range(n)])


def after(a, other):
    return lax.optimization_barrier((a, other))[0]


def order_masks(order, lead):
    first, second, third = order
    return [lead * first ^ s * second ^ t * third for s in (1, 0) for t in (1, 0)]


def body(adjoint, emission, step_weights, tile_list, counts):
    owners = lax.axis_size("tile")
    parts = lax.axis_size("tm")
    own = lax.axis_index("tile").astype(I32).reshape(1)
    me = lax.axis_index("tm").astype(I32).reshape(1)
    half = GRP // 2
    request, table = plan(own, counts, tile_list, owners, half)
    asked = lax.all_to_all(request, "tile", split_axis=0, concat_axis=0, tiled=True)
    outgoing = pack(asked, emission)
    far = lax.all_to_all(outgoing, "tile", split_axis=0, concat_axis=0, tiled=True)
    crowded = jnp.any(asked[:, CAP] > 0)
    weights = after(step_weights[:, None], crowded)

    cuts = (6, 5, 5)
    others = me ^ CORE ^ (2 * jnp.arange(parts // 2, dtype=I32))
    offsets = [[c * half + sum(cuts[:i]) for i in range(len(cuts))] for c in range(2)]

    def given(c, i, wt, e_blocks, last):
        return tiles(
            after(others, last), others, table, wt, e_blocks, offsets[c][i], cuts[i], 1
        )[0]

    def kept(c, i, wt, e_blocks, last, core):
        masks = [m for lead in (1, 0) for m in order_masks(ORDERS[i], lead)]
        mine = me ^ jnp.array(masks, I32)
        places = jnp.array([m // 2 for m in masks], I32)
        return tiles(
            after(mine, last), places, table, wt, e_blocks, offsets[c][i], cuts[i], 2, core
        )

    def exchange(outs, step):
        return [(out[1], swap(out[0], order[step])) for out, order in zip(outs, ORDERS)]

    def halve(pairs, last):
        outs = []
        for mine, came in pairs:
            out = add_pairs([(after(mine, last), came)])
            last = out[1]
            outs.append(out)
        return outs, last

    def first_kernels(c, wt, e_blocks):
        last, cores = wt, []
        for i in range(3):
            last = given(c, i, wt, e_blocks, last)
            cores.append(swap(last, CORE))
        return cores, last

    def second_kernels(c, wt, e_blocks, cores, last):
        outs = []
        for i in range(3):
            outs.append(kept(c, i, wt, e_blocks, last, cores[i]))
            last = outs[i][1]
        return outs, last

    wt, e_blocks = prep(after(weights, outgoing), adjoint, emission)
    cores, last = first_kernels(0, wt, e_blocks)
    early, last = second_kernels(0, wt, e_blocks, cores, last)
    early = exchange(early, 0)
    wt, e_blocks = prep(after(weights, last), adjoint, emission, far)
    cores, last = [], wt
    for i in range(3):
        last = given(1, i, wt, e_blocks, last)
        cores.append(swap(last, CORE))
        if i == 0:
            early, last = halve(early, last)
            early = exchange(early, 1)
    late = []
    for i in range(3):
        if i == 2:
            early, last = halve(early, last)
            early = exchange(early, 2)
        late.append(kept(1, i, wt, e_blocks, last, cores[i]))
        last = late[i][1]
    late = exchange(late, 0)
    late, last = halve(late, last)
    late, last = halve(exchange(late, 1), last)
    late = exchange(late, 2)
    firsts = tuple(offsets[0] + offsets[1])

    def crowded_group(early, late):
        wt, e_blocks = prep(weights, adjoint, emission, far)
        cores, last = first_kernels(0, wt, e_blocks)
        again, last = second_kernels(0, wt, e_blocks, cores, last)
        for step in range(2):
            again, last = halve(exchange(again, step), last)
        return finish(me, counts, table, exchange(again, 2) + late, firsts)

    def usual(early, late):
        return finish(me, counts, table, early + late, firsts)

    return lax.cond(crowded, crowded_group, usual, early, late)[None]


def solution(mesh):
    in_specs = (P("tm", "tile"), P("tm", "tile"), P("tm"), P("tile", None), P("tile"))
    out_specs = P("tile", "tm", None, None)
    return jax.shard_map(body, mesh=mesh, in_specs=in_specs, out_specs=out_specs, check_vma=False)
```

profile of v0, /device:TPU:0, one launch (start us, length us, event | category | flops | bytes accessed | tf_op | source)
XLA Modules:
  0.0 145.6 jit_solution(4673818821899089681)
XLA Ops:
  3.1 15.3 %all_to_all.16 = s32[8,1,128]{2,1,0:T(1,128)S(1)} all-to-all(s32[8,1,128]{2,1,0:T(1,128)S(1)} %bitcast.12), channel_id=1, replica_groups=mesh['tm'=16,'tile'=8] {'tile'}, dimensions={0} | all-to-all | bytes 8192 | tf_op jit(solution)/shard_map/all_to_all | solution.py:341
  18.4 4.2 %pack.1 = bf16[32,320,128]{2,1,0:T(8,128)(2,1)} custom-call(s32[8,128]{1,0:T(8,128)S(1)} %bitcast.10, bf16[320,16384]{1,0:T(8,128)(2,1)} %em_ref.5), custom_call_target="tpu_custom_call" | custom-call | tf_op jit(solution)/shard_map/pack/pallas_call | solution.py:210
  22.6 4.4 %all-to-all-start.1 = ((bf16[32,320,128]{2,1,0:T(8,128)(2,1)}), bf16[32,320,128]{2,1,0:T(8,128)(2,1)}, u32[]{:S(2)}, u32[]{:S(2)}) async-start(bf16[32,320,128]{2,1,0:T(8,128)(2,1)} %pack.1), calls=%async_computation.1 | async-start | bytes 5242880 | tf_op jit(solution)/shard_map/all_to_all | solution.py:343
  28.0 8.9 %prep.4 = (bf16[128,128,384]{2,1,0:T(8,128)(2,1)S(1)}, bf16[128,384,128]{2,1,0:T(8,128)(2,1)S(1)}) custom-call(f32[320,1]{1,0:T(8,128)S(1)} %copy.33.weights_ref, bf16[320,16384]{1,0:T(8,128)(2,1)} %adj_ref.3, bf16[320,16384]{1,0:T(8,128)(2,1)} %em_ref.5), custom_call_target="tpu_custom_call" | custom-call | tf_op jit(solution)/shard_map/prep/pallas_call | solution.py:169
  36.9 2.1 %tiles.24 = bf16[48,128,128]{2,1,0:T(8,128)(2,1)S(1)} custom-call(s32[8]{0:T(128)S(1)} %multiply_xor_fusion.refs_0_.refs_1_, s32[8]{0:T(128)S(1)} %multiply_xor_fusion.refs_0_.refs_1_, s32[16,128]{1,0:T(8,128)S(1)} %get-tuple-element.216.refs_2_, bf16[128,128,384]{2,1,0:T(8,128)(2,1)S(1)} %get-tuple-element.219.refs_3_, ...), custom_call_target="tpu_custom_call" | custom-call | tf_op jit(solution)/shard_map/tiles/pallas_call | solution.py:244
  39.1 1.9 %tiles.25 = bf16[40,128,128]{2,1,0:T(8,128)(2,1)S(1)} custom-call(s32[8]{0:T(128)S(1)} %multiply_xor_fusion.refs_0_.refs_1_, s32[8]{0:T(128)S(1)} %multiply_xor_fusion.refs_0_.refs_1_, s32[16,128]{1,0:T(8,128)S(1)} %get-tuple-element.216.refs_2_, bf16[128,128,384]{2,1,0:T(8,128)(2,1)S(1)} %get-tuple-element.219.refs_3_, ...), custom_call_target="tpu_custom_call" | custom-call | tf_op jit(solution)/shard_map/tiles/pallas_call | solution.py:244
  41.6 1.9 %tiles.26 = bf16[40,128,128]{2,1,0:T(8,128)(2,1)S(1)} custom-call(s32[8]{0:T(128)S(1)} %multiply_xor_fusion.refs_0_.refs_1_, s32[8]{0:T(128)S(1)} %multiply_xor_fusion.refs_0_.refs_1_, s32[16,128]{1,0:T(8,128)S(1)} %get-tuple-element.216.refs_2_, bf16[128,128,384]{2,1,0:T(8,128)(2,1)S(1)} %get-tuple-element.219.refs_3_, ...), custom_call_target="tpu_custom_call" | custom-call | tf_op jit(solution)/shard_map/tiles/pallas_call | solution.py:244
  43.6 2.8 %tiles.27 = (bf16[24,128,128]{2,1,0:T(8,128)(2,1)}, bf16[24,128,128]{2,1,0:T(8,128)(2,1)S(1)}) custom-call(s32[8]{0:T(128)S(1)} %broadcast_xor_fusion.5.refs_0_, s32[8]{0:T(128)S(1)} %copy-done.4, s32[16,128]{1,0:T(8,128)S(1)} %get-tuple-element.216.refs_2_, bf16[128,128,384]{2,1,0:T(8,128)(2,1)S(1)} %get-tuple-element.219.refs_3_, ...), custom_call_target="tpu_custom_call" | custom-call | tf_op jit(solution)/shard_map/tiles/pallas_call | solution.py:244
  47.0 2.5 %tiles.28 = (bf16[20,128,128]{2,1,0:T(8,128)(2,1)}, bf16[20,128,128]{2,1,0:T(8,128)(2,1)S(1)}) custom-call(s32[8]{0:T(128)S(1)} %broadcast_xor_fusion.3.refs_0_, s32[8]{0:T(128)S(1)} %copy-done.5, s32[16,128]{1,0:T(8,128)S(1)} %get-tuple-element.216.refs_2_, bf16[128,128,384]{2,1,0:T(8,128)(2,1)S(1)} %get-tuple-element.219.refs_3_, ...), custom_call_target="tpu_custom_call" | custom-call | tf_op jit(solution)/shard_map/tiles/pallas_call | solution.py:244
  49.5 1.8 %collective-permute-start.16 = (bf16[20,128,128]{2,1,0:T(8,128)(2,1)}, bf16[20,128,128]{2,1,0:T(8,128)(2,1)}, u32[]{:S(2)}, u32[]{:S(2)}) collective-permute-start(bf16[20,128,128]{2,1,0:T(8,128)(2,1)} %get-tuple-element.238), channel_id=1, source_target_pairs={{0,32},{8,40},{16,48},{24,56},{32,0},{40,8},{48,16},{56,24},{64,96... | collective-permute-start | bytes 1966088 | tf_op jit(solution)/shard_map/ppermute | solution.py:322
  51.4 2.6 %tiles.29 = (bf16[20,128,128]{2,1,0:T(8,128)(2,1)}, bf16[20,128,128]{2,1,0:T(8,128)(2,1)S(1)}) custom-call(s32[8]{0:T(128)S(1)} %broadcast_xor_fusion.4.refs_0_, s32[8]{0:T(128)S(1)} %copy-done.6, s32[16,128]{1,0:T(8,128)S(1)} %get-tuple-element.216.refs_2_, bf16[128,128,384]{2,1,0:T(8,128)(2,1)S(1)} %get-tuple-element.219.refs_3_, ...), custom_call_target="tpu_custom_call" | custom-call | tf_op jit(solution)/shard_map/tiles/pallas_call | solution.py:244
  54.8 2.2 %collective-permute-start.17 = (bf16[20,128,128]{2,1,0:T(8,128)(2,1)}, bf16[20,128,128]{2,1,0:T(8,128)(2,1)S(1)}, u32[]{:S(2)}, u32[]{:S(2)}) collective-permute-start(bf16[20,128,128]{2,1,0:T(8,128)(2,1)} %get-tuple-element.241), channel_id=1, source_target_pairs={{0,96},{8,104},{16,112},{24,120},{32,64},{40,72},{48,80},{56,88},{... | collective-permute-start | bytes 1966088 | tf_op jit(solution)/shard_map/ppermute | solution.py:322
  57.1 3.4 %all-to-all-done.1.refs_0_ = bf16[32,320,128]{2,1,0:T(8,128)(2,1)} async-done(((bf16[32,320,128]{2,1,0:T(8,128)(2,1)}), bf16[32,320,128]{2,1,0:T(8,128)(2,1)}, u32[]{:S(2)}, u32[]{:S(2)}) %all-to-all-start.1) | async-done | bytes 2621472 | tf_op jit(solution)/shard_map/all_to_all | solution.py:343
  60.5 9.5 %prep.5 = (bf16[128,128,384]{2,1,0:T(8,128)(2,1)S(1)}, bf16[160,384,128]{2,1,0:T(8,128)(2,1)S(1)}) custom-call(f32[320,1]{1,0:T(8,128)S(1)} %copy.34.weights_ref, bf16[320,16384]{1,0:T(8,128)(2,1)} %adj_ref.3, bf16[320,16384]{1,0:T(8,128)(2,1)} %em_ref.5, bf16[32,320,128]{2,1,0:T(8,128)(2,1)} %all-to-all-done.1.refs_0_), custom_call_target="tpu_custom_call" | custom-call | tf_op jit(solution)/shard_map/prep/pallas_call | solution.py:169
  70.0 2.1 %tiles.30 = bf16[48,128,128]{2,1,0:T(8,128)(2,1)S(1)} custom-call(s32[8]{0:T(128)S(1)} %multiply_xor_fusion.refs_0_.refs_1_, s32[8]{0:T(128)S(1)} %multiply_xor_fusion.refs_0_.refs_1_, s32[16,128]{1,0:T(8,128)S(1)} %get-tuple-element.216.refs_2_, bf16[128,128,384]{2,1,0:T(8,128)(2,1)S(1)} %get-tuple-element.231.refs_3_, ...), custom_call_target="tpu_custom_call" | custom-call | tf_op jit(solution)/shard_map/tiles/pallas_call | solution.py:244
  74.7 1.9 %tiles.31 = bf16[40,128,128]{2,1,0:T(8,128)(2,1)S(1)} custom-call(s32[8]{0:T(128)S(1)} %multiply_xor_fusion.refs_0_.refs_1_, s32[8]{0:T(128)S(1)} %multiply_xor_fusion.refs_0_.refs_1_, s32[16,128]{1,0:T(8,128)S(1)} %get-tuple-element.216.refs_2_, bf16[128,128,384]{2,1,0:T(8,128)(2,1)S(1)} %get-tuple-element.231.refs_3_, ...), custom_call_target="tpu_custom_call" | custom-call | tf_op jit(solution)/shard_map/tiles/pallas_call | solution.py:244
  76.6 1.9 %tiles.32 = bf16[40,128,128]{2,1,0:T(8,128)(2,1)S(1)} custom-call(s32[8]{0:T(128)S(1)} %multiply_xor_fusion.refs_0_.refs_1_, s32[8]{0:T(128)S(1)} %multiply_xor_fusion.refs_0_.refs_1_, s32[16,128]{1,0:T(8,128)S(1)} %get-tuple-element.216.refs_2_, bf16[128,128,384]{2,1,0:T(8,128)(2,1)S(1)} %get-tuple-element.231.refs_3_, ...), custom_call_target="tpu_custom_call" | custom-call | tf_op jit(solution)/shard_map/tiles/pallas_call | solution.py:244
  80.7 2.2 %collective-permute-start.22 = (bf16[10,128,128]{2,1,0:T(8,128)(2,1)S(1)}, bf16[10,128,128]{2,1,0:T(8,128)(2,1)S(1)}, u32[]{:S(2)}, u32[]{:S(2)}) collective-permute-start(bf16[10,128,128]{2,1,0:T(8,128)(2,1)S(1)} %get-tuple-element.254), channel_id=1, source_target_pairs={{0,96},{8,104},{16,112},{24,120},{32,64},{40,72},{48,80},{56,88},{... | collective-permute-start | bytes 983048 | tf_op jit(solution)/shard_map/ppermute | solution.py:322
  83.4 2.1 %tiles.33 = (bf16[24,128,128]{2,1,0:T(8,128)(2,1)S(1)}, bf16[24,128,128]{2,1,0:T(8,128)(2,1)S(1)}) custom-call(s32[8]{0:T(128)S(1)} %broadcast_xor_fusion.5.refs_0_, s32[8]{0:T(128)S(1)} %copy-done.4, s32[16,128]{1,0:T(8,128)S(1)} %get-tuple-element.216.refs_2_, bf16[128,128,384]{2,1,0:T(8,128)(2,1)S(1)} %get-tuple-element.231.refs_3_, ...), custom_call_target="tpu_custom_call" | custom-call | tf_op jit(solution)/shard_map/tiles/pallas_call | solution.py:244
  87.0 1.9 %tiles.34 = (bf16[20,128,128]{2,1,0:T(8,128)(2,1)S(1)}, bf16[20,128,128]{2,1,0:T(8,128)(2,1)S(1)}) custom-call(s32[8]{0:T(128)S(1)} %broadcast_xor_fusion.3.refs_0_, s32[8]{0:T(128)S(1)} %copy-done.5, s32[16,128]{1,0:T(8,128)S(1)} %get-tuple-element.216.refs_2_, bf16[128,128,384]{2,1,0:T(8,128)(2,1)S(1)} %get-tuple-element.231.refs_3_, ...), custom_call_target="tpu_custom_call" | custom-call | tf_op jit(solution)/shard_map/tiles/pallas_call | solution.py:244
  91.4 12.6 %collective-permute-start.28 = (bf16[20,128,128]{2,1,0:T(8,128)(2,1)S(1)}, bf16[20,128,128]{2,1,0:T(8,128)(2,1)S(1)}, u32[]{:S(2)}, u32[]{:S(2)}) collective-permute-start(bf16[20,128,128]{2,1,0:T(8,128)(2,1)S(1)} %get-tuple-element.267), channel_id=1, source_target_pairs={{0,32},{8,40},{16,48},{24,56},{32,0},{40,8},{48,16},{56,24},{64,96... | collective-permute-start | bytes 1966088 | tf_op jit(solution)/shard_map/ppermute | solution.py:322
  104.1 1.9 %tiles.35 = (bf16[20,128,128]{2,1,0:T(8,128)(2,1)S(1)}, bf16[20,128,128]{2,1,0:T(8,128)(2,1)S(1)}) custom-call(s32[8]{0:T(128)S(1)} %broadcast_xor_fusion.4.refs_0_, s32[8]{0:T(128)S(1)} %copy-done.6, s32[16,128]{1,0:T(8,128)S(1)} %get-tuple-element.216.refs_2_, bf16[128,128,384]{2,1,0:T(8,128)(2,1)S(1)} %get-tuple-element.231.refs_3_, ...), custom_call_target="tpu_custom_call" | custom-call | tf_op jit(solution)/shard_map/tiles/pallas_call | solution.py:244
  106.0 2.3 %collective-permute-start.29 = (bf16[20,128,128]{2,1,0:T(8,128)(2,1)S(1)}, bf16[20,128,128]{2,1,0:T(8,128)(2,1)S(1)}, u32[]{:S(2)}, u32[]{:S(2)}) collective-permute-start(bf16[20,128,128]{2,1,0:T(8,128)(2,1)S(1)} %get-tuple-element.270), channel_id=1, source_target_pairs={{0,96},{8,104},{16,112},{24,120},{32,64},{40,72},{48,80},{56,88},{... | collective-permute-start | bytes 1966088 | tf_op jit(solution)/shard_map/ppermute | solution.py:322
  109.8 11.3 %collective-permute-done.28.refs_1_ = bf16[20,128,128]{2,1,0:T(8,128)(2,1)S(1)} collective-permute-done((bf16[20,128,128]{2,1,0:T(8,128)(2,1)S(1)}, bf16[20,128,128]{2,1,0:T(8,128)(2,1)S(1)}, u32[]{:S(2)}, u32[]{:S(2)}) %collective-permute-start.28) | collective-permute-done | bytes 655392 | tf_op jit(solution)/shard_map/ppermute | solution.py:322
  121.3 2.3 %collective-permute-start.32 = (bf16[10,128,128]{2,1,0:T(8,128)(2,1)S(1)}, bf16[10,128,128]{2,1,0:T(8,128)(2,1)S(1)}, u32[]{:S(2)}, u32[]{:S(2)}) collective-permute-start(bf16[10,128,128]{2,1,0:T(8,128)(2,1)S(1)} %get-tuple-element.277), channel_id=1, source_target_pairs={{0,96},{8,104},{16,112},{24,120},{32,64},{40,72},{48,80},{56,88},{... | collective-permute-start | bytes 983048 | tf_op jit(solution)/shard_map/ppermute | solution.py:322
  125.5 1.9 %collective-permute-done.30.refs_1_ = bf16[12,128,128]{2,1,0:T(8,128)(2,1)S(1)} collective-permute-done((bf16[12,128,128]{2,1,0:T(8,128)(2,1)S(1)}, bf16[12,128,128]{2,1,0:T(8,128)(2,1)S(1)}, u32[]{:S(2)}, u32[]{:S(2)}) %collective-permute-start.30) | collective-permute-done | bytes 393248 | tf_op jit(solution)/shard_map/ppermute | solution.py:322
  127.5 2.4 %collective-permute-done.32.refs_1_ = bf16[10,128,128]{2,1,0:T(8,128)(2,1)S(1)} collective-permute-done((bf16[10,128,128]{2,1,0:T(8,128)(2,1)S(1)}, bf16[10,128,128]{2,1,0:T(8,128)(2,1)S(1)}, u32[]{:S(2)}, u32[]{:S(2)}) %collective-permute-start.32) | collective-permute-done | bytes 327712 | tf_op jit(solution)/shard_map/ppermute | solution.py:322
  130.0 2.0 %collective-permute-done.34.refs_1_ = bf16[10,128,128]{2,1,0:T(8,128)(2,1)S(1)} collective-permute-done((bf16[10,128,128]{2,1,0:T(8,128)(2,1)S(1)}, bf16[10,128,128]{2,1,0:T(8,128)(2,1)S(1)}, u32[]{:S(2)}, u32[]{:S(2)}) %collective-permute-start.34) | collective-permute-done | bytes 327712 | tf_op jit(solution)/shard_map/ppermute | solution.py:322
  132.2 2.3 %collective-permute-start.31 = (bf16[6,128,128]{2,1,0:T(8,128)(2,1)S(1)}, bf16[6,128,128]{2,1,0:T(8,128)(2,1)S(1)}, u32[]{:S(2)}, u32[]{:S(2)}) collective-permute-start(bf16[6,128,128]{2,1,0:T(8,128)(2,1)S(1)} %get-tuple-element.275), channel_id=1, source_target_pairs={{0,96},{8,104},{16,112},{24,120},{32,64},{40,72},{48,80},{56,88},{... | collective-permute-start | bytes 589832 | tf_op jit(solution)/shard_map/ppermute | solution.py:322
  138.9 1.9 %collective-permute-done.33 = bf16[5,128,128]{2,1,0:T(8,128)(2,1)S(1)} collective-permute-done((bf16[5,128,128]{2,1,0:T(8,128)(2,1)S(1)}, bf16[5,128,128]{2,1,0:T(8,128)(2,1)S(1)}, u32[]{:S(2)}, u32[]{:S(2)}) %collective-permute-start.33) | collective-permute-done | bytes 163872 | tf_op jit(solution)/shard_map/ppermute | solution.py:322
  142.8 2.6 %conditional.1 = (f32[1,32,128,128]{3,2,1,0:T(8,128)}) conditional(s32[]{:T(128)} %convert_element_type.3, (s32[1]{0:T(128)}, s32[1]{0:T(128)}, s32[16,128]{1,0:T(8,128)S(1)}, bf16[6,128,128]{2,1,0:T(8,128)(2,1)S(1)}, bf16[6,128,128]{2,1,0:T(8,128)(2,1)S(1)}, /*index=5*/bf16[5,128,128]{2,1,0:T(8,128)(2,1)S(1)}, bf16[5,128,128]{2,1,0:T(8,128)(2,1)S(1)}, ...), branch_computations={%region_1.0_spmd, %region_2.0_spmd} | conditional | flops 24 | bytes 31460532 | solution.py:425
  142.8 2.6 %finish.2 = f32[32,128,128]{2,1,0:T(8,128)} custom-call(s32[1]{0:T(128)} %get-tuple-element.79.me_ref, s32[1]{0:T(128)} %get-tuple-element.80.count_ref, s32[16,128]{1,0:T(8,128)S(1)} %get-tuple-element.81.table_ref, bf16[6,128,128]{2,1,0:T(8,128)(2,1)S(1)} %get-tuple-element.82.refs_0_, bf16[6,128,128]{2,1,0:T(8,128)(2,1)S(1)} %get-tuple-element.83.refs_1_, ...), custom_call_target="tpu_custom_call" | custom-call | tf_op jit(solution)/shard_map/cond/branch_0_fun/finish/pallas_call | solution.py:301
  (80 shorter events, 24.9 us)
Async XLA Ops:
  22.6 4.5 %copy-start.7 = (f32[320]{0:T(512)S(1)}, f32[320]{0:T(512)}, u32[]{:S(2)}) copy-start(f32[320]{0:T(512)} %param.27) | copy-start | bytes 3844
  22.6 37.9 %all-to-all-start.1 = ((bf16[32,320,128]{2,1,0:T(8,128)(2,1)}), bf16[32,320,128]{2,1,0:T(8,128)(2,1)}, u32[]{:S(2)}, u32[]{:S(2)}) async-start(bf16[32,320,128]{2,1,0:T(8,128)(2,1)} %pack.1), calls=%async_computation.1 | async-start | bytes 5242880 | tf_op jit(solution)/shard_map/all_to_all | solution.py:343
  39.0 4.6 %collective-permute-start.12 = (bf16[48,128,128]{2,1,0:T(8,128)(2,1)S(1)}, bf16[48,128,128]{2,1,0:T(8,128)(2,1)S(1)}, u32[]{:S(2)}, u32[]{:S(2)}) collective-permute-start(bf16[48,128,128]{2,1,0:T(8,128)(2,1)S(1)} %tiles.24), channel_id=1, source_target_pairs={{0,8},{8,0},{16,24},{24,16},{32,40},{40,32},{48,56},{56,48},{64,72... | collective-permute-start | bytes 4718600 | tf_op jit(solution)/shard_map/ppermute | solution.py:322
  41.0 2.6 %copy-start.9 = (s32[8]{0:T(128)S(1)}, s32[8]{0:T(128)}, u32[]{:S(2)}) copy-start(s32[8]{0:T(128)} %constant.31.clone) | copy-start | bytes 100
  41.0 2.6 %copy-start.4 = (s32[8]{0:T(128)S(1)}, s32[8]{0:T(128)}, u32[]{:S(2)}) copy-start(s32[8]{0:T(128)} %constant.30.clone.refs_1_) | copy-start | bytes 100
  41.0 6.0 %collective-permute-start.13 = (bf16[40,128,128]{2,1,0:T(8,128)(2,1)S(1)}, bf16[40,128,128]{2,1,0:T(8,128)(2,1)S(1)}, u32[]{:S(2)}, u32[]{:S(2)}) collective-permute-start(bf16[40,128,128]{2,1,0:T(8,128)(2,1)S(1)} %tiles.25), channel_id=1, source_target_pairs={{0,8},{8,0},{16,24},{24,16},{32,40},{40,32},{48,56},{56,48},{64,72... | collective-permute-start | bytes 3932168 | tf_op jit(solution)/shard_map/ppermute | solution.py:322
  43.4 7.9 %collective-permute-start.14 = (bf16[40,128,128]{2,1,0:T(8,128)(2,1)S(1)}, bf16[40,128,128]{2,1,0:T(8,128)(2,1)S(1)}, u32[]{:S(2)}, u32[]{:S(2)}) collective-permute-start(bf16[40,128,128]{2,1,0:T(8,128)(2,1)S(1)} %tiles.26), channel_id=1, source_target_pairs={{0,8},{8,0},{16,24},{24,16},{32,40},{40,32},{48,56},{56,48},{64,72... | collective-permute-start | bytes 3932168 | tf_op jit(solution)/shard_map/ppermute | solution.py:322
  43.6 3.4 %copy-start.10 = (s32[8]{0:T(128)S(1)}, s32[8]{0:T(128)}, u32[]{:S(2)}) copy-start(s32[8]{0:T(128)} %constant.33.clone) | copy-start | bytes 100
  43.6 3.4 %copy-start.5 = (s32[8]{0:T(128)S(1)}, s32[8]{0:T(128)}, u32[]{:S(2)}) copy-start(s32[8]{0:T(128)} %constant.32.clone.refs_1_) | copy-start | bytes 100
  46.4 25.8 %collective-permute-start.15 = (bf16[24,128,128]{2,1,0:T(8,128)(2,1)}, bf16[24,128,128]{2,1,0:T(8,128)(2,1)S(1)}, u32[]{:S(2)}, u32[]{:S(2)}) collective-permute-start(bf16[24,128,128]{2,1,0:T(8,128)(2,1)} %get-tuple-element.235), channel_id=1, source_target_pairs={{0,16},{8,24},{16,0},{24,8},{32,48},{40,56},{48,32},{56,40},{64,80... | collective-permute-start | bytes 2359304 | tf_op jit(solution)/shard_map/ppermute | solution.py:322
  47.0 4.4 %copy-start.6 = (s32[8]{0:T(128)S(1)}, s32[8]{0:T(128)}, u32[]{:S(2)}) copy-start(s32[8]{0:T(128)} %constant.34.clone.refs_1_) | copy-start | bytes 100
  49.5 4.4 %copy-start = (bf16[20,128,128]{2,1,0:T(8,128)(2,1)}, bf16[20,128,128]{2,1,0:T(8,128)(2,1)S(1)}, u32[]{:S(2)}) copy-start(bf16[20,128,128]{2,1,0:T(8,128)(2,1)S(1)} %get-tuple-element.237.refs_0_) | copy-start | bytes 1966084
  49.5 22.9 %collective-permute-start.16 = (bf16[20,128,128]{2,1,0:T(8,128)(2,1)}, bf16[20,128,128]{2,1,0:T(8,128)(2,1)}, u32[]{:S(2)}, u32[]{:S(2)}) collective-permute-start(bf16[20,128,128]{2,1,0:T(8,128)(2,1)} %get-tuple-element.238), channel_id=1, source_target_pairs={{0,32},{8,40},{16,48},{24,56},{32,0},{40,8},{48,16},{56,24},{64,96... | collective-permute-start | bytes 1966088 | tf_op jit(solution)/shard_map/ppermute | solution.py:322
  54.8 19.7 %collective-permute-start.17 = (bf16[20,128,128]{2,1,0:T(8,128)(2,1)}, bf16[20,128,128]{2,1,0:T(8,128)(2,1)S(1)}, u32[]{:S(2)}, u32[]{:S(2)}) collective-permute-start(bf16[20,128,128]{2,1,0:T(8,128)(2,1)} %get-tuple-element.241), channel_id=1, source_target_pairs={{0,96},{8,104},{16,112},{24,120},{32,64},{40,72},{48,80},{56,88},{... | collective-permute-start | bytes 1966088 | tf_op jit(solution)/shard_map/ppermute | solution.py:322
  72.1 10.7 %collective-permute-start.18 = (bf16[48,128,128]{2,1,0:T(8,128)(2,1)S(1)}, bf16[48,128,128]{2,1,0:T(8,128)(2,1)S(1)}, u32[]{:S(2)}, u32[]{:S(2)}) collective-permute-start(bf16[48,128,128]{2,1,0:T(8,128)(2,1)S(1)} %tiles.30), channel_id=1, source_target_pairs={{0,8},{8,0},{16,24},{24,16},{32,40},{40,32},{48,56},{56,48},{64,72... | collective-permute-start | bytes 4718600 | tf_op jit(solution)/shard_map/ppermute | solution.py:322
  76.6 9.0 %collective-permute-start.19 = (bf16[40,128,128]{2,1,0:T(8,128)(2,1)S(1)}, bf16[40,128,128]{2,1,0:T(8,128)(2,1)S(1)}, u32[]{:S(2)}, u32[]{:S(2)}) collective-permute-start(bf16[40,128,128]{2,1,0:T(8,128)(2,1)S(1)} %tiles.31), channel_id=1, source_target_pairs={{0,8},{8,0},{16,24},{24,16},{32,40},{40,32},{48,56},{56,48},{64,72... | collective-permute-start | bytes 3932168 | tf_op jit(solution)/shard_map/ppermute | solution.py:322
  78.5 25.6 %collective-permute-start.26 = (bf16[40,128,128]{2,1,0:T(8,128)(2,1)S(1)}, bf16[40,128,128]{2,1,0:T(8,128)(2,1)S(1)}, u32[]{:S(2)}, u32[]{:S(2)}) collective-permute-start(bf16[40,128,128]{2,1,0:T(8,128)(2,1)S(1)} %tiles.32), channel_id=1, source_target_pairs={{0,8},{8,0},{16,24},{24,16},{32,40},{40,32},{48,56},{56,48},{64,72... | collective-permute-start | bytes 3932168 | tf_op jit(solution)/shard_map/ppermute | solution.py:322
  79.1 11.1 %collective-permute-start.20 = (bf16[12,128,128]{2,1,0:T(8,128)(2,1)S(1)}, bf16[12,128,128]{2,1,0:T(8,128)(2,1)S(1)}, u32[]{:S(2)}, u32[]{:S(2)}) collective-permute-start(bf16[12,128,128]{2,1,0:T(8,128)(2,1)S(1)} %get-tuple-element.250), channel_id=1, source_target_pairs={{0,32},{8,40},{16,48},{24,56},{32,0},{40,8},{48,16},{56,24},{64,96... | collective-permute-start | bytes 1179656 | tf_op jit(solution)/shard_map/ppermute | solution.py:322
  80.7 10.6 %collective-permute-start.22 = (bf16[10,128,128]{2,1,0:T(8,128)(2,1)S(1)}, bf16[10,128,128]{2,1,0:T(8,128)(2,1)S(1)}, u32[]{:S(2)}, u32[]{:S(2)}) collective-permute-start(bf16[10,128,128]{2,1,0:T(8,128)(2,1)S(1)} %get-tuple-element.254), channel_id=1, source_target_pairs={{0,96},{8,104},{16,112},{24,120},{32,64},{40,72},{48,80},{56,88},{... | collective-permute-start | bytes 983048 | tf_op jit(solution)/shard_map/ppermute | solution.py:322
  82.8 21.2 %collective-permute-start.24 = (bf16[10,128,128]{2,1,0:T(8,128)(2,1)S(1)}, bf16[10,128,128]{2,1,0:T(8,128)(2,1)S(1)}, u32[]{:S(2)}, u32[]{:S(2)}) collective-permute-start(bf16[10,128,128]{2,1,0:T(8,128)(2,1)S(1)} %get-tuple-element.258), channel_id=1, source_target_pairs={{0,16},{8,24},{16,0},{24,8},{32,48},{40,56},{48,32},{56,40},{64,80... | collective-permute-start | bytes 983048 | tf_op jit(solution)/shard_map/ppermute | solution.py:322
  85.5 23.3 %collective-permute-start.27 = (bf16[24,128,128]{2,1,0:T(8,128)(2,1)S(1)}, bf16[24,128,128]{2,1,0:T(8,128)(2,1)S(1)}, u32[]{:S(2)}, u32[]{:S(2)}) collective-permute-start(bf16[24,128,128]{2,1,0:T(8,128)(2,1)S(1)} %get-tuple-element.264), channel_id=1, source_target_pairs={{0,16},{8,24},{16,0},{24,8},{32,48},{40,56},{48,32},{56,40},{64,80... | collective-permute-start | bytes 2359304 | tf_op jit(solution)/shard_map/ppermute | solution.py:322
  91.4 29.7 %collective-permute-start.28 = (bf16[20,128,128]{2,1,0:T(8,128)(2,1)S(1)}, bf16[20,128,128]{2,1,0:T(8,128)(2,1)S(1)}, u32[]{:S(2)}, u32[]{:S(2)}) collective-permute-start(bf16[20,128,128]{2,1,0:T(8,128)(2,1)S(1)} %get-tuple-element.267), channel_id=1, source_target_pairs={{0,32},{8,40},{16,48},{24,56},{32,0},{40,8},{48,16},{56,24},{64,96... | collective-permute-start | bytes 1966088 | tf_op jit(solution)/shard_map/ppermute | solution.py:322
  106.0 18.7 %collective-permute-start.29 = (bf16[20,128,128]{2,1,0:T(8,128)(2,1)S(1)}, bf16[20,128,128]{2,1,0:T(8,128)(2,1)S(1)}, u32[]{:S(2)}, u32[]{:S(2)}) collective-permute-start(bf16[20,128,128]{2,1,0:T(8,128)(2,1)S(1)} %get-tuple-element.270), channel_id=1, source_target_pairs={{0,96},{8,104},{16,112},{24,120},{32,64},{40,72},{48,80},{56,88},{... | collective-permute-start | bytes 1966088 | tf_op jit(solution)/shard_map/ppermute | solution.py:322
  109.1 18.4 %collective-permute-start.30 = (bf16[12,128,128]{2,1,0:T(8,128)(2,1)S(1)}, bf16[12,128,128]{2,1,0:T(8,128)(2,1)S(1)}, u32[]{:S(2)}, u32[]{:S(2)}) collective-permute-start(bf16[12,128,128]{2,1,0:T(8,128)(2,1)S(1)} %get-tuple-element.273), channel_id=1, source_target_pairs={{0,32},{8,40},{16,48},{24,56},{32,0},{40,8},{48,16},{56,24},{64,96... | collective-permute-start | bytes 1179656 | tf_op jit(solution)/shard_map/ppermute | solution.py:322
  121.3 8.7 %collective-permute-start.32 = (bf16[10,128,128]{2,1,0:T(8,128)(2,1)S(1)}, bf16[10,128,128]{2,1,0:T(8,128)(2,1)S(1)}, u32[]{:S(2)}, u32[]{:S(2)}) collective-permute-start(bf16[10,128,128]{2,1,0:T(8,128)(2,1)S(1)} %get-tuple-element.277), channel_id=1, source_target_pairs={{0,96},{8,104},{16,112},{24,120},{32,64},{40,72},{48,80},{56,88},{... | collective-permute-start | bytes 983048 | tf_op jit(solution)/shard_map/ppermute | solution.py:322
  124.8 7.2 %collective-permute-start.34 = (bf16[10,128,128]{2,1,0:T(8,128)(2,1)S(1)}, bf16[10,128,128]{2,1,0:T(8,128)(2,1)S(1)}, u32[]{:S(2)}, u32[]{:S(2)}) collective-permute-start(bf16[10,128,128]{2,1,0:T(8,128)(2,1)S(1)} %get-tuple-element.281), channel_id=1, source_target_pairs={{0,16},{8,24},{16,0},{24,8},{32,48},{40,56},{48,32},{56,40},{64,80... | collective-permute-start | bytes 983048 | tf_op jit(solution)/shard_map/ppermute | solution.py:322
  132.1 5.4 %collective-permute-start.35 = (bf16[5,128,128]{2,1,0:T(8,128)(2,1)S(1)}, bf16[5,128,128]{2,1,0:T(8,128)(2,1)S(1)}, u32[]{:S(2)}, u32[]{:S(2)}) collective-permute-start(bf16[5,128,128]{2,1,0:T(8,128)(2,1)S(1)} %get-tuple-element.283), channel_id=1, source_target_pairs={{0,32},{8,40},{16,48},{24,56},{32,0},{40,8},{48,16},{56,24},{64,96... | collective-permute-start | bytes 491528 | tf_op jit(solution)/shard_map/ppermute | solution.py:322
  132.2 8.6 %collective-permute-start.31 = (bf16[6,128,128]{2,1,0:T(8,128)(2,1)S(1)}, bf16[6,128,128]{2,1,0:T(8,128)(2,1)S(1)}, u32[]{:S(2)}, u32[]{:S(2)}) collective-permute-start(bf16[6,128,128]{2,1,0:T(8,128)(2,1)S(1)} %get-tuple-element.275), channel_id=1, source_target_pairs={{0,96},{8,104},{16,112},{24,120},{32,64},{40,72},{48,80},{56,88},{... | collective-permute-start | bytes 589832 | tf_op jit(solution)/shard_map/ppermute | solution.py:322
  134.4 8.4 %collective-permute-start.21 = (bf16[6,128,128]{2,1,0:T(8,128)(2,1)S(1)}, bf16[6,128,128]{2,1,0:T(8,128)(2,1)S(1)}, u32[]{:S(2)}, u32[]{:S(2)}) collective-permute-start(bf16[6,128,128]{2,1,0:T(8,128)(2,1)S(1)} %get-tuple-element.252), channel_id=1, source_target_pairs={{0,96},{8,104},{16,112},{24,120},{32,64},{40,72},{48,80},{56,88},{... | collective-permute-start | bytes 589832 | tf_op jit(solution)/shard_map/ppermute | solution.py:322
  135.5 5.3 %collective-permute-start.33 = (bf16[5,128,128]{2,1,0:T(8,128)(2,1)S(1)}, bf16[5,128,128]{2,1,0:T(8,128)(2,1)S(1)}, u32[]{:S(2)}, u32[]{:S(2)}) collective-permute-start(bf16[5,128,128]{2,1,0:T(8,128)(2,1)S(1)} %get-tuple-element.279), channel_id=1, source_target_pairs={{0,16},{8,24},{16,0},{24,8},{32,48},{40,56},{48,32},{56,40},{64,80... | collective-permute-start | bytes 491528 | tf_op jit(solution)/shard_map/ppermute | solution.py:322
  136.1 5.3 %collective-permute-start.25 = (bf16[5,128,128]{2,1,0:T(8,128)(2,1)S(1)}, bf16[5,128,128]{2,1,0:T(8,128)(2,1)S(1)}, u32[]{:S(2)}, u32[]{:S(2)}) collective-permute-start(bf16[5,128,128]{2,1,0:T(8,128)(2,1)S(1)} %get-tuple-element.260), channel_id=1, source_target_pairs={{0,32},{8,40},{16,48},{24,56},{32,0},{40,8},{48,16},{56,24},{64,96... | collective-permute-start | bytes 491528 | tf_op jit(solution)/shard_map/ppermute | solution.py:322
  137.5 5.3 %collective-permute-start.23 = (bf16[5,128,128]{2,1,0:T(8,128)(2,1)S(1)}, bf16[5,128,128]{2,1,0:T(8,128)(2,1)S(1)}, u32[]{:S(2)}, u32[]{:S(2)}) collective-permute-start(bf16[5,128,128]{2,1,0:T(8,128)(2,1)S(1)} %get-tuple-element.256), channel_id=1, source_target_pairs={{0,16},{8,24},{16,0},{24,8},{32,48},{40,56},{48,32},{56,40},{64,80... | collective-permute-start | bytes 491528 | tf_op jit(solution)/shard_map/ppermute | solution.py:322
  (4 other events, 6.9 us)
where the time goes:
time: 148 us; the launch traced here: 146 us
  Pallas kernels  54.9 us (37%)
  starting transfers between devices  40.4 us (27%)
  waiting for transfers between devices  29.6 us (20%)
  blocking collectives  15.3 us (10%)
  local copies, waits for them, and re-layouts  2.76 us (2%)
  between operations  1.95 us (1%)
    ppermute x24, starting transfers between devices, swap(): return lax.ppermute(a, 'tm', [(i, i ^ mask) for i in range(n)])  36 us
    ppermute x24, waiting for transfers between devices, swap(): return lax.ppermute(a, 'tm', [(i, i ^ mask) for i in range(n)])  26.2 us
    pallas_call x12, Pallas kernels, tiles(): pl.pallas_call(functools.partial(tiles_kernel, first, per, with_add), in_...  25.4 us
    pallas_call x2, Pallas kernels, prep(): pl.pallas_call(functools.partial(prep_kernel, with_far), in_specs=[vmem]...  18.4 us
    all_to_all x1, blocking collectives, body(): lax.all_to_all(request, 'tile', split_axis=0, concat_axis=0, tiled=True)  15.3 us
    all_to_all x1, starting transfers between devices, body(): lax.all_to_all(outgoing, 'tile', split_axis=0, concat_axis=0, tiled=True)  4.43 us
    pallas_call x1, Pallas kernels, pack(): pl.pallas_call(pack_kernel, in_specs=[pl.BlockSpec(memory_space=pltpu.SME...  4.24 us
    all_to_all x1, waiting for transfers between devices, body(): lax.all_to_all(outgoing, 'tile', split_axis=0, concat_axis=0, tiled=True)  3.36 us
  transfers between devices with their start and end apart: 25, of which 13 were waited for; matrix products, arithmetic and copies ran while one was open for 1% of the time, Pallas kernels for 32%

commit v1 on v0

--- a/solution.py
+++ b/solution.py
@@ -411,18 +411,17 @@
     late = exchange(late, 2)
     firsts = tuple(offsets[0] + offsets[1])
 
-    def crowded_group(early, late):
-        wt, e_blocks = prep(weights, adjoint, emission, far)
+    def crowded_group(state):
+        wt, e_blocks = prep(after(weights, state[1]), adjoint, emission, far)
         cores, last = first_kernels(0, wt, e_blocks)
         again, last = second_kernels(0, wt, e_blocks, cores, last)
         for step in range(2):
             again, last = halve(exchange(again, step), last)
-        return finish(me, counts, table, exchange(again, 2) + late, firsts)
-
-    def usual(early, late):
-        return finish(me, counts, table, early + late, firsts)
-
-    return lax.cond(crowded, crowded_group, usual, early, late)[None]
+        out = finish(me, counts, table, exchange(again, 2) + late, firsts)
+        return jnp.zeros((), bool), out
+
+    out = finish(me, counts, table, early + late, firsts)
+    return lax.while_loop(lambda state: state[0], crowded_group, (crowded, out))[1][None]
 
 
 def solution(mesh):

time: 148 us -> 146 us (0.986)
  blocking collectives: 15.3 us -> 0 us
  starting transfers between devices: 40.4 us -> 49.8 us
  waiting for transfers between devices: 29.6 us -> 33.1 us
    all_to_all x1 -> x0, blocking collectives: 15.3 us -> none  [body(): lax.all_to_all(request, 'tile', split_axis=0, concat_axis=0, tiled=True)]
    all_to_all x0 -> x1, starting transfers between devices: none -> 7.86 us  [body(): lax.all_to_all(request, 'tile', split_axis=0, concat_axis=0, tiled=True)]
    all_to_all x0 -> x1, waiting for transfers between devices: none -> 6.9 us  [body(): lax.all_to_all(request, 'tile', split_axis=0, concat_axis=0, tiled=True)]
    ppermute x24, waiting for transfers between devices: 26.2 us -> 22.8 us  [swap(): return lax.ppermute(a, 'tm', [(i, i ^ mask) for i in range(n)])]
    ppermute x24, starting transfers between devices: 36 us -> 37.6 us  [swap(): return lax.ppermute(a, 'tm', [(i, i ^ mask) for i in range(n)])]
  transfers between devices with their start and end apart: 25 -> 26, of which waited for: 13 -> 12; matrix products, arithmetic and copies ran while one was open for 1% -> 1% of each run, Pallas kernels for 32% -> 32%
where the time goes in v1:
time: 146 us; the launch traced here: 144 us
  Pallas kernels  54.8 us (38%)
  starting transfers between devices  49.8 us (34%)
  waiting for transfers between devices  33.1 us (23%)
  local copies, waits for them, and re-layouts  3.54 us (2%)
    ppermute x24, starting transfers between devices, swap(): return lax.ppermute(a, 'tm', [(i, i ^ mask) for i in range(n)])  37.6 us
    pallas_call x12, Pallas kernels, tiles(): pl.pallas_call(functools.partial(tiles_kernel, first, per, with_add), in_...  25.4 us
    ppermute x24, waiting for transfers between devices, swap(): return lax.ppermute(a, 'tm', [(i, i ^ mask) for i in range(n)])  22.8 us
    pallas_call x2, Pallas kernels, prep(): pl.pallas_call(functools.partial(prep_kernel, with_far), in_specs=[vmem]...  18.4 us
    all_to_all x1, starting transfers between devices, body(): lax.all_to_all(request, 'tile', split_axis=0, concat_axis=0, tiled=True)  7.86 us
    all_to_all x1, waiting for transfers between devices, body(): lax.all_to_all(request, 'tile', split_axis=0, concat_axis=0, tiled=True)  6.9 us
    all_to_all x1, starting transfers between devices, body(): lax.all_to_all(outgoing, 'tile', split_axis=0, concat_axis=0, tiled=True)  4.41 us
    pallas_call x1, Pallas kernels, pack(): pl.pallas_call(pack_kernel, in_specs=[pl.BlockSpec(memory_space=pltpu.SME...  4.23 us
  transfers between devices with their start and end apart: 26, of which 12 were waited for; matrix products, arithmetic and copies ran while one was open for 1% of the time, Pallas kernels for 32%

profile of v1, /device:TPU:0, one launch (start us, length us, event | category | flops | bytes accessed | tf_op | source)
XLA Modules:
  0.0 143.8 jit_solution(951236328960882087)
XLA Ops:
  1.5 2.1 %plan.1 = (s32[8,128]{1,0:T(8,128)}, s32[16,128]{1,0:T(8,128)S(1)}) custom-call(s32[1]{0:T(128)} %bitcast.own_ref, s32[1]{0:T(128)S(6)} %copy.41.count_ref, s32[512,2]{1,0:T(8,128)S(1)} %copy.29.tiles_ref), custom_call_target="tpu_custom_call" | custom-call | tf_op jit(solution)/shard_map/plan/pallas_call | solution.py:87
  3.6 7.9 %all-to-all-start = ((s32[8,1,128]{2,1,0:T(1,128)}), s32[8,1,128]{2,1,0:T(1,128)S(1)}, u32[]{:S(2)}, u32[]{:S(2)}) async-start(s32[8,1,128]{2,1,0:T(1,128)} %bitcast.2), calls=%async_computation | async-start | bytes 8192 | tf_op jit(solution)/shard_map/all_to_all | solution.py:341
  12.1 6.9 %all-to-all-done = s32[8,1,128]{2,1,0:T(1,128)S(1)} async-done(((s32[8,1,128]{2,1,0:T(1,128)}), s32[8,1,128]{2,1,0:T(1,128)S(1)}, u32[]{:S(2)}, u32[]{:S(2)}) %all-to-all-start) | async-done | bytes 4128 | tf_op jit(solution)/shard_map/all_to_all | solution.py:341
  19.0 4.2 %pack.1 = bf16[32,320,128]{2,1,0:T(8,128)(2,1)} custom-call(s32[8,128]{1,0:T(8,128)S(1)} %bitcast.9, bf16[320,16384]{1,0:T(8,128)(2,1)} %em_ref.5), custom_call_target="tpu_custom_call" | custom-call | tf_op jit(solution)/shard_map/pack/pallas_call | solution.py:210
  23.2 4.4 %all-to-all-start.1 = ((bf16[32,320,128]{2,1,0:T(8,128)(2,1)}), bf16[32,320,128]{2,1,0:T(8,128)(2,1)}, u32[]{:S(2)}, u32[]{:S(2)}) async-start(bf16[32,320,128]{2,1,0:T(8,128)(2,1)} %pack.1), calls=%async_computation.1 | async-start | bytes 5242880 | tf_op jit(solution)/shard_map/all_to_all | solution.py:343
  28.5 8.9 %prep.3 = (bf16[128,128,384]{2,1,0:T(8,128)(2,1)S(1)}, bf16[128,384,128]{2,1,0:T(8,128)(2,1)S(1)}) custom-call(f32[320,1]{1,0:T(8,128)S(1)} %copy.31.weights_ref, bf16[320,16384]{1,0:T(8,128)(2,1)} %adj_ref.3, bf16[320,16384]{1,0:T(8,128)(2,1)} %em_ref.5), custom_call_target="tpu_custom_call" | custom-call | tf_op jit(solution)/shard_map/prep/pallas_call | solution.py:169
  37.4 2.1 %tiles.18 = bf16[48,128,128]{2,1,0:T(8,128)(2,1)S(1)} custom-call(s32[8]{0:T(128)S(1)} %multiply_xor_fusion.1.refs_0_.refs_1_, s32[8]{0:T(128)S(1)} %multiply_xor_fusion.1.refs_0_.refs_1_, s32[16,128]{1,0:T(8,128)S(1)} %get-tuple-element.559.refs_2_.table_ref, bf16[128,128,384]{2,1,0:T(8,128)(2,1)S(1)} %get-tuple-element.220.refs_3_, ...), custom_call_target="tpu_custom_call" | custom-call | tf_op jit(solution)/shard_map/tiles/pallas_call | solution.py:244
  39.6 1.9 %tiles.19 = bf16[40,128,128]{2,1,0:T(8,128)(2,1)S(1)} custom-call(s32[8]{0:T(128)S(1)} %multiply_xor_fusion.1.refs_0_.refs_1_, s32[8]{0:T(128)S(1)} %multiply_xor_fusion.1.refs_0_.refs_1_, s32[16,128]{1,0:T(8,128)S(1)} %get-tuple-element.559.refs_2_.table_ref, bf16[128,128,384]{2,1,0:T(8,128)(2,1)S(1)} %get-tuple-element.220.refs_3_, ...), custom_call_target="tpu_custom_call" | custom-call | tf_op jit(solution)/shard_map/tiles/pallas_call | solution.py:244
  42.1 1.9 %tiles.20 = bf16[40,128,128]{2,1,0:T(8,128)(2,1)S(1)} custom-call(s32[8]{0:T(128)S(1)} %multiply_xor_fusion.1.refs_0_.refs_1_, s32[8]{0:T(128)S(1)} %multiply_xor_fusion.1.refs_0_.refs_1_, s32[16,128]{1,0:T(8,128)S(1)} %get-tuple-element.559.refs_2_.table_ref, bf16[128,128,384]{2,1,0:T(8,128)(2,1)S(1)} %get-tuple-element.220.refs_3_, ...), custom_call_target="tpu_custom_call" | custom-call | tf_op jit(solution)/shard_map/tiles/pallas_call | solution.py:244
  44.1 2.8 %tiles.21 = (bf16[24,128,128]{2,1,0:T(8,128)(2,1)}, bf16[24,128,128]{2,1,0:T(8,128)(2,1)S(1)}) custom-call(s32[8]{0:T(128)S(1)} %broadcast_xor_fusion.5.refs_0_, s32[8]{0:T(128)S(1)} %copy-done.9, s32[16,128]{1,0:T(8,128)S(1)} %get-tuple-element.559.refs_2_.table_ref, bf16[128,128,384]{2,1,0:T(8,128)(2,1)S(1)} %get-tuple-element.220.refs_3_, ...), custom_call_target="tpu_custom_call" | custom-call | tf_op jit(solution)/shard_map/tiles/pallas_call | solution.py:244
  47.5 2.5 %tiles.22 = (bf16[20,128,128]{2,1,0:T(8,128)(2,1)}, bf16[20,128,128]{2,1,0:T(8,128)(2,1)S(1)}) custom-call(s32[8]{0:T(128)S(1)} %broadcast_xor_fusion.3.refs_0_, s32[8]{0:T(128)S(1)} %copy-done.8, s32[16,128]{1,0:T(8,128)S(1)} %get-tuple-element.559.refs_2_.table_ref, bf16[128,128,384]{2,1,0:T(8,128)(2,1)S(1)} %get-tuple-element.220.refs_3_, ...), custom_call_target="tpu_custom_call" | custom-call | tf_op jit(solution)/shard_map/tiles/pallas_call | solution.py:244
  50.1 1.8 %collective-permute-start.16 = (bf16[20,128,128]{2,1,0:T(8,128)(2,1)}, bf16[20,128,128]{2,1,0:T(8,128)(2,1)}, u32[]{:S(2)}, u32[]{:S(2)}) collective-permute-start(bf16[20,128,128]{2,1,0:T(8,128)(2,1)} %get-tuple-element.239), channel_id=1, source_target_pairs={{0,32},{8,40},{16,48},{24,56},{32,0},{40,8},{48,16},{56,24},{64,96... | collective-permute-start | bytes 1966088 | tf_op jit(solution)/shard_map/ppermute | solution.py:322
  51.9 2.6 %tiles.23 = (bf16[20,128,128]{2,1,0:T(8,128)(2,1)}, bf16[20,128,128]{2,1,0:T(8,128)(2,1)S(1)}) custom-call(s32[8]{0:T(128)S(1)} %broadcast_xor_fusion.4.refs_0_, s32[8]{0:T(128)S(1)} %copy-done.7, s32[16,128]{1,0:T(8,128)S(1)} %get-tuple-element.559.refs_2_.table_ref, bf16[128,128,384]{2,1,0:T(8,128)(2,1)S(1)} %get-tuple-element.220.refs_3_, ...), custom_call_target="tpu_custom_call" | custom-call | tf_op jit(solution)/shard_map/tiles/pallas_call | solution.py:244
  55.3 2.2 %collective-permute-start.17 = (bf16[20,128,128]{2,1,0:T(8,128)(2,1)}, bf16[20,128,128]{2,1,0:T(8,128)(2,1)S(1)}, u32[]{:S(2)}, u32[]{:S(2)}) collective-permute-start(bf16[20,128,128]{2,1,0:T(8,128)(2,1)} %get-tuple-element.242), channel_id=1, source_target_pairs={{0,96},{8,104},{16,112},{24,120},{32,64},{40,72},{48,80},{56,88},{... | collective-permute-start | bytes 1966088 | tf_op jit(solution)/shard_map/ppermute | solution.py:322
  57.7 3.4 %all-to-all-done.1.refs_0_ = bf16[32,320,128]{2,1,0:T(8,128)(2,1)} async-done(((bf16[32,320,128]{2,1,0:T(8,128)(2,1)}), bf16[32,320,128]{2,1,0:T(8,128)(2,1)}, u32[]{:S(2)}, u32[]{:S(2)}) %all-to-all-start.1) | async-done | bytes 2621472 | tf_op jit(solution)/shard_map/all_to_all | solution.py:343
  61.1 9.5 %prep.4 = (bf16[128,128,384]{2,1,0:T(8,128)(2,1)S(1)}, bf16[160,384,128]{2,1,0:T(8,128)(2,1)S(1)}) custom-call(f32[320,1]{1,0:T(8,128)S(1)} %copy.32.weights_ref, bf16[320,16384]{1,0:T(8,128)(2,1)} %adj_ref.3, bf16[320,16384]{1,0:T(8,128)(2,1)} %em_ref.5, bf16[32,320,128]{2,1,0:T(8,128)(2,1)} %all-to-all-done.1.refs_0_), custom_call_target="tpu_custom_call" | custom-call | tf_op jit(solution)/shard_map/prep/pallas_call | solution.py:169
  70.6 2.1 %tiles.24 = bf16[48,128,128]{2,1,0:T(8,128)(2,1)S(1)} custom-call(s32[8]{0:T(128)S(1)} %multiply_xor_fusion.1.refs_0_.refs_1_, s32[8]{0:T(128)S(1)} %multiply_xor_fusion.1.refs_0_.refs_1_, s32[16,128]{1,0:T(8,128)S(1)} %get-tuple-element.559.refs_2_.table_ref, bf16[128,128,384]{2,1,0:T(8,128)(2,1)S(1)} %get-tuple-element.232.refs_3_, ...), custom_call_target="tpu_custom_call" | custom-call | tf_op jit(solution)/shard_map/tiles/pallas_call | solution.py:244
  75.3 1.9 %tiles.25 = bf16[40,128,128]{2,1,0:T(8,128)(2,1)S(1)} custom-call(s32[8]{0:T(128)S(1)} %multiply_xor_fusion.1.refs_0_.refs_1_, s32[8]{0:T(128)S(1)} %multiply_xor_fusion.1.refs_0_.refs_1_, s32[16,128]{1,0:T(8,128)S(1)} %get-tuple-element.559.refs_2_.table_ref, bf16[128,128,384]{2,1,0:T(8,128)(2,1)S(1)} %get-tuple-element.232.refs_3_, ...), custom_call_target="tpu_custom_call" | custom-call | tf_op jit(solution)/shard_map/tiles/pallas_call | solution.py:244
  77.3 1.9 %tiles.26 = bf16[40,128,128]{2,1,0:T(8,128)(2,1)S(1)} custom-call(s32[8]{0:T(128)S(1)} %multiply_xor_fusion.1.refs_0_.refs_1_, s32[8]{0:T(128)S(1)} %multiply_xor_fusion.1.refs_0_.refs_1_, s32[16,128]{1,0:T(8,128)S(1)} %get-tuple-element.559.refs_2_.table_ref, bf16[128,128,384]{2,1,0:T(8,128)(2,1)S(1)} %get-tuple-element.232.refs_3_, ...), custom_call_target="tpu_custom_call" | custom-call | tf_op jit(solution)/shard_map/tiles/pallas_call | solution.py:244
  79.7 1.6 %collective-permute-start.20 = (bf16[12,128,128]{2,1,0:T(8,128)(2,1)S(1)}, bf16[12,128,128]{2,1,0:T(8,128)(2,1)S(1)}, u32[]{:S(2)}, u32[]{:S(2)}) collective-permute-start(bf16[12,128,128]{2,1,0:T(8,128)(2,1)S(1)} %get-tuple-element.251), channel_id=1, source_target_pairs={{0,32},{8,40},{16,48},{24,56},{32,0},{40,8},{48,16},{56,24},{64,96... | collective-permute-start | bytes 1179656 | tf_op jit(solution)/shard_map/ppermute | solution.py:322
  81.3 2.2 %collective-permute-start.22 = (bf16[10,128,128]{2,1,0:T(8,128)(2,1)S(1)}, bf16[10,128,128]{2,1,0:T(8,128)(2,1)S(1)}, u32[]{:S(2)}, u32[]{:S(2)}) collective-permute-start(bf16[10,128,128]{2,1,0:T(8,128)(2,1)S(1)} %get-tuple-element.255), channel_id=1, source_target_pairs={{0,96},{8,104},{16,112},{24,120},{32,64},{40,72},{48,80},{56,88},{... | collective-permute-start | bytes 983048 | tf_op jit(solution)/shard_map/ppermute | solution.py:322
  84.1 2.1 %tiles.27 = (bf16[24,128,128]{2,1,0:T(8,128)(2,1)S(1)}, bf16[24,128,128]{2,1,0:T(8,128)(2,1)S(1)}) custom-call(s32[8]{0:T(128)S(1)} %broadcast_xor_fusion.5.refs_0_, s32[8]{0:T(128)S(1)} %copy-done.9, s32[16,128]{1,0:T(8,128)S(1)} %get-tuple-element.559.refs_2_.table_ref, bf16[128,128,384]{2,1,0:T(8,128)(2,1)S(1)} %get-tuple-element.232.refs_3_, ...), custom_call_target="tpu_custom_call" | custom-call | tf_op jit(solution)/shard_map/tiles/pallas_call | solution.py:244
  87.7 1.9 %tiles.28 = (bf16[20,128,128]{2,1,0:T(8,128)(2,1)S(1)}, bf16[20,128,128]{2,1,0:T(8,128)(2,1)S(1)}) custom-call(s32[8]{0:T(128)S(1)} %broadcast_xor_fusion.3.refs_0_, s32[8]{0:T(128)S(1)} %copy-done.8, s32[16,128]{1,0:T(8,128)S(1)} %get-tuple-element.559.refs_2_.table_ref, bf16[128,128,384]{2,1,0:T(8,128)(2,1)S(1)} %get-tuple-element.232.refs_3_, ...), custom_call_target="tpu_custom_call" | custom-call | tf_op jit(solution)/shard_map/tiles/pallas_call | solution.py:244
  92.0 12.7 %collective-permute-start.28 = (bf16[20,128,128]{2,1,0:T(8,128)(2,1)S(1)}, bf16[20,128,128]{2,1,0:T(8,128)(2,1)S(1)}, u32[]{:S(2)}, u32[]{:S(2)}) collective-permute-start(bf16[20,128,128]{2,1,0:T(8,128)(2,1)S(1)} %get-tuple-element.268), channel_id=1, source_target_pairs={{0,32},{8,40},{16,48},{24,56},{32,0},{40,8},{48,16},{56,24},{64,96... | collective-permute-start | bytes 1966088 | tf_op jit(solution)/shard_map/ppermute | solution.py:322
  104.8 1.9 %tiles.29 = (bf16[20,128,128]{2,1,0:T(8,128)(2,1)S(1)}, bf16[20,128,128]{2,1,0:T(8,128)(2,1)S(1)}) custom-call(s32[8]{0:T(128)S(1)} %broadcast_xor_fusion.4.refs_0_, s32[8]{0:T(128)S(1)} %copy-done.7, s32[16,128]{1,0:T(8,128)S(1)} %get-tuple-element.559.refs_2_.table_ref, bf16[128,128,384]{2,1,0:T(8,128)(2,1)S(1)} %get-tuple-element.232.refs_3_, ...), custom_call_target="tpu_custom_call" | custom-call | tf_op jit(solution)/shard_map/tiles/pallas_call | solution.py:244
  106.7 2.3 %collective-permute-start.29 = (bf16[20,128,128]{2,1,0:T(8,128)(2,1)S(1)}, bf16[20,128,128]{2,1,0:T(8,128)(2,1)S(1)}, u32[]{:S(2)}, u32[]{:S(2)}) collective-permute-start(bf16[20,128,128]{2,1,0:T(8,128)(2,1)S(1)} %get-tuple-element.271), channel_id=1, source_target_pairs={{0,96},{8,104},{16,112},{24,120},{32,64},{40,72},{48,80},{56,88},{... | collective-permute-start | bytes 1966088 | tf_op jit(solution)/shard_map/ppermute | solution.py:322
  110.4 11.3 %collective-permute-done.28.refs_1_ = bf16[20,128,128]{2,1,0:T(8,128)(2,1)S(1)} collective-permute-done((bf16[20,128,128]{2,1,0:T(8,128)(2,1)S(1)}, bf16[20,128,128]{2,1,0:T(8,128)(2,1)S(1)}, u32[]{:S(2)}, u32[]{:S(2)}) %collective-permute-start.28) | collective-permute-done | bytes 655392 | tf_op jit(solution)/shard_map/ppermute | solution.py:322
  121.9 2.3 %collective-permute-start.32 = (bf16[10,128,128]{2,1,0:T(8,128)(2,1)S(1)}, bf16[10,128,128]{2,1,0:T(8,128)(2,1)S(1)}, u32[]{:S(2)}, u32[]{:S(2)}) collective-permute-start(bf16[10,128,128]{2,1,0:T(8,128)(2,1)S(1)} %get-tuple-element.278), channel_id=1, source_target_pairs={{0,96},{8,104},{16,112},{24,120},{32,64},{40,72},{48,80},{56,88},{... | collective-permute-start | bytes 983048 | tf_op jit(solution)/shard_map/ppermute | solution.py:322
  126.2 2.3 %collective-permute-start.21 = (bf16[6,128,128]{2,1,0:T(8,128)(2,1)S(1)}, bf16[6,128,128]{2,1,0:T(8,128)(2,1)S(1)}, u32[]{:S(2)}, u32[]{:S(2)}) collective-permute-start(bf16[6,128,128]{2,1,0:T(8,128)(2,1)S(1)} %get-tuple-element.253), channel_id=1, source_target_pairs={{0,96},{8,104},{16,112},{24,120},{32,64},{40,72},{48,80},{56,88},{... | collective-permute-start | bytes 589832 | tf_op jit(solution)/shard_map/ppermute | solution.py:322
  129.9 2.4 %collective-permute-start.31 = (bf16[6,128,128]{2,1,0:T(8,128)(2,1)S(1)}, bf16[6,128,128]{2,1,0:T(8,128)(2,1)S(1)}, u32[]{:S(2)}, u32[]{:S(2)}) collective-permute-start(bf16[6,128,128]{2,1,0:T(8,128)(2,1)S(1)} %get-tuple-element.276), channel_id=1, source_target_pairs={{0,96},{8,104},{16,112},{24,120},{32,64},{40,72},{48,80},{56,88},{... | collective-permute-start | bytes 589832 | tf_op jit(solution)/shard_map/ppermute | solution.py:322
  136.5 2.9 %collective-permute-done.23.refs_3_ = bf16[5,128,128]{2,1,0:T(8,128)(2,1)S(1)} collective-permute-done((bf16[5,128,128]{2,1,0:T(8,128)(2,1)S(1)}, bf16[5,128,128]{2,1,0:T(8,128)(2,1)S(1)}, u32[]{:S(2)}, u32[]{:S(2)}) %collective-permute-start.23) | collective-permute-done | bytes 163872 | tf_op jit(solution)/shard_map/ppermute | solution.py:322
  141.1 2.0 %finish.2 = f32[32,128,128]{2,1,0:T(8,128)} custom-call(s32[1]{0:T(128)} %bitcast.4.me_ref, s32[1]{0:T(128)S(6)} %copy.41.count_ref, s32[16,128]{1,0:T(8,128)S(1)} %get-tuple-element.559.refs_2_.table_ref, bf16[6,128,128]{2,1,0:T(8,128)(2,1)S(1)} %get-tuple-element.252.refs_0_, bf16[6,128,128]{2,1,0:T(8,128)(2,1)S(1)} %collective-permute-done.21.refs_1_, ...), custom_call_target="tpu_custom_call" | custom-call | tf_op jit(solution)/shard_map/finish/pallas_call | solution.py:301
  (80 shorter events, 23.9 us)
Async XLA Ops:
  3.6 15.4 %all-to-all-start = ((s32[8,1,128]{2,1,0:T(1,128)}), s32[8,1,128]{2,1,0:T(1,128)S(1)}, u32[]{:S(2)}, u32[]{:S(2)}) async-start(s32[8,1,128]{2,1,0:T(1,128)} %bitcast.2), calls=%async_computation | async-start | bytes 8192 | tf_op jit(solution)/shard_map/all_to_all | solution.py:341
  23.2 37.9 %all-to-all-start.1 = ((bf16[32,320,128]{2,1,0:T(8,128)(2,1)}), bf16[32,320,128]{2,1,0:T(8,128)(2,1)}, u32[]{:S(2)}, u32[]{:S(2)}) async-start(bf16[32,320,128]{2,1,0:T(8,128)(2,1)} %pack.1), calls=%async_computation.1 | async-start | bytes 5242880 | tf_op jit(solution)/shard_map/all_to_all | solution.py:343
  39.5 4.6 %collective-permute-start.12 = (bf16[48,128,128]{2,1,0:T(8,128)(2,1)S(1)}, bf16[48,128,128]{2,1,0:T(8,128)(2,1)S(1)}, u32[]{:S(2)}, u32[]{:S(2)}) collective-permute-start(bf16[48,128,128]{2,1,0:T(8,128)(2,1)S(1)} %tiles.18), channel_id=1, source_target_pairs={{0,8},{8,0},{16,24},{24,16},{32,40},{40,32},{48,56},{56,48},{64,72... | collective-permute-start | bytes 4718600 | tf_op jit(solution)/shard_map/ppermute | solution.py:322
  41.5 2.6 %copy-start.11 = (s32[8]{0:T(128)S(1)}, s32[8]{0:T(128)}, u32[]{:S(2)}) copy-start(s32[8]{0:T(128)} %constant.33.clone) | copy-start | bytes 100
  41.5 2.6 %copy-start.9 = (s32[8]{0:T(128)S(1)}, s32[8]{0:T(128)}, u32[]{:S(2)}) copy-start(s32[8]{0:T(128)} %constant.32.clone.refs_1_) | copy-start | bytes 100
  41.5 6.0 %collective-permute-start.13 = (bf16[40,128,128]{2,1,0:T(8,128)(2,1)S(1)}, bf16[40,128,128]{2,1,0:T(8,128)(2,1)S(1)}, u32[]{:S(2)}, u32[]{:S(2)}) collective-permute-start(bf16[40,128,128]{2,1,0:T(8,128)(2,1)S(1)} %tiles.19), channel_id=1, source_target_pairs={{0,8},{8,0},{16,24},{24,16},{32,40},{40,32},{48,56},{56,48},{64,72... | collective-permute-start | bytes 3932168 | tf_op jit(solution)/shard_map/ppermute | solution.py:322
  44.0 7.9 %collective-permute-start.14 = (bf16[40,128,128]{2,1,0:T(8,128)(2,1)S(1)}, bf16[40,128,128]{2,1,0:T(8,128)(2,1)S(1)}, u32[]{:S(2)}, u32[]{:S(2)}) collective-permute-start(bf16[40,128,128]{2,1,0:T(8,128)(2,1)S(1)} %tiles.20), channel_id=1, source_target_pairs={{0,8},{8,0},{16,24},{24,16},{32,40},{40,32},{48,56},{56,48},{64,72... | collective-permute-start | bytes 3932168 | tf_op jit(solution)/shard_map/ppermute | solution.py:322
  44.1 3.4 %copy-start.10 = (s32[8]{0:T(128)S(1)}, s32[8]{0:T(128)}, u32[]{:S(2)}) copy-start(s32[8]{0:T(128)} %constant.35.clone) | copy-start | bytes 100
  44.1 3.4 %copy-start.8 = (s32[8]{0:T(128)S(1)}, s32[8]{0:T(128)}, u32[]{:S(2)}) copy-start(s32[8]{0:T(128)} %constant.34.clone.refs_1_) | copy-start | bytes 100
  46.9 25.9 %collective-permute-start.15 = (bf16[24,128,128]{2,1,0:T(8,128)(2,1)}, bf16[24,128,128]{2,1,0:T(8,128)(2,1)S(1)}, u32[]{:S(2)}, u32[]{:S(2)}) collective-permute-start(bf16[24,128,128]{2,1,0:T(8,128)(2,1)} %get-tuple-element.236), channel_id=1, source_target_pairs={{0,16},{8,24},{16,0},{24,8},{32,48},{40,56},{48,32},{56,40},{64,80... | collective-permute-start | bytes 2359304 | tf_op jit(solution)/shard_map/ppermute | solution.py:322
  47.5 4.4 %copy-start.7 = (s32[8]{0:T(128)S(1)}, s32[8]{0:T(128)}, u32[]{:S(2)}) copy-start(s32[8]{0:T(128)} %constant.36.clone.refs_1_) | copy-start | bytes 100
  50.1 4.4 %copy-start = (bf16[20,128,128]{2,1,0:T(8,128)(2,1)}, bf16[20,128,128]{2,1,0:T(8,128)(2,1)S(1)}, u32[]{:S(2)}) copy-start(bf16[20,128,128]{2,1,0:T(8,128)(2,1)S(1)} %get-tuple-element.238.refs_0_) | copy-start | bytes 1966084
  50.1 23.0 %collective-permute-start.16 = (bf16[20,128,128]{2,1,0:T(8,128)(2,1)}, bf16[20,128,128]{2,1,0:T(8,128)(2,1)}, u32[]{:S(2)}, u32[]{:S(2)}) collective-permute-start(bf16[20,128,128]{2,1,0:T(8,128)(2,1)} %get-tuple-element.239), channel_id=1, source_target_pairs={{0,32},{8,40},{16,48},{24,56},{32,0},{40,8},{48,16},{56,24},{64,96... | collective-permute-start | bytes 1966088 | tf_op jit(solution)/shard_map/ppermute | solution.py:322
  55.3 19.8 %collective-permute-start.17 = (bf16[20,128,128]{2,1,0:T(8,128)(2,1)}, bf16[20,128,128]{2,1,0:T(8,128)(2,1)S(1)}, u32[]{:S(2)}, u32[]{:S(2)}) collective-permute-start(bf16[20,128,128]{2,1,0:T(8,128)(2,1)} %get-tuple-element.242), channel_id=1, source_target_pairs={{0,96},{8,104},{16,112},{24,120},{32,64},{40,72},{48,80},{56,88},{... | collective-permute-start | bytes 1966088 | tf_op jit(solution)/shard_map/ppermute | solution.py:322
  72.7 10.7 %collective-permute-start.18 = (bf16[48,128,128]{2,1,0:T(8,128)(2,1)S(1)}, bf16[48,128,128]{2,1,0:T(8,128)(2,1)S(1)}, u32[]{:S(2)}, u32[]{:S(2)}) collective-permute-start(bf16[48,128,128]{2,1,0:T(8,128)(2,1)S(1)} %tiles.24), channel_id=1, source_target_pairs={{0,8},{8,0},{16,24},{24,16},{32,40},{40,32},{48,56},{56,48},{64,72... | collective-permute-start | bytes 4718600 | tf_op jit(solution)/shard_map/ppermute | solution.py:322
  77.2 9.0 %collective-permute-start.19 = (bf16[40,128,128]{2,1,0:T(8,128)(2,1)S(1)}, bf16[40,128,128]{2,1,0:T(8,128)(2,1)S(1)}, u32[]{:S(2)}, u32[]{:S(2)}) collective-permute-start(bf16[40,128,128]{2,1,0:T(8,128)(2,1)S(1)} %tiles.25), channel_id=1, source_target_pairs={{0,8},{8,0},{16,24},{24,16},{32,40},{40,32},{48,56},{56,48},{64,72... | collective-permute-start | bytes 3932168 | tf_op jit(solution)/shard_map/ppermute | solution.py:322
  79.1 25.6 %collective-permute-start.26 = (bf16[40,128,128]{2,1,0:T(8,128)(2,1)S(1)}, bf16[40,128,128]{2,1,0:T(8,128)(2,1)S(1)}, u32[]{:S(2)}, u32[]{:S(2)}) collective-permute-start(bf16[40,128,128]{2,1,0:T(8,128)(2,1)S(1)} %tiles.26), channel_id=1, source_target_pairs={{0,8},{8,0},{16,24},{24,16},{32,40},{40,32},{48,56},{56,48},{64,72... | collective-permute-start | bytes 3932168 | tf_op jit(solution)/shard_map/ppermute | solution.py:322
  79.7 11.1 %collective-permute-start.20 = (bf16[12,128,128]{2,1,0:T(8,128)(2,1)S(1)}, bf16[12,128,128]{2,1,0:T(8,128)(2,1)S(1)}, u32[]{:S(2)}, u32[]{:S(2)}) collective-permute-start(bf16[12,128,128]{2,1,0:T(8,128)(2,1)S(1)} %get-tuple-element.251), channel_id=1, source_target_pairs={{0,32},{8,40},{16,48},{24,56},{32,0},{40,8},{48,16},{56,24},{64,96... | collective-permute-start | bytes 1179656 | tf_op jit(solution)/shard_map/ppermute | solution.py:322
  81.3 10.6 %collective-permute-start.22 = (bf16[10,128,128]{2,1,0:T(8,128)(2,1)S(1)}, bf16[10,128,128]{2,1,0:T(8,128)(2,1)S(1)}, u32[]{:S(2)}, u32[]{:S(2)}) collective-permute-start(bf16[10,128,128]{2,1,0:T(8,128)(2,1)S(1)} %get-tuple-element.255), channel_id=1, source_target_pairs={{0,96},{8,104},{16,112},{24,120},{32,64},{40,72},{48,80},{56,88},{... | collective-permute-start | bytes 983048 | tf_op jit(solution)/shard_map/ppermute | solution.py:322
  83.5 21.2 %collective-permute-start.24 = (bf16[10,128,128]{2,1,0:T(8,128)(2,1)S(1)}, bf16[10,128,128]{2,1,0:T(8,128)(2,1)S(1)}, u32[]{:S(2)}, u32[]{:S(2)}) collective-permute-start(bf16[10,128,128]{2,1,0:T(8,128)(2,1)S(1)} %get-tuple-element.259), channel_id=1, source_target_pairs={{0,16},{8,24},{16,0},{24,8},{32,48},{40,56},{48,32},{56,40},{64,80... | collective-permute-start | bytes 983048 | tf_op jit(solution)/shard_map/ppermute | solution.py:322
  86.2 23.3 %collective-permute-start.27 = (bf16[24,128,128]{2,1,0:T(8,128)(2,1)S(1)}, bf16[24,128,128]{2,1,0:T(8,128)(2,1)S(1)}, u32[]{:S(2)}, u32[]{:S(2)}) collective-permute-start(bf16[24,128,128]{2,1,0:T(8,128)(2,1)S(1)} %get-tuple-element.265), channel_id=1, source_target_pairs={{0,16},{8,24},{16,0},{24,8},{32,48},{40,56},{48,32},{56,40},{64,80... | collective-permute-start | bytes 2359304 | tf_op jit(solution)/shard_map/ppermute | solution.py:322
  92.0 29.7 %collective-permute-start.28 = (bf16[20,128,128]{2,1,0:T(8,128)(2,1)S(1)}, bf16[20,128,128]{2,1,0:T(8,128)(2,1)S(1)}, u32[]{:S(2)}, u32[]{:S(2)}) collective-permute-start(bf16[20,128,128]{2,1,0:T(8,128)(2,1)S(1)} %get-tuple-element.268), channel_id=1, source_target_pairs={{0,32},{8,40},{16,48},{24,56},{32,0},{40,8},{48,16},{56,24},{64,96... | collective-permute-start | bytes 1966088 | tf_op jit(solution)/shard_map/ppermute | solution.py:322
  106.7 18.7 %collective-permute-start.29 = (bf16[20,128,128]{2,1,0:T(8,128)(2,1)S(1)}, bf16[20,128,128]{2,1,0:T(8,128)(2,1)S(1)}, u32[]{:S(2)}, u32[]{:S(2)}) collective-permute-start(bf16[20,128,128]{2,1,0:T(8,128)(2,1)S(1)} %get-tuple-element.271), channel_id=1, source_target_pairs={{0,96},{8,104},{16,112},{24,120},{32,64},{40,72},{48,80},{56,88},{... | collective-permute-start | bytes 1966088 | tf_op jit(solution)/shard_map/ppermute | solution.py:322
  109.7 20.2 %collective-permute-start.30 = (bf16[12,128,128]{2,1,0:T(8,128)(2,1)S(1)}, bf16[12,128,128]{2,1,0:T(8,128)(2,1)S(1)}, u32[]{:S(2)}, u32[]{:S(2)}) collective-permute-start(bf16[12,128,128]{2,1,0:T(8,128)(2,1)S(1)} %get-tuple-element.274), channel_id=1, source_target_pairs={{0,32},{8,40},{16,48},{24,56},{32,0},{40,8},{48,16},{56,24},{64,96... | collective-permute-start | bytes 1179656 | tf_op jit(solution)/shard_map/ppermute | solution.py:322
  121.9 11.9 %collective-permute-start.32 = (bf16[10,128,128]{2,1,0:T(8,128)(2,1)S(1)}, bf16[10,128,128]{2,1,0:T(8,128)(2,1)S(1)}, u32[]{:S(2)}, u32[]{:S(2)}) collective-permute-start(bf16[10,128,128]{2,1,0:T(8,128)(2,1)S(1)} %get-tuple-element.278), channel_id=1, source_target_pairs={{0,96},{8,104},{16,112},{24,120},{32,64},{40,72},{48,80},{56,88},{... | collective-permute-start | bytes 983048 | tf_op jit(solution)/shard_map/ppermute | solution.py:322
  125.5 9.1 %collective-permute-start.34 = (bf16[10,128,128]{2,1,0:T(8,128)(2,1)S(1)}, bf16[10,128,128]{2,1,0:T(8,128)(2,1)S(1)}, u32[]{:S(2)}, u32[]{:S(2)}) collective-permute-start(bf16[10,128,128]{2,1,0:T(8,128)(2,1)S(1)} %get-tuple-element.282), channel_id=1, source_target_pairs={{0,16},{8,24},{16,0},{24,8},{32,48},{40,56},{48,32},{56,40},{64,80... | collective-permute-start | bytes 983048 | tf_op jit(solution)/shard_map/ppermute | solution.py:322
  126.2 8.6 %collective-permute-start.25 = (bf16[5,128,128]{2,1,0:T(8,128)(2,1)S(1)}, bf16[5,128,128]{2,1,0:T(8,128)(2,1)S(1)}, u32[]{:S(2)}, u32[]{:S(2)}) collective-permute-start(bf16[5,128,128]{2,1,0:T(8,128)(2,1)S(1)} %get-tuple-element.261), channel_id=1, source_target_pairs={{0,32},{8,40},{16,48},{24,56},{32,0},{40,8},{48,16},{56,24},{64,96... | collective-permute-start | bytes 491528 | tf_op jit(solution)/shard_map/ppermute | solution.py:322
  126.2 13.2 %collective-permute-start.21 = (bf16[6,128,128]{2,1,0:T(8,128)(2,1)S(1)}, bf16[6,128,128]{2,1,0:T(8,128)(2,1)S(1)}, u32[]{:S(2)}, u32[]{:S(2)}) collective-permute-start(bf16[6,128,128]{2,1,0:T(8,128)(2,1)S(1)} %get-tuple-element.253), channel_id=1, source_target_pairs={{0,96},{8,104},{16,112},{24,120},{32,64},{40,72},{48,80},{56,88},{... | collective-permute-start | bytes 589832 | tf_op jit(solution)/shard_map/ppermute | solution.py:322
  129.9 11.2 %collective-permute-start.31 = (bf16[6,128,128]{2,1,0:T(8,128)(2,1)S(1)}, bf16[6,128,128]{2,1,0:T(8,128)(2,1)S(1)}, u32[]{:S(2)}, u32[]{:S(2)}) collective-permute-start(bf16[6,128,128]{2,1,0:T(8,128)(2,1)S(1)} %get-tuple-element.276), channel_id=1, source_target_pairs={{0,96},{8,104},{16,112},{24,120},{32,64},{40,72},{48,80},{56,88},{... | collective-permute-start | bytes 589832 | tf_op jit(solution)/shard_map/ppermute | solution.py:322
  133.9 5.4 %collective-permute-start.23 = (bf16[5,128,128]{2,1,0:T(8,128)(2,1)S(1)}, bf16[5,128,128]{2,1,0:T(8,128)(2,1)S(1)}, u32[]{:S(2)}, u32[]{:S(2)}) collective-permute-start(bf16[5,128,128]{2,1,0:T(8,128)(2,1)S(1)} %get-tuple-element.257), channel_id=1, source_target_pairs={{0,16},{8,24},{16,0},{24,8},{32,48},{40,56},{48,32},{56,40},{64,80... | collective-permute-start | bytes 491528 | tf_op jit(solution)/shard_map/ppermute | solution.py:322
  134.7 5.4 %collective-permute-start.35 = (bf16[5,128,128]{2,1,0:T(8,128)(2,1)S(1)}, bf16[5,128,128]{2,1,0:T(8,128)(2,1)S(1)}, u32[]{:S(2)}, u32[]{:S(2)}) collective-permute-start(bf16[5,128,128]{2,1,0:T(8,128)(2,1)S(1)} %get-tuple-element.284), channel_id=1, source_target_pairs={{0,32},{8,40},{16,48},{24,56},{32,0},{40,8},{48,16},{56,24},{64,96... | collective-permute-start | bytes 491528 | tf_op jit(solution)/shard_map/ppermute | solution.py:322
  134.8 6.3 %collective-permute-start.33 = (bf16[5,128,128]{2,1,0:T(8,128)(2,1)S(1)}, bf16[5,128,128]{2,1,0:T(8,128)(2,1)S(1)}, u32[]{:S(2)}, u32[]{:S(2)}) collective-permute-start(bf16[5,128,128]{2,1,0:T(8,128)(2,1)S(1)} %get-tuple-element.280), channel_id=1, source_target_pairs={{0,16},{8,24},{16,0},{24,8},{32,48},{40,56},{48,32},{56,40},{64,80... | collective-permute-start | bytes 491528 | tf_op jit(solution)/shard_map/ppermute | solution.py:322
  (4 other events, 6.9 us)

commit v2 on v1

--- a/solution.py
+++ b/solution.py
@@ -218,31 +218,40 @@
     )(asked, in_hbm(emission))
 
 
-def tiles_kernel(first, per, with_add, *refs):
+def tiles_kernel(first, per, with_add, rolled, *refs):
     groups_ref, places_ref, table_ref, wt_ref, e_ref = refs[:5]
     outs = refs[6:] if with_add else refs[5:]
     last = e_ref.shape[0] - 1
     n = 0
     for out_ref in outs:
-        for j in range(out_ref.shape[0] // per):
-            g = groups_ref[n]
+        size = out_ref.shape[0] // per
+
+        def one(j, carry, out_ref=out_ref, n=n):
+            g = groups_ref[n + j]
             for q in range(per):
                 row = table_ref[g, first + q]
                 col = jnp.minimum(table_ref[g, GRP + first + q], last)
                 acc = jnp.dot(wt_ref[row], e_ref[col], preferred_element_type=F32)
                 if with_add:
-                    acc = acc + refs[5][places_ref[n] * per + q].astype(F32)
+                    acc = acc + refs[5][places_ref[n + j] * per + q].astype(F32)
                 out_ref[j * per + q] = acc.astype(BF16)
-            n += 1
-
-
-def tiles(groups, places, table, wt, e_blocks, first, per, outs, add=None):
+            return carry
+
+        if rolled:
+            lax.fori_loop(0, size, one, 0)
+        else:
+            for j in range(size):
+                one(j, 0)
+        n += size
+
+
+def tiles(groups, places, table, wt, e_blocks, first, per, outs, rolled, add=None):
     smem = pl.BlockSpec(memory_space=pltpu.SMEM)
     vmem = pl.BlockSpec(memory_space=pltpu.VMEM)
     count = groups.shape[0] * per
     with_add = add is not None
     return pl.pallas_call(
-        functools.partial(tiles_kernel, first, per, with_add),
+        functools.partial(tiles_kernel, first, per, with_add, rolled),
         in_specs=[smem, smem, smem, vmem, vmem] + ([vmem] if with_add else []),
         out_specs=[vmem] * outs,
         out_shape=[jax.ShapeDtypeStruct((count // outs, BLK, BLK), BF16)] * outs,
@@ -283,30 +292,38 @@
 
 def finish_kernel(firsts, me_ref, count_ref, table_ref, *refs):
     me = me_ref[0]
-    out_ref, stage, sem = refs[-3:]
+    out_ref, done_ref, stage, sem = refs[-4:]
+    n = 0
     for i, first in enumerate(firsts):
         mine, came = refs[2 * i], refs[2 * i + 1]
         for j in range(mine.shape[0]):
             s = table_ref[me, 2 * GRP + first + j]
             live = jnp.where(me * GRP + s < count_ref[0], 1.0, 0.0).astype(F32)
-            stage[first + j] = (mine[j].astype(F32) + came[j].astype(F32)) * live
-            pltpu.make_async_copy(stage.at[first + j], out_ref.at[s], sem).start()
-    pltpu.make_async_copy(stage, out_ref, sem).wait()
-
-
-def finish(me, counts, table, pairs, firsts):
+            stage[n] = (mine[j].astype(F32) + came[j].astype(F32)) * live
+            pltpu.make_async_copy(stage.at[n], out_ref.at[s], sem).start()
+            n += 1
+    done_ref[...] = jnp.zeros_like(done_ref)
+    pltpu.make_async_copy(stage, out_ref.at[pl.ds(0, n)], sem).wait()
+
+
+def finish(me, counts, table, pairs, firsts, out=None):
     smem = pl.BlockSpec(memory_space=pltpu.SMEM)
     vmem = pl.BlockSpec(memory_space=pltpu.VMEM)
+    hbm = pl.BlockSpec(memory_space=pltpu.HBM)
     flat = [a for pair in pairs for a in pair]
+    n = sum(mine.shape[0] for mine, _ in pairs)
+    given = out is not None
     return pl.pallas_call(
         functools.partial(finish_kernel, firsts),
-        in_specs=[smem, smem, smem] + [vmem] * len(flat),
-        out_specs=pl.BlockSpec(memory_space=pltpu.HBM),
-        out_shape=pltpu.HBM((GRP, BLK, BLK), F32),
-        scratch_shapes=[pltpu.VMEM((GRP, BLK, BLK), F32), pltpu.SemaphoreType.DMA],
+        in_specs=[smem, smem, smem] + [vmem] * len(flat)
+        + ([hbm, pl.BlockSpec(memory_space=pl.ANY)] if given else []),
+        out_specs=[hbm, vmem],
+        out_shape=[pltpu.HBM((GRP, BLK, BLK), F32), jax.ShapeDtypeStruct((8, BLK), F32)],
+        input_output_aliases={3 + len(flat): 0} if given else {},
+        scratch_shapes=[pltpu.VMEM((n, BLK, BLK), F32), pltpu.SemaphoreType.DMA],
         compiler_params=pltpu.CompilerParams(vmem_limit_bytes=16 * 2**20),
         name="finish",
-    )(me, counts, table, *flat)
+    )(me, counts, table, *flat, *(out if given else ()))
 
 
 CORE, ALONG_X, UP_Y, DOWN_Y = 1, 2, 4, 12
@@ -336,29 +353,29 @@
     parts = lax.axis_size("tm")
     own = lax.axis_index("tile").astype(I32).reshape(1)
     me = lax.axis_index("tm").astype(I32).reshape(1)
-    half = GRP // 2
-    request, table = plan(own, counts, tile_list, owners, half)
+    cuts = ((6, 6, 6), (5, 5, 4))
+    split = sum(cuts[0])
+    request, table = plan(own, counts, tile_list, owners, split)
     asked = lax.all_to_all(request, "tile", split_axis=0, concat_axis=0, tiled=True)
     outgoing = pack(asked, emission)
     far = lax.all_to_all(outgoing, "tile", split_axis=0, concat_axis=0, tiled=True)
     crowded = jnp.any(asked[:, CAP] > 0)
-    weights = after(step_weights[:, None], crowded)
-
-    cuts = (6, 5, 5)
+    weights = step_weights[:, None]
+
     others = me ^ CORE ^ (2 * jnp.arange(parts // 2, dtype=I32))
-    offsets = [[c * half + sum(cuts[:i]) for i in range(len(cuts))] for c in range(2)]
-
-    def given(c, i, wt, e_blocks, last):
+    offsets = [[c * split + sum(cuts[c][:i]) for i in range(3)] for c in range(2)]
+
+    def given(c, i, wt, e_blocks, last, rolled=False):
         return tiles(
-            after(others, last), others, table, wt, e_blocks, offsets[c][i], cuts[i], 1
+            after(others, last), others, table, wt, e_blocks, offsets[c][i], cuts[c][i], 1, rolled
         )[0]
 
-    def kept(c, i, wt, e_blocks, last, core):
+    def kept(c, i, wt, e_blocks, last, core, rolled=False):
         masks = [m for lead in (1, 0) for m in order_masks(ORDERS[i], lead)]
         mine = me ^ jnp.array(masks, I32)
         places = jnp.array([m // 2 for m in masks], I32)
         return tiles(
-            after(mine, last), places, table, wt, e_blocks, offsets[c][i], cuts[i], 2, core
+            after(mine, last), places, table, wt, e_blocks, offsets[c][i], cuts[c][i], 2, rolled, core
         )
 
     def exchange(outs, step):
@@ -372,33 +389,23 @@
             outs.append(out)
         return outs, last
 
-    def first_kernels(c, wt, e_blocks):
-        last, cores = wt, []
-        for i in range(3):
-            last = given(c, i, wt, e_blocks, last)
-            cores.append(swap(last, CORE))
-        return cores, last
-
-    def second_kernels(c, wt, e_blocks, cores, last):
-        outs = []
-        for i in range(3):
-            outs.append(kept(c, i, wt, e_blocks, last, cores[i]))
-            last = outs[i][1]
-        return outs, last
-
     wt, e_blocks = prep(after(weights, outgoing), adjoint, emission)
-    cores, last = first_kernels(0, wt, e_blocks)
-    early, last = second_kernels(0, wt, e_blocks, cores, last)
+    last, cores, early = wt, [], []
+    for i in range(3):
+        last = given(0, i, wt, e_blocks, last)
+        cores.append(swap(last, CORE))
+    for i in range(3):
+        early.append(kept(0, i, wt, e_blocks, last, cores[i]))
+        last = early[i][1]
     early = exchange(early, 0)
     wt, e_blocks = prep(after(weights, last), adjoint, emission, far)
-    cores, last = [], wt
+    last, cores, late = wt, [], []
     for i in range(3):
         last = given(1, i, wt, e_blocks, last)
         cores.append(swap(last, CORE))
         if i == 0:
             early, last = halve(early, last)
             early = exchange(early, 1)
-    late = []
     for i in range(3):
         if i == 2:
             early, last = halve(early, last)
@@ -406,21 +413,27 @@
         late.append(kept(1, i, wt, e_blocks, last, cores[i]))
         last = late[i][1]
     late = exchange(late, 0)
-    late, last = halve(late, last)
-    late, last = halve(exchange(late, 1), last)
+    late, last = halve(late, (last, crowded))
+    out, done = finish(after(me, last), counts, table, early, tuple(offsets[0]))
+    late, last = halve(exchange(late, 1), done)
     late = exchange(late, 2)
-    firsts = tuple(offsets[0] + offsets[1])
+    out, _ = finish(me, counts, table, late, tuple(offsets[1]), (out, done))
 
     def crowded_group(state):
-        wt, e_blocks = prep(after(weights, state[1]), adjoint, emission, far)
-        cores, last = first_kernels(0, wt, e_blocks)
-        again, last = second_kernels(0, wt, e_blocks, cores, last)
+        out = state[1]
+        wt, e_blocks = prep(after(weights, out), adjoint, emission, far)
+        last, cores, again = wt, [], []
+        for i in range(3):
+            last = given(0, i, wt, e_blocks, last, True)
+            cores.append(swap(last, CORE))
+        for i in range(3):
+            again.append(kept(0, i, wt, e_blocks, last, cores[i], True))
+            last = again[i][1]
         for step in range(2):
             again, last = halve(exchange(again, step), last)
-        out = finish(me, counts, table, exchange(again, 2) + late, firsts)
+        out, _ = finish(me, counts, table, exchange(again, 2), tuple(offsets[0]), (out, counts))
         return jnp.zeros((), bool), out
 
-    out = finish(me, counts, table, early + late, firsts)
     return lax.while_loop(lambda state: state[0], crowded_group, (crowded, out))[1][None]
 
 

time: 146 us -> 136 us (0.932); the launches traced: 144 us -> 136 us
  starting transfers between devices: 49.8 us -> 35.2 us
  waiting for transfers between devices: 33.1 us -> 36.9 us
  Pallas kernels: 54.8 us -> 57.9 us
    ppermute x24, starting transfers between devices: 37.6 us -> 22.9 us  [swap(): return lax.ppermute(a, 'tm', [(i, i ^ mask) for i in range(n)])]
    ppermute x24, waiting for transfers between devices: 22.8 us -> 26.6 us  [swap(): return lax.ppermute(a, 'tm', [(i, i ^ mask) for i in range(n)])]
    pallas_call x1 -> x2, Pallas kernels: 1.97 us -> 3.86 us  [finish(): pl.pallas_call(functools.partial(finish_kernel, firsts), in_specs=[smem,...]
  transfers between devices with their start and end apart: 26 -> 26, of which waited for: 12 -> 12; matrix products, arithmetic and copies ran while one was open for 1% -> 1% of each run, Pallas kernels for 32% -> 36%
where the time goes in v2:
time: 136 us
  Pallas kernels  57.9 us (43%)
  waiting for transfers between devices  36.9 us (27%)
  starting transfers between devices  35.2 us (26%)
  local copies, waits for them, and re-layouts  2.84 us (2%)
    ppermute x24, waiting for transfers between devices, swap(): return lax.ppermute(a, 'tm', [(i, i ^ mask) for i in range(n)])  26.6 us
    pallas_call x12, Pallas kernels, tiles(): pl.pallas_call(functools.partial(tiles_kernel, first, per, with_add, roll...  25.5 us
    ppermute x24, starting transfers between devices, swap(): return lax.ppermute(a, 'tm', [(i, i ^ mask) for i in range(n)])  22.9 us
    pallas_call x2, Pallas kernels, prep(): pl.pallas_call(functools.partial(prep_kernel, with_far), in_specs=[vmem]...  18.4 us
    all_to_all x1, starting transfers between devices, body(): lax.all_to_all(request, 'tile', split_axis=0, concat_axis=0, tiled=True)  7.86 us
    all_to_all x1, waiting for transfers between devices, body(): lax.all_to_all(request, 'tile', split_axis=0, concat_axis=0, tiled=True)  6.9 us
    all_to_all x1, starting transfers between devices, body(): lax.all_to_all(outgoing, 'tile', split_axis=0, concat_axis=0, tiled=True)  4.41 us
    pallas_call x1, Pallas kernels, pack(): pl.pallas_call(pack_kernel, in_specs=[pl.BlockSpec(memory_space=pltpu.SME...  4.23 us
  transfers between devices with their start and end apart: 26, of which 12 were waited for; matrix products, arithmetic and copies ran while one was open for 1% of the time, Pallas kernels for 36%

profile of v2, /device:TPU:0, one launch (start us, length us, event | category | flops | bytes accessed | tf_op | source)
XLA Modules:
  0.0 135.6 jit_solution(9360481438709294189)
XLA Ops:
  1.5 2.1 %plan.1 = (s32[8,128]{1,0:T(8,128)}, s32[16,128]{1,0:T(8,128)S(1)}) custom-call(s32[1]{0:T(128)} %bitcast.own_ref, s32[1]{0:T(128)S(6)} %copy.45.count_ref, s32[512,2]{1,0:T(8,128)S(1)} %copy.31.tiles_ref), custom_call_target="tpu_custom_call" | custom-call | tf_op jit(solution)/shard_map/plan/pallas_call | solution.py:87
  3.6 7.9 %all-to-all-start = ((s32[8,1,128]{2,1,0:T(1,128)}), s32[8,1,128]{2,1,0:T(1,128)S(1)}, u32[]{:S(2)}, u32[]{:S(2)}) async-start(s32[8,1,128]{2,1,0:T(1,128)} %bitcast.2), calls=%async_computation | async-start | bytes 8192 | tf_op jit(solution)/shard_map/all_to_all | solution.py:359
  12.1 6.9 %all-to-all-done = s32[8,1,128]{2,1,0:T(1,128)S(1)} async-done(((s32[8,1,128]{2,1,0:T(1,128)}), s32[8,1,128]{2,1,0:T(1,128)S(1)}, u32[]{:S(2)}, u32[]{:S(2)}) %all-to-all-start) | async-done | bytes 4128 | tf_op jit(solution)/shard_map/all_to_all | solution.py:359
  19.0 4.2 %pack.1 = bf16[32,320,128]{2,1,0:T(8,128)(2,1)} custom-call(s32[8,128]{1,0:T(8,128)S(1)} %bitcast.9, bf16[320,16384]{1,0:T(8,128)(2,1)} %em_ref.5), custom_call_target="tpu_custom_call" | custom-call | tf_op jit(solution)/shard_map/pack/pallas_call | solution.py:210
  23.2 4.4 %all-to-all-start.1 = ((bf16[32,320,128]{2,1,0:T(8,128)(2,1)}), bf16[32,320,128]{2,1,0:T(8,128)(2,1)}, u32[]{:S(2)}, u32[]{:S(2)}) async-start(bf16[32,320,128]{2,1,0:T(8,128)(2,1)} %pack.1), calls=%async_computation.1 | async-start | bytes 5242880 | tf_op jit(solution)/shard_map/all_to_all | solution.py:361
  27.8 8.9 %prep.3 = (bf16[128,128,384]{2,1,0:T(8,128)(2,1)S(1)}, bf16[128,384,128]{2,1,0:T(8,128)(2,1)S(1)}) custom-call(f32[320,1]{1,0:T(8,128)S(1)} %copy.33.weights_ref, bf16[320,16384]{1,0:T(8,128)(2,1)} %adj_ref.3, bf16[320,16384]{1,0:T(8,128)(2,1)} %em_ref.5), custom_call_target="tpu_custom_call" | custom-call | tf_op jit(solution)/shard_map/prep/pallas_call | solution.py:169
  36.7 2.1 %tiles.18 = bf16[48,128,128]{2,1,0:T(8,128)(2,1)S(1)} custom-call(s32[8]{0:T(128)S(1)} %multiply_xor_fusion.1.refs_0_.refs_1_, s32[8]{0:T(128)S(1)} %multiply_xor_fusion.1.refs_0_.refs_1_, s32[16,128]{1,0:T(8,128)S(1)} %get-tuple-element.487.refs_2_.table_ref, bf16[128,128,384]{2,1,0:T(8,128)(2,1)S(1)} %get-tuple-element.195.refs_3_, ...), custom_call_target="tpu_custom_call" | custom-call | tf_op jit(solution)/shard_map/tiles/pallas_call | solution.py:253
  38.9 2.1 %tiles.19 = bf16[48,128,128]{2,1,0:T(8,128)(2,1)S(1)} custom-call(s32[8]{0:T(128)S(1)} %multiply_xor_fusion.1.refs_0_.refs_1_, s32[8]{0:T(128)S(1)} %multiply_xor_fusion.1.refs_0_.refs_1_, s32[16,128]{1,0:T(8,128)S(1)} %get-tuple-element.487.refs_2_.table_ref, bf16[128,128,384]{2,1,0:T(8,128)(2,1)S(1)} %get-tuple-element.195.refs_3_, ...), custom_call_target="tpu_custom_call" | custom-call | tf_op jit(solution)/shard_map/tiles/pallas_call | solution.py:253
  41.6 2.1 %tiles.20 = bf16[48,128,128]{2,1,0:T(8,128)(2,1)S(1)} custom-call(s32[8]{0:T(128)S(1)} %multiply_xor_fusion.1.refs_0_.refs_1_, s32[8]{0:T(128)S(1)} %multiply_xor_fusion.1.refs_0_.refs_1_, s32[16,128]{1,0:T(8,128)S(1)} %get-tuple-element.487.refs_2_.table_ref, bf16[128,128,384]{2,1,0:T(8,128)(2,1)S(1)} %get-tuple-element.195.refs_3_, ...), custom_call_target="tpu_custom_call" | custom-call | tf_op jit(solution)/shard_map/tiles/pallas_call | solution.py:253
  43.9 2.8 %tiles.21 = (bf16[24,128,128]{2,1,0:T(8,128)(2,1)}, bf16[24,128,128]{2,1,0:T(8,128)(2,1)S(1)}) custom-call(s32[8]{0:T(128)S(1)} %broadcast_xor_fusion.5.refs_0_, s32[8]{0:T(128)S(1)} %copy-done.7, s32[16,128]{1,0:T(8,128)S(1)} %get-tuple-element.487.refs_2_.table_ref, bf16[128,128,384]{2,1,0:T(8,128)(2,1)S(1)} %get-tuple-element.195.refs_3_, ...), custom_call_target="tpu_custom_call" | custom-call | tf_op jit(solution)/shard_map/tiles/pallas_call | solution.py:253
  47.3 2.8 %tiles.22 = (bf16[24,128,128]{2,1,0:T(8,128)(2,1)}, bf16[24,128,128]{2,1,0:T(8,128)(2,1)S(1)}) custom-call(s32[8]{0:T(128)S(1)} %broadcast_xor_fusion.3.refs_0_, s32[8]{0:T(128)S(1)} %copy-done.6, s32[16,128]{1,0:T(8,128)S(1)} %get-tuple-element.487.refs_2_.table_ref, bf16[128,128,384]{2,1,0:T(8,128)(2,1)S(1)} %get-tuple-element.195.refs_3_, ...), custom_call_target="tpu_custom_call" | custom-call | tf_op jit(solution)/shard_map/tiles/pallas_call | solution.py:253
  51.6 2.9 %tiles.23 = (bf16[24,128,128]{2,1,0:T(8,128)(2,1)}, bf16[24,128,128]{2,1,0:T(8,128)(2,1)S(1)}) custom-call(s32[8]{0:T(128)S(1)} %broadcast_xor_fusion.4.refs_0_, s32[8]{0:T(128)S(1)} %copy-done.5, s32[16,128]{1,0:T(8,128)S(1)} %get-tuple-element.487.refs_2_.table_ref, bf16[128,128,384]{2,1,0:T(8,128)(2,1)S(1)} %get-tuple-element.195.refs_3_, ...), custom_call_target="tpu_custom_call" | custom-call | tf_op jit(solution)/shard_map/tiles/pallas_call | solution.py:253
  55.4 2.2 %collective-permute-start.17 = (bf16[24,128,128]{2,1,0:T(8,128)(2,1)}, bf16[24,128,128]{2,1,0:T(8,128)(2,1)S(1)}, u32[]{:S(2)}, u32[]{:S(2)}) collective-permute-start(bf16[24,128,128]{2,1,0:T(8,128)(2,1)} %get-tuple-element.217), channel_id=1, source_target_pairs={{0,96},{8,104},{16,112},{24,120},{32,64},{40,72},{48,80},{56,88},{... | collective-permute-start | bytes 2359304 | tf_op jit(solution)/shard_map/ppermute | solution.py:339
  57.7 3.4 %all-to-all-done.1.refs_0_ = bf16[32,320,128]{2,1,0:T(8,128)(2,1)} async-done(((bf16[32,320,128]{2,1,0:T(8,128)(2,1)}), bf16[32,320,128]{2,1,0:T(8,128)(2,1)}, u32[]{:S(2)}, u32[]{:S(2)}) %all-to-all-start.1) | async-done | bytes 2621472 | tf_op jit(solution)/shard_map/all_to_all | solution.py:361
  61.1 9.5 %prep.4 = (bf16[128,128,384]{2,1,0:T(8,128)(2,1)S(1)}, bf16[160,384,128]{2,1,0:T(8,128)(2,1)S(1)}) custom-call(f32[320,1]{1,0:T(8,128)S(1)} %copy.34.weights_ref, bf16[320,16384]{1,0:T(8,128)(2,1)} %adj_ref.3, bf16[320,16384]{1,0:T(8,128)(2,1)} %em_ref.5, bf16[32,320,128]{2,1,0:T(8,128)(2,1)} %all-to-all-done.1.refs_0_), custom_call_target="tpu_custom_call" | custom-call | tf_op jit(solution)/shard_map/prep/pallas_call | solution.py:169
  70.6 1.9 %tiles.24 = bf16[40,128,128]{2,1,0:T(8,128)(2,1)S(1)} custom-call(s32[8]{0:T(128)S(1)} %multiply_xor_fusion.1.refs_0_.refs_1_, s32[8]{0:T(128)S(1)} %multiply_xor_fusion.1.refs_0_.refs_1_, s32[16,128]{1,0:T(8,128)S(1)} %get-tuple-element.487.refs_2_.table_ref, bf16[128,128,384]{2,1,0:T(8,128)(2,1)S(1)} %get-tuple-element.207.refs_3_, ...), custom_call_target="tpu_custom_call" | custom-call | tf_op jit(solution)/shard_map/tiles/pallas_call | solution.py:253
  76.4 1.9 %tiles.25 = bf16[40,128,128]{2,1,0:T(8,128)(2,1)S(1)} custom-call(s32[8]{0:T(128)S(1)} %multiply_xor_fusion.1.refs_0_.refs_1_, s32[8]{0:T(128)S(1)} %multiply_xor_fusion.1.refs_0_.refs_1_, s32[16,128]{1,0:T(8,128)S(1)} %get-tuple-element.487.refs_2_.table_ref, bf16[128,128,384]{2,1,0:T(8,128)(2,1)S(1)} %get-tuple-element.207.refs_3_, ...), custom_call_target="tpu_custom_call" | custom-call | tf_op jit(solution)/shard_map/tiles/pallas_call | solution.py:253
  78.3 1.7 %tiles.26 = bf16[32,128,128]{2,1,0:T(8,128)(2,1)S(1)} custom-call(s32[8]{0:T(128)S(1)} %multiply_xor_fusion.1.refs_0_.refs_1_, s32[8]{0:T(128)S(1)} %multiply_xor_fusion.1.refs_0_.refs_1_, s32[16,128]{1,0:T(8,128)S(1)} %get-tuple-element.487.refs_2_.table_ref, bf16[128,128,384]{2,1,0:T(8,128)(2,1)S(1)} %get-tuple-element.207.refs_3_, ...), custom_call_target="tpu_custom_call" | custom-call | tf_op jit(solution)/shard_map/tiles/pallas_call | solution.py:253
  81.5 2.2 %collective-permute-start.21 = (bf16[12,128,128]{2,1,0:T(8,128)(2,1)S(1)}, bf16[12,128,128]{2,1,0:T(8,128)(2,1)S(1)}, u32[]{:S(2)}, u32[]{:S(2)}) collective-permute-start(bf16[12,128,128]{2,1,0:T(8,128)(2,1)S(1)} %get-tuple-element.229), channel_id=1, source_target_pairs={{0,96},{8,104},{16,112},{24,120},{32,64},{40,72},{48,80},{56,88},{... | collective-permute-start | bytes 1179656 | tf_op jit(solution)/shard_map/ppermute | solution.py:339
  85.0 1.9 %tiles.27 = (bf16[20,128,128]{2,1,0:T(8,128)(2,1)S(1)}, bf16[20,128,128]{2,1,0:T(8,128)(2,1)S(1)}) custom-call(s32[8]{0:T(128)S(1)} %broadcast_xor_fusion.5.refs_0_, s32[8]{0:T(128)S(1)} %copy-done.7, s32[16,128]{1,0:T(8,128)S(1)} %get-tuple-element.487.refs_2_.table_ref, bf16[128,128,384]{2,1,0:T(8,128)(2,1)S(1)} %get-tuple-element.207.refs_3_, ...), custom_call_target="tpu_custom_call" | custom-call | tf_op jit(solution)/shard_map/tiles/pallas_call | solution.py:253
  87.7 1.9 %tiles.28 = (bf16[20,128,128]{2,1,0:T(8,128)(2,1)S(1)}, bf16[20,128,128]{2,1,0:T(8,128)(2,1)S(1)}) custom-call(s32[8]{0:T(128)S(1)} %broadcast_xor_fusion.3.refs_0_, s32[8]{0:T(128)S(1)} %copy-done.6, s32[16,128]{1,0:T(8,128)S(1)} %get-tuple-element.487.refs_2_.table_ref, bf16[128,128,384]{2,1,0:T(8,128)(2,1)S(1)} %get-tuple-element.207.refs_3_, ...), custom_call_target="tpu_custom_call" | custom-call | tf_op jit(solution)/shard_map/tiles/pallas_call | solution.py:253
  89.6 2.1 %collective-permute-done.20.refs_1_ = bf16[12,128,128]{2,1,0:T(8,128)(2,1)S(1)} collective-permute-done((bf16[12,128,128]{2,1,0:T(8,128)(2,1)S(1)}, bf16[12,128,128]{2,1,0:T(8,128)(2,1)S(1)}, u32[]{:S(2)}, u32[]{:S(2)}) %collective-permute-start.20) | collective-permute-done | bytes 393248 | tf_op jit(solution)/shard_map/ppermute | solution.py:339
  93.9 1.8 %collective-permute-done.22.refs_1_ = bf16[12,128,128]{2,1,0:T(8,128)(2,1)S(1)} collective-permute-done((bf16[12,128,128]{2,1,0:T(8,128)(2,1)S(1)}, bf16[12,128,128]{2,1,0:T(8,128)(2,1)S(1)}, u32[]{:S(2)}, u32[]{:S(2)}) %collective-permute-start.22) | collective-permute-done | bytes 393248 | tf_op jit(solution)/shard_map/ppermute | solution.py:339
  95.8 1.7 %tiles.29 = (bf16[16,128,128]{2,1,0:T(8,128)(2,1)S(1)}, bf16[16,128,128]{2,1,0:T(8,128)(2,1)S(1)}) custom-call(s32[8]{0:T(128)S(1)} %broadcast_xor_fusion.4.refs_0_, s32[8]{0:T(128)S(1)} %copy-done.5, s32[16,128]{1,0:T(8,128)S(1)} %get-tuple-element.487.refs_2_.table_ref, bf16[128,128,384]{2,1,0:T(8,128)(2,1)S(1)} %get-tuple-element.207.refs_3_, ...), custom_call_target="tpu_custom_call" | custom-call | tf_op jit(solution)/shard_map/tiles/pallas_call | solution.py:253
  99.6 9.0 %collective-permute-done.24.refs_1_ = bf16[20,128,128]{2,1,0:T(8,128)(2,1)S(1)} collective-permute-done((bf16[20,128,128]{2,1,0:T(8,128)(2,1)S(1)}, bf16[20,128,128]{2,1,0:T(8,128)(2,1)S(1)}, u32[]{:S(2)}, u32[]{:S(2)}) %collective-permute-start.24) | collective-permute-done | bytes 655392 | tf_op jit(solution)/shard_map/ppermute | solution.py:339
  109.7 2.6 %collective-permute-start.32 = (bf16[10,128,128]{2,1,0:T(8,128)(2,1)S(1)}, bf16[10,128,128]{2,1,0:T(8,128)(2,1)S(1)}, u32[]{:S(2)}, u32[]{:S(2)}) collective-permute-start(bf16[10,128,128]{2,1,0:T(8,128)(2,1)S(1)} %get-tuple-element.255), channel_id=1, source_target_pairs={{0,96},{8,104},{16,112},{24,120},{32,64},{40,72},{48,80},{56,88},{... | collective-permute-start | bytes 983048 | tf_op jit(solution)/shard_map/ppermute | solution.py:339
  114.5 1.7 %collective-permute-start.27 = (bf16[6,128,128]{2,1,0:T(8,128)(2,1)S(1)}, bf16[6,128,128]{2,1,0:T(8,128)(2,1)S(1)}, u32[]{:S(2)}, u32[]{:S(2)}) collective-permute-start(bf16[6,128,128]{2,1,0:T(8,128)(2,1)S(1)} %get-tuple-element.246), channel_id=1, source_target_pairs={{0,96},{8,104},{16,112},{24,120},{32,64},{40,72},{48,80},{56,88},{... | collective-permute-start | bytes 589832 | tf_op jit(solution)/shard_map/ppermute | solution.py:339
  116.2 5.6 %collective-permute-done.28.refs_3_ = bf16[6,128,128]{2,1,0:T(8,128)(2,1)S(1)} collective-permute-done((bf16[6,128,128]{2,1,0:T(8,128)(2,1)S(1)}, bf16[6,128,128]{2,1,0:T(8,128)(2,1)S(1)}, u32[]{:S(2)}, u32[]{:S(2)}) %collective-permute-start.28) | collective-permute-done | bytes 196640 | tf_op jit(solution)/shard_map/ppermute | solution.py:339
  121.8 1.6 %collective-permute-done.27.refs_1_ = bf16[6,128,128]{2,1,0:T(8,128)(2,1)S(1)} collective-permute-done((bf16[6,128,128]{2,1,0:T(8,128)(2,1)S(1)}, bf16[6,128,128]{2,1,0:T(8,128)(2,1)S(1)}, u32[]{:S(2)}, u32[]{:S(2)}) %collective-permute-start.27) | collective-permute-done | bytes 196640 | tf_op jit(solution)/shard_map/ppermute | solution.py:339
  123.4 1.7 %finish.3 = (f32[32,128,128]{2,1,0:T(8,128)}, f32[8,128]{1,0:T(8,128)S(1)}) custom-call(s32[1]{0:T(128)} %bitcast.4.me_ref, s32[1]{0:T(128)S(6)} %copy.45.count_ref, s32[16,128]{1,0:T(8,128)S(1)} %get-tuple-element.487.refs_2_.table_ref, bf16[6,128,128]{2,1,0:T(8,128)(2,1)S(1)} %get-tuple-element.227.refs_0_, ...), custom_call_target="tpu_custom_call" | custom-call | tf_op jit(solution)/shard_map/finish/pallas_call | solution.py:316
  127.7 4.1 %collective-permute-done.31.refs_1_ = bf16[5,128,128]{2,1,0:T(8,128)(2,1)S(1)} collective-permute-done((bf16[5,128,128]{2,1,0:T(8,128)(2,1)S(1)}, bf16[5,128,128]{2,1,0:T(8,128)(2,1)S(1)}, u32[]{:S(2)}, u32[]{:S(2)}) %collective-permute-start.31) | collective-permute-done | bytes 163872 | tf_op jit(solution)/shard_map/ppermute | solution.py:339
  132.5 2.2 %finish.4 = (f32[32,128,128]{2,1,0:T(8,128)}, f32[8,128]{1,0:T(8,128)}) custom-call(s32[1]{0:T(128)} %bitcast.4.me_ref, s32[1]{0:T(128)S(6)} %copy.45.count_ref, s32[16,128]{1,0:T(8,128)S(1)} %get-tuple-element.487.refs_2_.table_ref, bf16[5,128,128]{2,1,0:T(8,128)(2,1)S(1)} %get-tuple-element.252.refs_0_, ...), custom_call_target="tpu_custom_call", output_to_operand_aliasing={{0}: (9, {})} | custom-call | tf_op jit(solution)/shard_map/finish/pallas_call | solution.py:316
  (77 shorter events, 24.8 us)
Async XLA Ops:
  3.6 15.4 %all-to-all-start = ((s32[8,1,128]{2,1,0:T(1,128)}), s32[8,1,128]{2,1,0:T(1,128)S(1)}, u32[]{:S(2)}, u32[]{:S(2)}) async-start(s32[8,1,128]{2,1,0:T(1,128)} %bitcast.2), calls=%async_computation | async-start | bytes 8192 | tf_op jit(solution)/shard_map/all_to_all | solution.py:359
  23.2 37.9 %all-to-all-start.1 = ((bf16[32,320,128]{2,1,0:T(8,128)(2,1)}), bf16[32,320,128]{2,1,0:T(8,128)(2,1)}, u32[]{:S(2)}, u32[]{:S(2)}) async-start(bf16[32,320,128]{2,1,0:T(8,128)(2,1)} %pack.1), calls=%async_computation.1 | async-start | bytes 5242880 | tf_op jit(solution)/shard_map/all_to_all | solution.py:361
  38.8 5.1 %collective-permute-start.12 = (bf16[48,128,128]{2,1,0:T(8,128)(2,1)S(1)}, bf16[48,128,128]{2,1,0:T(8,128)(2,1)S(1)}, u32[]{:S(2)}, u32[]{:S(2)}) collective-permute-start(bf16[48,128,128]{2,1,0:T(8,128)(2,1)S(1)} %tiles.18), channel_id=1, source_target_pairs={{0,8},{8,0},{16,24},{24,16},{32,40},{40,32},{48,56},{56,48},{64,72... | collective-permute-start | bytes 4718600 | tf_op jit(solution)/shard_map/ppermute | solution.py:339
  41.0 2.8 %copy-start.9 = (s32[8]{0:T(128)S(1)}, s32[8]{0:T(128)}, u32[]{:S(2)}) copy-start(s32[8]{0:T(128)} %constant.33.clone) | copy-start | bytes 100
  41.0 2.8 %copy-start.8 = (s32[8]{0:T(128)S(1)}, s32[8]{0:T(128)}, u32[]{:S(2)}) copy-start(s32[8]{0:T(128)} %constant.35.clone) | copy-start | bytes 100
  41.0 2.9 %copy-start.7 = (s32[8]{0:T(128)S(1)}, s32[8]{0:T(128)}, u32[]{:S(2)}) copy-start(s32[8]{0:T(128)} %constant.32.clone.refs_1_) | copy-start | bytes 100
  41.0 6.2 %collective-permute-start.13 = (bf16[48,128,128]{2,1,0:T(8,128)(2,1)S(1)}, bf16[48,128,128]{2,1,0:T(8,128)(2,1)S(1)}, u32[]{:S(2)}, u32[]{:S(2)}) collective-permute-start(bf16[48,128,128]{2,1,0:T(8,128)(2,1)S(1)} %tiles.19), channel_id=1, source_target_pairs={{0,8},{8,0},{16,24},{24,16},{32,40},{40,32},{48,56},{56,48},{64,72... | collective-permute-start | bytes 4718600 | tf_op jit(solution)/shard_map/ppermute | solution.py:339
  43.7 7.9 %collective-permute-start.14 = (bf16[48,128,128]{2,1,0:T(8,128)(2,1)S(1)}, bf16[48,128,128]{2,1,0:T(8,128)(2,1)S(1)}, u32[]{:S(2)}, u32[]{:S(2)}) collective-permute-start(bf16[48,128,128]{2,1,0:T(8,128)(2,1)S(1)} %tiles.20), channel_id=1, source_target_pairs={{0,8},{8,0},{16,24},{24,16},{32,40},{40,32},{48,56},{56,48},{64,72... | collective-permute-start | bytes 4718600 | tf_op jit(solution)/shard_map/ppermute | solution.py:339
  43.9 3.4 %copy-start.6 = (s32[8]{0:T(128)S(1)}, s32[8]{0:T(128)}, u32[]{:S(2)}) copy-start(s32[8]{0:T(128)} %constant.34.clone.refs_1_) | copy-start | bytes 100
  46.7 5.0 %copy-start.5 = (s32[8]{0:T(128)S(1)}, s32[8]{0:T(128)}, u32[]{:S(2)}) copy-start(s32[8]{0:T(128)} %constant.36.clone.refs_1_) | copy-start | bytes 100
  46.7 26.1 %collective-permute-start.15 = (bf16[24,128,128]{2,1,0:T(8,128)(2,1)}, bf16[24,128,128]{2,1,0:T(8,128)(2,1)}, u32[]{:S(2)}, u32[]{:S(2)}) collective-permute-start(bf16[24,128,128]{2,1,0:T(8,128)(2,1)} %get-tuple-element.211), channel_id=1, source_target_pairs={{0,16},{8,24},{16,0},{24,8},{32,48},{40,56},{48,32},{56,40},{64,80... | collective-permute-start | bytes 2359304 | tf_op jit(solution)/shard_map/ppermute | solution.py:339
  50.0 24.1 %collective-permute-start.16 = (bf16[24,128,128]{2,1,0:T(8,128)(2,1)}, bf16[24,128,128]{2,1,0:T(8,128)(2,1)}, u32[]{:S(2)}, u32[]{:S(2)}) collective-permute-start(bf16[24,128,128]{2,1,0:T(8,128)(2,1)} %get-tuple-element.214), channel_id=1, source_target_pairs={{0,32},{8,40},{16,48},{24,56},{32,0},{40,8},{48,16},{56,24},{64,96... | collective-permute-start | bytes 2359304 | tf_op jit(solution)/shard_map/ppermute | solution.py:339
  55.4 20.8 %collective-permute-start.17 = (bf16[24,128,128]{2,1,0:T(8,128)(2,1)}, bf16[24,128,128]{2,1,0:T(8,128)(2,1)S(1)}, u32[]{:S(2)}, u32[]{:S(2)}) collective-permute-start(bf16[24,128,128]{2,1,0:T(8,128)(2,1)} %get-tuple-element.217), channel_id=1, source_target_pairs={{0,96},{8,104},{16,112},{24,120},{32,64},{40,72},{48,80},{56,88},{... | collective-permute-start | bytes 2359304 | tf_op jit(solution)/shard_map/ppermute | solution.py:339
  72.5 3.6 %copy-start.1 = (bf16[24,128,128]{2,1,0:T(8,128)(2,1)S(1)}, bf16[24,128,128]{2,1,0:T(8,128)(2,1)}, u32[]{:S(2)}) copy-start(bf16[24,128,128]{2,1,0:T(8,128)(2,1)} %copy-done) | copy-start | bytes 2359300
  72.5 11.2 %collective-permute-start.18 = (bf16[40,128,128]{2,1,0:T(8,128)(2,1)S(1)}, bf16[40,128,128]{2,1,0:T(8,128)(2,1)S(1)}, u32[]{:S(2)}, u32[]{:S(2)}) collective-permute-start(bf16[40,128,128]{2,1,0:T(8,128)(2,1)S(1)} %tiles.24), channel_id=1, source_target_pairs={{0,8},{8,0},{16,24},{24,16},{32,40},{40,32},{48,56},{56,48},{64,72... | collective-permute-start | bytes 3932168 | tf_op jit(solution)/shard_map/ppermute | solution.py:339
  78.2 8.7 %collective-permute-start.19 = (bf16[40,128,128]{2,1,0:T(8,128)(2,1)S(1)}, bf16[40,128,128]{2,1,0:T(8,128)(2,1)S(1)}, u32[]{:S(2)}, u32[]{:S(2)}) collective-permute-start(bf16[40,128,128]{2,1,0:T(8,128)(2,1)S(1)} %tiles.25), channel_id=1, source_target_pairs={{0,8},{8,0},{16,24},{24,16},{32,40},{40,32},{48,56},{56,48},{64,72... | collective-permute-start | bytes 3932168 | tf_op jit(solution)/shard_map/ppermute | solution.py:339
  80.0 15.8 %collective-permute-start.23 = (bf16[32,128,128]{2,1,0:T(8,128)(2,1)S(1)}, bf16[32,128,128]{2,1,0:T(8,128)(2,1)S(1)}, u32[]{:S(2)}, u32[]{:S(2)}) collective-permute-start(bf16[32,128,128]{2,1,0:T(8,128)(2,1)S(1)} %tiles.26), channel_id=1, source_target_pairs={{0,8},{8,0},{16,24},{24,16},{32,40},{40,32},{48,56},{56,48},{64,72... | collective-permute-start | bytes 3145736 | tf_op jit(solution)/shard_map/ppermute | solution.py:339
  80.6 11.1 %collective-permute-start.20 = (bf16[12,128,128]{2,1,0:T(8,128)(2,1)S(1)}, bf16[12,128,128]{2,1,0:T(8,128)(2,1)S(1)}, u32[]{:S(2)}, u32[]{:S(2)}) collective-permute-start(bf16[12,128,128]{2,1,0:T(8,128)(2,1)S(1)} %get-tuple-element.226), channel_id=1, source_target_pairs={{0,32},{8,40},{16,48},{24,56},{32,0},{40,8},{48,16},{56,24},{64,96... | collective-permute-start | bytes 1179656 | tf_op jit(solution)/shard_map/ppermute | solution.py:339
  81.5 12.3 %collective-permute-start.21 = (bf16[12,128,128]{2,1,0:T(8,128)(2,1)S(1)}, bf16[12,128,128]{2,1,0:T(8,128)(2,1)S(1)}, u32[]{:S(2)}, u32[]{:S(2)}) collective-permute-start(bf16[12,128,128]{2,1,0:T(8,128)(2,1)S(1)} %get-tuple-element.229), channel_id=1, source_target_pairs={{0,96},{8,104},{16,112},{24,120},{32,64},{40,72},{48,80},{56,88},{... | collective-permute-start | bytes 1179656 | tf_op jit(solution)/shard_map/ppermute | solution.py:339
  83.7 12.0 %collective-permute-start.22 = (bf16[12,128,128]{2,1,0:T(8,128)(2,1)S(1)}, bf16[12,128,128]{2,1,0:T(8,128)(2,1)S(1)}, u32[]{:S(2)}, u32[]{:S(2)}) collective-permute-start(bf16[12,128,128]{2,1,0:T(8,128)(2,1)S(1)} %get-tuple-element.232), channel_id=1, source_target_pairs={{0,16},{8,24},{16,0},{24,8},{32,48},{40,56},{48,32},{56,40},{64,80... | collective-permute-start | bytes 1179656 | tf_op jit(solution)/shard_map/ppermute | solution.py:339
  86.9 21.6 %collective-permute-start.24 = (bf16[20,128,128]{2,1,0:T(8,128)(2,1)S(1)}, bf16[20,128,128]{2,1,0:T(8,128)(2,1)S(1)}, u32[]{:S(2)}, u32[]{:S(2)}) collective-permute-start(bf16[20,128,128]{2,1,0:T(8,128)(2,1)S(1)} %get-tuple-element.237), channel_id=1, source_target_pairs={{0,16},{8,24},{16,0},{24,8},{32,48},{40,56},{48,32},{56,40},{64,80... | collective-permute-start | bytes 1966088 | tf_op jit(solution)/shard_map/ppermute | solution.py:339
  91.7 17.8 %collective-permute-start.25 = (bf16[20,128,128]{2,1,0:T(8,128)(2,1)S(1)}, bf16[20,128,128]{2,1,0:T(8,128)(2,1)S(1)}, u32[]{:S(2)}, u32[]{:S(2)}) collective-permute-start(bf16[20,128,128]{2,1,0:T(8,128)(2,1)S(1)} %get-tuple-element.240), channel_id=1, source_target_pairs={{0,32},{8,40},{16,48},{24,56},{32,0},{40,8},{48,16},{56,24},{64,96... | collective-permute-start | bytes 1966088 | tf_op jit(solution)/shard_map/ppermute | solution.py:339
  97.5 14.7 %collective-permute-start.26 = (bf16[16,128,128]{2,1,0:T(8,128)(2,1)S(1)}, bf16[16,128,128]{2,1,0:T(8,128)(2,1)S(1)}, u32[]{:S(2)}, u32[]{:S(2)}) collective-permute-start(bf16[16,128,128]{2,1,0:T(8,128)(2,1)S(1)} %get-tuple-element.243), channel_id=1, source_target_pairs={{0,96},{8,104},{16,112},{24,120},{32,64},{40,72},{48,80},{56,88},{... | collective-permute-start | bytes 1572872 | tf_op jit(solution)/shard_map/ppermute | solution.py:339
  98.8 15.7 %collective-permute-start.29 = (bf16[6,128,128]{2,1,0:T(8,128)(2,1)S(1)}, bf16[6,128,128]{2,1,0:T(8,128)(2,1)S(1)}, u32[]{:S(2)}, u32[]{:S(2)}) collective-permute-start(bf16[6,128,128]{2,1,0:T(8,128)(2,1)S(1)} %get-tuple-element.248), channel_id=1, source_target_pairs={{0,32},{8,40},{16,48},{24,56},{32,0},{40,8},{48,16},{56,24},{64,96... | collective-permute-start | bytes 589832 | tf_op jit(solution)/shard_map/ppermute | solution.py:339
  108.7 16.4 %collective-permute-start.30 = (bf16[10,128,128]{2,1,0:T(8,128)(2,1)S(1)}, bf16[10,128,128]{2,1,0:T(8,128)(2,1)S(1)}, u32[]{:S(2)}, u32[]{:S(2)}) collective-permute-start(bf16[10,128,128]{2,1,0:T(8,128)(2,1)S(1)} %get-tuple-element.251), channel_id=1, source_target_pairs={{0,32},{8,40},{16,48},{24,56},{32,0},{40,8},{48,16},{56,24},{64,96... | collective-permute-start | bytes 983048 | tf_op jit(solution)/shard_map/ppermute | solution.py:339
  109.7 16.9 %collective-permute-start.32 = (bf16[10,128,128]{2,1,0:T(8,128)(2,1)S(1)}, bf16[10,128,128]{2,1,0:T(8,128)(2,1)S(1)}, u32[]{:S(2)}, u32[]{:S(2)}) collective-permute-start(bf16[10,128,128]{2,1,0:T(8,128)(2,1)S(1)} %get-tuple-element.255), channel_id=1, source_target_pairs={{0,96},{8,104},{16,112},{24,120},{32,64},{40,72},{48,80},{56,88},{... | collective-permute-start | bytes 983048 | tf_op jit(solution)/shard_map/ppermute | solution.py:339
  112.4 15.1 %collective-permute-start.34 = (bf16[8,128,128]{2,1,0:T(8,128)(2,1)S(1)}, bf16[8,128,128]{2,1,0:T(8,128)(2,1)S(1)}, u32[]{:S(2)}, u32[]{:S(2)}) collective-permute-start(bf16[8,128,128]{2,1,0:T(8,128)(2,1)S(1)} %get-tuple-element.259), channel_id=1, source_target_pairs={{0,16},{8,24},{16,0},{24,8},{32,48},{40,56},{48,32},{56,40},{64,80... | collective-permute-start | bytes 786440 | tf_op jit(solution)/shard_map/ppermute | solution.py:339
  113.6 8.2 %collective-permute-start.28 = (bf16[6,128,128]{2,1,0:T(8,128)(2,1)S(1)}, bf16[6,128,128]{2,1,0:T(8,128)(2,1)S(1)}, u32[]{:S(2)}, u32[]{:S(2)}) collective-permute-start(bf16[6,128,128]{2,1,0:T(8,128)(2,1)S(1)} %get-tuple-element.247), channel_id=1, source_target_pairs={{0,16},{8,24},{16,0},{24,8},{32,48},{40,56},{48,32},{56,40},{64,80... | collective-permute-start | bytes 589832 | tf_op jit(solution)/shard_map/ppermute | solution.py:339
  114.5 8.9 %collective-permute-start.27 = (bf16[6,128,128]{2,1,0:T(8,128)(2,1)S(1)}, bf16[6,128,128]{2,1,0:T(8,128)(2,1)S(1)}, u32[]{:S(2)}, u32[]{:S(2)}) collective-permute-start(bf16[6,128,128]{2,1,0:T(8,128)(2,1)S(1)} %get-tuple-element.246), channel_id=1, source_target_pairs={{0,96},{8,104},{16,112},{24,120},{32,64},{40,72},{48,80},{56,88},{... | collective-permute-start | bytes 589832 | tf_op jit(solution)/shard_map/ppermute | solution.py:339
  125.2 6.6 %collective-permute-start.31 = (bf16[5,128,128]{2,1,0:T(8,128)(2,1)S(1)}, bf16[5,128,128]{2,1,0:T(8,128)(2,1)S(1)}, u32[]{:S(2)}, u32[]{:S(2)}) collective-permute-start(bf16[5,128,128]{2,1,0:T(8,128)(2,1)S(1)} %get-tuple-element.253), channel_id=1, source_target_pairs={{0,96},{8,104},{16,112},{24,120},{32,64},{40,72},{48,80},{56,88},{... | collective-permute-start | bytes 491528 | tf_op jit(solution)/shard_map/ppermute | solution.py:339
  126.7 5.9 %collective-permute-start.33 = (bf16[5,128,128]{2,1,0:T(8,128)(2,1)S(1)}, bf16[5,128,128]{2,1,0:T(8,128)(2,1)S(1)}, u32[]{:S(2)}, u32[]{:S(2)}) collective-permute-start(bf16[5,128,128]{2,1,0:T(8,128)(2,1)S(1)} %get-tuple-element.257), channel_id=1, source_target_pairs={{0,16},{8,24},{16,0},{24,8},{32,48},{40,56},{48,32},{56,40},{64,80... | collective-permute-start | bytes 491528 | tf_op jit(solution)/shard_map/ppermute | solution.py:339
  127.5 5.0 %collective-permute-start.35 = (bf16[4,128,128]{2,1,0:T(8,128)(2,1)S(1)}, bf16[4,128,128]{2,1,0:T(8,128)(2,1)S(1)}, u32[]{:S(2)}, u32[]{:S(2)}) collective-permute-start(bf16[4,128,128]{2,1,0:T(8,128)(2,1)S(1)} %get-tuple-element.261), channel_id=1, source_target_pairs={{0,32},{8,40},{16,48},{24,56},{32,0},{40,8},{48,16},{56,24},{64,96... | collective-permute-start | bytes 393224 | tf_op jit(solution)/shard_map/ppermute | solution.py:339
  (2 other events, 3.7 us)

commit v3 on v2

--- a/solution.py
+++ b/solution.py
@@ -400,12 +400,14 @@
     early = exchange(early, 0)
     wt, e_blocks = prep(after(weights, last), adjoint, emission, far)
     last, cores, late = wt, [], []
+    halved = []
     for i in range(3):
         last = given(1, i, wt, e_blocks, last)
         cores.append(swap(last, CORE))
-        if i == 0:
-            early, last = halve(early, last)
-            early = exchange(early, 1)
+        for j in ((0,), (1, 2), ())[i]:
+            some, last = halve(early[j : j + 1], last)
+            halved += some
+    early = exchange(halved, 1)
     for i in range(3):
         if i == 2:
             early, last = halve(early, last)
@@ -414,9 +416,9 @@
         last = late[i][1]
     late = exchange(late, 0)
     late, last = halve(late, (last, crowded))
+    late, last = halve(exchange(late, 1), last)
+    late = exchange(late, 2)
     out, done = finish(after(me, last), counts, table, early, tuple(offsets[0]))
-    late, last = halve(exchange(late, 1), done)
-    late = exchange(late, 2)
     out, _ = finish(me, counts, table, late, tuple(offsets[1]), (out, done))
 
     def crowded_group(state):

time: 136 us -> 132 us (0.971)
  waiting for transfers between devices: 36.9 us -> 32.6 us
    ppermute x24, waiting for transfers between devices: 26.6 us -> 22.2 us  [swap(): return lax.ppermute(a, 'tm', [(i, i ^ mask) for i in range(n)])]
  transfers between devices with their start and end apart: 26 -> 26, of which waited for: 12 -> 11; matrix products, arithmetic and copies ran while one was open for 1% -> 1% of each run, Pallas kernels for 36% -> 37%
where the time goes in v3:
time: 132 us
  Pallas kernels  57.9 us (44%)
  starting transfers between devices  35.9 us (27%)
  waiting for transfers between devices  32.6 us (25%)
  local copies, waits for them, and re-layouts  2.84 us (2%)
    pallas_call x12, Pallas kernels, tiles(): pl.pallas_call(functools.partial(tiles_kernel, first, per, with_add, roll...  25.5 us
    ppermute x24, starting transfers between devices, swap(): return lax.ppermute(a, 'tm', [(i, i ^ mask) for i in range(n)])  23.6 us
    ppermute x24, waiting for transfers between devices, swap(): return lax.ppermute(a, 'tm', [(i, i ^ mask) for i in range(n)])  22.2 us
    pallas_call x2, Pallas kernels, prep(): pl.pallas_call(functools.partial(prep_kernel, with_far), in_specs=[vmem]...  18.4 us
    all_to_all x1, starting transfers between devices, body(): lax.all_to_all(request, 'tile', split_axis=0, concat_axis=0, tiled=True)  7.86 us
    all_to_all x1, waiting for transfers between devices, body(): lax.all_to_all(request, 'tile', split_axis=0, concat_axis=0, tiled=True)  6.9 us
    all_to_all x1, starting transfers between devices, body(): lax.all_to_all(outgoing, 'tile', split_axis=0, concat_axis=0, tiled=True)  4.41 us
    pallas_call x1, Pallas kernels, pack(): pl.pallas_call(pack_kernel, in_specs=[pl.BlockSpec(memory_space=pltpu.SME...  4.23 us
  transfers between devices with their start and end apart: 26, of which 11 were waited for; matrix products, arithmetic and copies ran while one was open for 1% of the time, Pallas kernels for 37%

profile of v3, /device:TPU:0, one launch (start us, length us, event | category | flops | bytes accessed | tf_op | source)
XLA Modules:
  0.0 131.9 jit_solution(6890512423563884696)
XLA Ops:
  1.5 2.1 %plan.1 = (s32[8,128]{1,0:T(8,128)}, s32[16,128]{1,0:T(8,128)S(1)}) custom-call(s32[1]{0:T(128)} %bitcast.own_ref, s32[1]{0:T(128)S(6)} %copy.45.count_ref, s32[512,2]{1,0:T(8,128)S(1)} %copy.31.tiles_ref), custom_call_target="tpu_custom_call" | custom-call | tf_op jit(solution)/shard_map/plan/pallas_call | solution.py:87
  3.6 7.9 %all-to-all-start = ((s32[8,1,128]{2,1,0:T(1,128)}), s32[8,1,128]{2,1,0:T(1,128)S(1)}, u32[]{:S(2)}, u32[]{:S(2)}) async-start(s32[8,1,128]{2,1,0:T(1,128)} %bitcast.2), calls=%async_computation | async-start | bytes 8192 | tf_op jit(solution)/shard_map/all_to_all | solution.py:359
  12.1 6.9 %all-to-all-done = s32[8,1,128]{2,1,0:T(1,128)S(1)} async-done(((s32[8,1,128]{2,1,0:T(1,128)}), s32[8,1,128]{2,1,0:T(1,128)S(1)}, u32[]{:S(2)}, u32[]{:S(2)}) %all-to-all-start) | async-done | bytes 4128 | tf_op jit(solution)/shard_map/all_to_all | solution.py:359
  19.0 4.2 %pack.1 = bf16[32,320,128]{2,1,0:T(8,128)(2,1)} custom-call(s32[8,128]{1,0:T(8,128)S(1)} %bitcast.9, bf16[320,16384]{1,0:T(8,128)(2,1)} %em_ref.5), custom_call_target="tpu_custom_call" | custom-call | tf_op jit(solution)/shard_map/pack/pallas_call | solution.py:210
  23.2 4.4 %all-to-all-start.1 = ((bf16[32,320,128]{2,1,0:T(8,128)(2,1)}), bf16[32,320,128]{2,1,0:T(8,128)(2,1)}, u32[]{:S(2)}, u32[]{:S(2)}) async-start(bf16[32,320,128]{2,1,0:T(8,128)(2,1)} %pack.1), calls=%async_computation.1 | async-start | bytes 5242880 | tf_op jit(solution)/shard_map/all_to_all | solution.py:361
  27.8 8.9 %prep.3 = (bf16[128,128,384]{2,1,0:T(8,128)(2,1)S(1)}, bf16[128,384,128]{2,1,0:T(8,128)(2,1)S(1)}) custom-call(f32[320,1]{1,0:T(8,128)S(1)} %copy.33.weights_ref, bf16[320,16384]{1,0:T(8,128)(2,1)} %adj_ref.3, bf16[320,16384]{1,0:T(8,128)(2,1)} %em_ref.5), custom_call_target="tpu_custom_call" | custom-call | tf_op jit(solution)/shard_map/prep/pallas_call | solution.py:169
  36.7 2.1 %tiles.18 = bf16[48,128,128]{2,1,0:T(8,128)(2,1)S(1)} custom-call(s32[8]{0:T(128)S(1)} %multiply_xor_fusion.1.refs_0_.refs_1_, s32[8]{0:T(128)S(1)} %multiply_xor_fusion.1.refs_0_.refs_1_, s32[16,128]{1,0:T(8,128)S(1)} %get-tuple-element.487.refs_2_.table_ref, bf16[128,128,384]{2,1,0:T(8,128)(2,1)S(1)} %get-tuple-element.195.refs_3_, ...), custom_call_target="tpu_custom_call" | custom-call | tf_op jit(solution)/shard_map/tiles/pallas_call | solution.py:253
  38.9 2.1 %tiles.19 = bf16[48,128,128]{2,1,0:T(8,128)(2,1)S(1)} custom-call(s32[8]{0:T(128)S(1)} %multiply_xor_fusion.1.refs_0_.refs_1_, s32[8]{0:T(128)S(1)} %multiply_xor_fusion.1.refs_0_.refs_1_, s32[16,128]{1,0:T(8,128)S(1)} %get-tuple-element.487.refs_2_.table_ref, bf16[128,128,384]{2,1,0:T(8,128)(2,1)S(1)} %get-tuple-element.195.refs_3_, ...), custom_call_target="tpu_custom_call" | custom-call | tf_op jit(solution)/shard_map/tiles/pallas_call | solution.py:253
  41.6 2.1 %tiles.20 = bf16[48,128,128]{2,1,0:T(8,128)(2,1)S(1)} custom-call(s32[8]{0:T(128)S(1)} %multiply_xor_fusion.1.refs_0_.refs_1_, s32[8]{0:T(128)S(1)} %multiply_xor_fusion.1.refs_0_.refs_1_, s32[16,128]{1,0:T(8,128)S(1)} %get-tuple-element.487.refs_2_.table_ref, bf16[128,128,384]{2,1,0:T(8,128)(2,1)S(1)} %get-tuple-element.195.refs_3_, ...), custom_call_target="tpu_custom_call" | custom-call | tf_op jit(solution)/shard_map/tiles/pallas_call | solution.py:253
  43.8 2.8 %tiles.21 = (bf16[24,128,128]{2,1,0:T(8,128)(2,1)}, bf16[24,128,128]{2,1,0:T(8,128)(2,1)S(1)}) custom-call(s32[8]{0:T(128)S(1)} %broadcast_xor_fusion.5.refs_0_, s32[8]{0:T(128)S(1)} %copy-done.7, s32[16,128]{1,0:T(8,128)S(1)} %get-tuple-element.487.refs_2_.table_ref, bf16[128,128,384]{2,1,0:T(8,128)(2,1)S(1)} %get-tuple-element.195.refs_3_, ...), custom_call_target="tpu_custom_call" | custom-call | tf_op jit(solution)/shard_map/tiles/pallas_call | solution.py:253
  47.3 2.8 %tiles.22 = (bf16[24,128,128]{2,1,0:T(8,128)(2,1)}, bf16[24,128,128]{2,1,0:T(8,128)(2,1)S(1)}) custom-call(s32[8]{0:T(128)S(1)} %broadcast_xor_fusion.3.refs_0_, s32[8]{0:T(128)S(1)} %copy-done.6, s32[16,128]{1,0:T(8,128)S(1)} %get-tuple-element.487.refs_2_.table_ref, bf16[128,128,384]{2,1,0:T(8,128)(2,1)S(1)} %get-tuple-element.195.refs_3_, ...), custom_call_target="tpu_custom_call" | custom-call | tf_op jit(solution)/shard_map/tiles/pallas_call | solution.py:253
  50.0 1.6 %collective-permute-start.16 = (bf16[24,128,128]{2,1,0:T(8,128)(2,1)}, bf16[24,128,128]{2,1,0:T(8,128)(2,1)}, u32[]{:S(2)}, u32[]{:S(2)}) collective-permute-start(bf16[24,128,128]{2,1,0:T(8,128)(2,1)} %get-tuple-element.215), channel_id=1, source_target_pairs={{0,32},{8,40},{16,48},{24,56},{32,0},{40,8},{48,16},{56,24},{64,96... | collective-permute-start | bytes 2359304 | tf_op jit(solution)/shard_map/ppermute | solution.py:339
  51.6 2.9 %tiles.23 = (bf16[24,128,128]{2,1,0:T(8,128)(2,1)}, bf16[24,128,128]{2,1,0:T(8,128)(2,1)S(1)}) custom-call(s32[8]{0:T(128)S(1)} %broadcast_xor_fusion.4.refs_0_, s32[8]{0:T(128)S(1)} %copy-done.5, s32[16,128]{1,0:T(8,128)S(1)} %get-tuple-element.487.refs_2_.table_ref, bf16[128,128,384]{2,1,0:T(8,128)(2,1)S(1)} %get-tuple-element.195.refs_3_, ...), custom_call_target="tpu_custom_call" | custom-call | tf_op jit(solution)/shard_map/tiles/pallas_call | solution.py:253
  55.4 2.2 %collective-permute-start.17 = (bf16[24,128,128]{2,1,0:T(8,128)(2,1)}, bf16[24,128,128]{2,1,0:T(8,128)(2,1)S(1)}, u32[]{:S(2)}, u32[]{:S(2)}) collective-permute-start(bf16[24,128,128]{2,1,0:T(8,128)(2,1)} %get-tuple-element.218), channel_id=1, source_target_pairs={{0,96},{8,104},{16,112},{24,120},{32,64},{40,72},{48,80},{56,88},{... | collective-permute-start | bytes 2359304 | tf_op jit(solution)/shard_map/ppermute | solution.py:339
  57.7 3.4 %all-to-all-done.1.refs_0_ = bf16[32,320,128]{2,1,0:T(8,128)(2,1)} async-done(((bf16[32,320,128]{2,1,0:T(8,128)(2,1)}), bf16[32,320,128]{2,1,0:T(8,128)(2,1)}, u32[]{:S(2)}, u32[]{:S(2)}) %all-to-all-start.1) | async-done | bytes 2621472 | tf_op jit(solution)/shard_map/all_to_all | solution.py:361
  61.1 9.5 %prep.4 = (bf16[128,128,384]{2,1,0:T(8,128)(2,1)S(1)}, bf16[160,384,128]{2,1,0:T(8,128)(2,1)S(1)}) custom-call(f32[320,1]{1,0:T(8,128)S(1)} %copy.34.weights_ref, bf16[320,16384]{1,0:T(8,128)(2,1)} %adj_ref.3, bf16[320,16384]{1,0:T(8,128)(2,1)} %em_ref.5, bf16[32,320,128]{2,1,0:T(8,128)(2,1)} %all-to-all-done.1.refs_0_), custom_call_target="tpu_custom_call" | custom-call | tf_op jit(solution)/shard_map/prep/pallas_call | solution.py:169
  70.6 1.9 %tiles.24 = bf16[40,128,128]{2,1,0:T(8,128)(2,1)S(1)} custom-call(s32[8]{0:T(128)S(1)} %multiply_xor_fusion.1.refs_0_.refs_1_, s32[8]{0:T(128)S(1)} %multiply_xor_fusion.1.refs_0_.refs_1_, s32[16,128]{1,0:T(8,128)S(1)} %get-tuple-element.487.refs_2_.table_ref, bf16[128,128,384]{2,1,0:T(8,128)(2,1)S(1)} %get-tuple-element.207.refs_3_, ...), custom_call_target="tpu_custom_call" | custom-call | tf_op jit(solution)/shard_map/tiles/pallas_call | solution.py:253
  74.0 1.9 %tiles.25 = bf16[40,128,128]{2,1,0:T(8,128)(2,1)S(1)} custom-call(s32[8]{0:T(128)S(1)} %multiply_xor_fusion.1.refs_0_.refs_1_, s32[8]{0:T(128)S(1)} %multiply_xor_fusion.1.refs_0_.refs_1_, s32[16,128]{1,0:T(8,128)S(1)} %get-tuple-element.487.refs_2_.table_ref, bf16[128,128,384]{2,1,0:T(8,128)(2,1)S(1)} %get-tuple-element.207.refs_3_, ...), custom_call_target="tpu_custom_call" | custom-call | tf_op jit(solution)/shard_map/tiles/pallas_call | solution.py:253
  78.0 1.7 %tiles.26 = bf16[32,128,128]{2,1,0:T(8,128)(2,1)S(1)} custom-call(s32[8]{0:T(128)S(1)} %multiply_xor_fusion.1.refs_0_.refs_1_, s32[8]{0:T(128)S(1)} %multiply_xor_fusion.1.refs_0_.refs_1_, s32[16,128]{1,0:T(8,128)S(1)} %get-tuple-element.487.refs_2_.table_ref, bf16[128,128,384]{2,1,0:T(8,128)(2,1)S(1)} %get-tuple-element.207.refs_3_, ...), custom_call_target="tpu_custom_call" | custom-call | tf_op jit(solution)/shard_map/tiles/pallas_call | solution.py:253
  79.9 1.6 %collective-permute-start.20 = (bf16[12,128,128]{2,1,0:T(8,128)(2,1)S(1)}, bf16[12,128,128]{2,1,0:T(8,128)(2,1)S(1)}, u32[]{:S(2)}, u32[]{:S(2)}) collective-permute-start(bf16[12,128,128]{2,1,0:T(8,128)(2,1)S(1)} %get-tuple-element.226), channel_id=1, source_target_pairs={{0,32},{8,40},{16,48},{24,56},{32,0},{40,8},{48,16},{56,24},{64,96... | collective-permute-start | bytes 1179656 | tf_op jit(solution)/shard_map/ppermute | solution.py:339
  81.5 2.2 %collective-permute-start.21 = (bf16[12,128,128]{2,1,0:T(8,128)(2,1)S(1)}, bf16[12,128,128]{2,1,0:T(8,128)(2,1)S(1)}, u32[]{:S(2)}, u32[]{:S(2)}) collective-permute-start(bf16[12,128,128]{2,1,0:T(8,128)(2,1)S(1)} %get-tuple-element.229), channel_id=1, source_target_pairs={{0,96},{8,104},{16,112},{24,120},{32,64},{40,72},{48,80},{56,88},{... | collective-permute-start | bytes 1179656 | tf_op jit(solution)/shard_map/ppermute | solution.py:339
  85.1 1.9 %tiles.27 = (bf16[20,128,128]{2,1,0:T(8,128)(2,1)S(1)}, bf16[20,128,128]{2,1,0:T(8,128)(2,1)S(1)}) custom-call(s32[8]{0:T(128)S(1)} %broadcast_xor_fusion.5.refs_0_, s32[8]{0:T(128)S(1)} %copy-done.7, s32[16,128]{1,0:T(8,128)S(1)} %get-tuple-element.487.refs_2_.table_ref, bf16[128,128,384]{2,1,0:T(8,128)(2,1)S(1)} %get-tuple-element.207.refs_3_, ...), custom_call_target="tpu_custom_call" | custom-call | tf_op jit(solution)/shard_map/tiles/pallas_call | solution.py:253
  87.7 1.9 %tiles.28 = (bf16[20,128,128]{2,1,0:T(8,128)(2,1)S(1)}, bf16[20,128,128]{2,1,0:T(8,128)(2,1)S(1)}) custom-call(s32[8]{0:T(128)S(1)} %broadcast_xor_fusion.3.refs_0_, s32[8]{0:T(128)S(1)} %copy-done.6, s32[16,128]{1,0:T(8,128)S(1)} %get-tuple-element.487.refs_2_.table_ref, bf16[128,128,384]{2,1,0:T(8,128)(2,1)S(1)} %get-tuple-element.207.refs_3_, ...), custom_call_target="tpu_custom_call" | custom-call | tf_op jit(solution)/shard_map/tiles/pallas_call | solution.py:253
  89.6 1.7 %collective-permute-done.20.refs_1_ = bf16[12,128,128]{2,1,0:T(8,128)(2,1)S(1)} collective-permute-done((bf16[12,128,128]{2,1,0:T(8,128)(2,1)S(1)}, bf16[12,128,128]{2,1,0:T(8,128)(2,1)S(1)}, u32[]{:S(2)}, u32[]{:S(2)}) %collective-permute-start.20) | collective-permute-done | bytes 393248 | tf_op jit(solution)/shard_map/ppermute | solution.py:339
  93.9 1.8 %collective-permute-done.22.refs_1_ = bf16[12,128,128]{2,1,0:T(8,128)(2,1)S(1)} collective-permute-done((bf16[12,128,128]{2,1,0:T(8,128)(2,1)S(1)}, bf16[12,128,128]{2,1,0:T(8,128)(2,1)S(1)}, u32[]{:S(2)}, u32[]{:S(2)}) %collective-permute-start.22) | collective-permute-done | bytes 393248 | tf_op jit(solution)/shard_map/ppermute | solution.py:339
  95.8 1.7 %tiles.29 = (bf16[16,128,128]{2,1,0:T(8,128)(2,1)S(1)}, bf16[16,128,128]{2,1,0:T(8,128)(2,1)S(1)}) custom-call(s32[8]{0:T(128)S(1)} %broadcast_xor_fusion.4.refs_0_, s32[8]{0:T(128)S(1)} %copy-done.5, s32[16,128]{1,0:T(8,128)S(1)} %get-tuple-element.487.refs_2_.table_ref, bf16[128,128,384]{2,1,0:T(8,128)(2,1)S(1)} %get-tuple-element.207.refs_3_, ...), custom_call_target="tpu_custom_call" | custom-call | tf_op jit(solution)/shard_map/tiles/pallas_call | solution.py:253
  99.6 9.0 %collective-permute-done.24.refs_1_ = bf16[20,128,128]{2,1,0:T(8,128)(2,1)S(1)} collective-permute-done((bf16[20,128,128]{2,1,0:T(8,128)(2,1)S(1)}, bf16[20,128,128]{2,1,0:T(8,128)(2,1)S(1)}, u32[]{:S(2)}, u32[]{:S(2)}) %collective-permute-start.24) | collective-permute-done | bytes 655392 | tf_op jit(solution)/shard_map/ppermute | solution.py:339
  113.7 5.7 %collective-permute-done.27.refs_1_ = bf16[10,128,128]{2,1,0:T(8,128)(2,1)S(1)} collective-permute-done((bf16[10,128,128]{2,1,0:T(8,128)(2,1)S(1)}, bf16[10,128,128]{2,1,0:T(8,128)(2,1)S(1)}, u32[]{:S(2)}, u32[]{:S(2)}) %collective-permute-start.27) | collective-permute-done | bytes 327712 | tf_op jit(solution)/shard_map/ppermute | solution.py:339
  120.6 2.3 %collective-permute-start.28 = (bf16[5,128,128]{2,1,0:T(8,128)(2,1)S(1)}, bf16[5,128,128]{2,1,0:T(8,128)(2,1)S(1)}, u32[]{:S(2)}, u32[]{:S(2)}) collective-permute-start(bf16[5,128,128]{2,1,0:T(8,128)(2,1)S(1)} %get-tuple-element.248), channel_id=1, source_target_pairs={{0,96},{8,104},{16,112},{24,120},{32,64},{40,72},{48,80},{56,88},{... | collective-permute-start | bytes 491528 | tf_op jit(solution)/shard_map/ppermute | solution.py:339
  124.1 2.2 %collective-permute-done.33.refs_1_ = bf16[6,128,128]{2,1,0:T(8,128)(2,1)S(1)} collective-permute-done((bf16[6,128,128]{2,1,0:T(8,128)(2,1)S(1)}, bf16[6,128,128]{2,1,0:T(8,128)(2,1)S(1)}, u32[]{:S(2)}, u32[]{:S(2)}) %collective-permute-start.33) | collective-permute-done | bytes 196640 | tf_op jit(solution)/shard_map/ppermute | solution.py:339
  126.3 1.7 %finish.3 = (f32[32,128,128]{2,1,0:T(8,128)}, f32[8,128]{1,0:T(8,128)S(1)}) custom-call(s32[1]{0:T(128)} %bitcast.4.me_ref, s32[1]{0:T(128)S(6)} %copy.45.count_ref, s32[16,128]{1,0:T(8,128)S(1)} %get-tuple-element.487.refs_2_.table_ref, bf16[6,128,128]{2,1,0:T(8,128)(2,1)S(1)} %get-tuple-element.227.refs_0_, ...), custom_call_target="tpu_custom_call" | custom-call | tf_op jit(solution)/shard_map/finish/pallas_call | solution.py:316
  128.9 2.2 %finish.4 = (f32[32,128,128]{2,1,0:T(8,128)}, f32[8,128]{1,0:T(8,128)}) custom-call(s32[1]{0:T(128)} %bitcast.4.me_ref, s32[1]{0:T(128)S(6)} %copy.45.count_ref, s32[16,128]{1,0:T(8,128)S(1)} %get-tuple-element.487.refs_2_.table_ref, bf16[5,128,128]{2,1,0:T(8,128)(2,1)S(1)} %get-tuple-element.247.refs_0_, ...), custom_call_target="tpu_custom_call", output_to_operand_aliasing={{0}: (9, {})} | custom-call | tf_op jit(solution)/shard_map/finish/pallas_call | solution.py:316
  (77 shorter events, 23.7 us)
Async XLA Ops:
  3.6 15.4 %all-to-all-start = ((s32[8,1,128]{2,1,0:T(1,128)}), s32[8,1,128]{2,1,0:T(1,128)S(1)}, u32[]{:S(2)}, u32[]{:S(2)}) async-start(s32[8,1,128]{2,1,0:T(1,128)} %bitcast.2), calls=%async_computation | async-start | bytes 8192 | tf_op jit(solution)/shard_map/all_to_all | solution.py:359
  23.2 37.9 %all-to-all-start.1 = ((bf16[32,320,128]{2,1,0:T(8,128)(2,1)}), bf16[32,320,128]{2,1,0:T(8,128)(2,1)}, u32[]{:S(2)}, u32[]{:S(2)}) async-start(bf16[32,320,128]{2,1,0:T(8,128)(2,1)} %pack.1), calls=%async_computation.1 | async-start | bytes 5242880 | tf_op jit(solution)/shard_map/all_to_all | solution.py:361
  38.8 5.0 %collective-permute-start.12 = (bf16[48,128,128]{2,1,0:T(8,128)(2,1)S(1)}, bf16[48,128,128]{2,1,0:T(8,128)(2,1)S(1)}, u32[]{:S(2)}, u32[]{:S(2)}) collective-permute-start(bf16[48,128,128]{2,1,0:T(8,128)(2,1)S(1)} %tiles.18), channel_id=1, source_target_pairs={{0,8},{8,0},{16,24},{24,16},{32,40},{40,32},{48,56},{56,48},{64,72... | collective-permute-start | bytes 4718600 | tf_op jit(solution)/shard_map/ppermute | solution.py:339
  41.0 2.8 %copy-start.10 = (s32[8]{0:T(128)S(1)}, s32[8]{0:T(128)}, u32[]{:S(2)}) copy-start(s32[8]{0:T(128)} %constant.31.clone) | copy-start | bytes 100
  41.0 2.8 %copy-start.7 = (s32[8]{0:T(128)S(1)}, s32[8]{0:T(128)}, u32[]{:S(2)}) copy-start(s32[8]{0:T(128)} %constant.32.clone.refs_1_) | copy-start | bytes 100
  41.0 6.2 %collective-permute-start.13 = (bf16[48,128,128]{2,1,0:T(8,128)(2,1)S(1)}, bf16[48,128,128]{2,1,0:T(8,128)(2,1)S(1)}, u32[]{:S(2)}, u32[]{:S(2)}) collective-permute-start(bf16[48,128,128]{2,1,0:T(8,128)(2,1)S(1)} %tiles.19), channel_id=1, source_target_pairs={{0,8},{8,0},{16,24},{24,16},{32,40},{40,32},{48,56},{56,48},{64,72... | collective-permute-start | bytes 4718600 | tf_op jit(solution)/shard_map/ppermute | solution.py:339
  43.7 8.0 %collective-permute-start.14 = (bf16[48,128,128]{2,1,0:T(8,128)(2,1)S(1)}, bf16[48,128,128]{2,1,0:T(8,128)(2,1)S(1)}, u32[]{:S(2)}, u32[]{:S(2)}) collective-permute-start(bf16[48,128,128]{2,1,0:T(8,128)(2,1)S(1)} %tiles.20), channel_id=1, source_target_pairs={{0,8},{8,0},{16,24},{24,16},{32,40},{40,32},{48,56},{56,48},{64,72... | collective-permute-start | bytes 4718600 | tf_op jit(solution)/shard_map/ppermute | solution.py:339
  43.8 3.4 %copy-start.9 = (s32[8]{0:T(128)S(1)}, s32[8]{0:T(128)}, u32[]{:S(2)}) copy-start(s32[8]{0:T(128)} %constant.33.clone) | copy-start | bytes 100
  43.8 3.4 %copy-start.8 = (s32[8]{0:T(128)S(1)}, s32[8]{0:T(128)}, u32[]{:S(2)}) copy-start(s32[8]{0:T(128)} %constant.35.clone) | copy-start | bytes 100
  43.8 3.4 %copy-start.6 = (s32[8]{0:T(128)S(1)}, s32[8]{0:T(128)}, u32[]{:S(2)}) copy-start(s32[8]{0:T(128)} %constant.34.clone.refs_1_) | copy-start | bytes 100
  46.6 26.1 %collective-permute-start.15 = (bf16[24,128,128]{2,1,0:T(8,128)(2,1)}, bf16[24,128,128]{2,1,0:T(8,128)(2,1)}, u32[]{:S(2)}, u32[]{:S(2)}) collective-permute-start(bf16[24,128,128]{2,1,0:T(8,128)(2,1)} %get-tuple-element.211), channel_id=1, source_target_pairs={{0,16},{8,24},{16,0},{24,8},{32,48},{40,56},{48,32},{56,40},{64,80... | collective-permute-start | bytes 2359304 | tf_op jit(solution)/shard_map/ppermute | solution.py:339
  47.2 4.4 %copy-start.5 = (s32[8]{0:T(128)S(1)}, s32[8]{0:T(128)}, u32[]{:S(2)}) copy-start(s32[8]{0:T(128)} %constant.36.clone.refs_1_) | copy-start | bytes 100
  50.0 26.4 %collective-permute-start.16 = (bf16[24,128,128]{2,1,0:T(8,128)(2,1)}, bf16[24,128,128]{2,1,0:T(8,128)(2,1)}, u32[]{:S(2)}, u32[]{:S(2)}) collective-permute-start(bf16[24,128,128]{2,1,0:T(8,128)(2,1)} %get-tuple-element.215), channel_id=1, source_target_pairs={{0,32},{8,40},{16,48},{24,56},{32,0},{40,8},{48,16},{56,24},{64,96... | collective-permute-start | bytes 2359304 | tf_op jit(solution)/shard_map/ppermute | solution.py:339
  55.4 22.4 %collective-permute-start.17 = (bf16[24,128,128]{2,1,0:T(8,128)(2,1)}, bf16[24,128,128]{2,1,0:T(8,128)(2,1)S(1)}, u32[]{:S(2)}, u32[]{:S(2)}) collective-permute-start(bf16[24,128,128]{2,1,0:T(8,128)(2,1)} %get-tuple-element.218), channel_id=1, source_target_pairs={{0,96},{8,104},{16,112},{24,120},{32,64},{40,72},{48,80},{56,88},{... | collective-permute-start | bytes 2359304 | tf_op jit(solution)/shard_map/ppermute | solution.py:339
  72.5 11.2 %collective-permute-start.18 = (bf16[40,128,128]{2,1,0:T(8,128)(2,1)S(1)}, bf16[40,128,128]{2,1,0:T(8,128)(2,1)S(1)}, u32[]{:S(2)}, u32[]{:S(2)}) collective-permute-start(bf16[40,128,128]{2,1,0:T(8,128)(2,1)S(1)} %tiles.24), channel_id=1, source_target_pairs={{0,8},{8,0},{16,24},{24,16},{32,40},{40,32},{48,56},{56,48},{64,72... | collective-permute-start | bytes 3932168 | tf_op jit(solution)/shard_map/ppermute | solution.py:339
  75.9 11.0 %collective-permute-start.19 = (bf16[40,128,128]{2,1,0:T(8,128)(2,1)S(1)}, bf16[40,128,128]{2,1,0:T(8,128)(2,1)S(1)}, u32[]{:S(2)}, u32[]{:S(2)}) collective-permute-start(bf16[40,128,128]{2,1,0:T(8,128)(2,1)S(1)} %tiles.25), channel_id=1, source_target_pairs={{0,8},{8,0},{16,24},{24,16},{32,40},{40,32},{48,56},{56,48},{64,72... | collective-permute-start | bytes 3932168 | tf_op jit(solution)/shard_map/ppermute | solution.py:339
  79.7 16.1 %collective-permute-start.23 = (bf16[32,128,128]{2,1,0:T(8,128)(2,1)S(1)}, bf16[32,128,128]{2,1,0:T(8,128)(2,1)S(1)}, u32[]{:S(2)}, u32[]{:S(2)}) collective-permute-start(bf16[32,128,128]{2,1,0:T(8,128)(2,1)S(1)} %tiles.26), channel_id=1, source_target_pairs={{0,8},{8,0},{16,24},{24,16},{32,40},{40,32},{48,56},{56,48},{64,72... | collective-permute-start | bytes 3145736 | tf_op jit(solution)/shard_map/ppermute | solution.py:339
  79.9 11.4 %collective-permute-start.20 = (bf16[12,128,128]{2,1,0:T(8,128)(2,1)S(1)}, bf16[12,128,128]{2,1,0:T(8,128)(2,1)S(1)}, u32[]{:S(2)}, u32[]{:S(2)}) collective-permute-start(bf16[12,128,128]{2,1,0:T(8,128)(2,1)S(1)} %get-tuple-element.226), channel_id=1, source_target_pairs={{0,32},{8,40},{16,48},{24,56},{32,0},{40,8},{48,16},{56,24},{64,96... | collective-permute-start | bytes 1179656 | tf_op jit(solution)/shard_map/ppermute | solution.py:339
  81.5 12.3 %collective-permute-start.21 = (bf16[12,128,128]{2,1,0:T(8,128)(2,1)S(1)}, bf16[12,128,128]{2,1,0:T(8,128)(2,1)S(1)}, u32[]{:S(2)}, u32[]{:S(2)}) collective-permute-start(bf16[12,128,128]{2,1,0:T(8,128)(2,1)S(1)} %get-tuple-element.229), channel_id=1, source_target_pairs={{0,96},{8,104},{16,112},{24,120},{32,64},{40,72},{48,80},{56,88},{... | collective-permute-start | bytes 1179656 | tf_op jit(solution)/shard_map/ppermute | solution.py:339
  83.7 12.0 %collective-permute-start.22 = (bf16[12,128,128]{2,1,0:T(8,128)(2,1)S(1)}, bf16[12,128,128]{2,1,0:T(8,128)(2,1)S(1)}, u32[]{:S(2)}, u32[]{:S(2)}) collective-permute-start(bf16[12,128,128]{2,1,0:T(8,128)(2,1)S(1)} %get-tuple-element.232), channel_id=1, source_target_pairs={{0,16},{8,24},{16,0},{24,8},{32,48},{40,56},{48,32},{56,40},{64,80... | collective-permute-start | bytes 1179656 | tf_op jit(solution)/shard_map/ppermute | solution.py:339
  87.0 21.6 %collective-permute-start.24 = (bf16[20,128,128]{2,1,0:T(8,128)(2,1)S(1)}, bf16[20,128,128]{2,1,0:T(8,128)(2,1)S(1)}, u32[]{:S(2)}, u32[]{:S(2)}) collective-permute-start(bf16[20,128,128]{2,1,0:T(8,128)(2,1)S(1)} %get-tuple-element.237), channel_id=1, source_target_pairs={{0,16},{8,24},{16,0},{24,8},{32,48},{40,56},{48,32},{56,40},{64,80... | collective-permute-start | bytes 1966088 | tf_op jit(solution)/shard_map/ppermute | solution.py:339
  91.3 18.2 %collective-permute-start.25 = (bf16[20,128,128]{2,1,0:T(8,128)(2,1)S(1)}, bf16[20,128,128]{2,1,0:T(8,128)(2,1)S(1)}, u32[]{:S(2)}, u32[]{:S(2)}) collective-permute-start(bf16[20,128,128]{2,1,0:T(8,128)(2,1)S(1)} %get-tuple-element.240), channel_id=1, source_target_pairs={{0,32},{8,40},{16,48},{24,56},{32,0},{40,8},{48,16},{56,24},{64,96... | collective-permute-start | bytes 1966088 | tf_op jit(solution)/shard_map/ppermute | solution.py:339
  97.5 13.3 %collective-permute-start.26 = (bf16[16,128,128]{2,1,0:T(8,128)(2,1)S(1)}, bf16[16,128,128]{2,1,0:T(8,128)(2,1)S(1)}, u32[]{:S(2)}, u32[]{:S(2)}) collective-permute-start(bf16[16,128,128]{2,1,0:T(8,128)(2,1)S(1)} %get-tuple-element.243), channel_id=1, source_target_pairs={{0,96},{8,104},{16,112},{24,120},{32,64},{40,72},{48,80},{56,88},{... | collective-permute-start | bytes 1572872 | tf_op jit(solution)/shard_map/ppermute | solution.py:339
  108.7 10.7 %collective-permute-start.27 = (bf16[10,128,128]{2,1,0:T(8,128)(2,1)S(1)}, bf16[10,128,128]{2,1,0:T(8,128)(2,1)S(1)}, u32[]{:S(2)}, u32[]{:S(2)}) collective-permute-start(bf16[10,128,128]{2,1,0:T(8,128)(2,1)S(1)} %get-tuple-element.246), channel_id=1, source_target_pairs={{0,32},{8,40},{16,48},{24,56},{32,0},{40,8},{48,16},{56,24},{64,96... | collective-permute-start | bytes 983048 | tf_op jit(solution)/shard_map/ppermute | solution.py:339
  109.6 10.9 %collective-permute-start.29 = (bf16[10,128,128]{2,1,0:T(8,128)(2,1)S(1)}, bf16[10,128,128]{2,1,0:T(8,128)(2,1)S(1)}, u32[]{:S(2)}, u32[]{:S(2)}) collective-permute-start(bf16[10,128,128]{2,1,0:T(8,128)(2,1)S(1)} %get-tuple-element.250), channel_id=1, source_target_pairs={{0,96},{8,104},{16,112},{24,120},{32,64},{40,72},{48,80},{56,88},{... | collective-permute-start | bytes 983048 | tf_op jit(solution)/shard_map/ppermute | solution.py:339
  110.9 12.0 %collective-permute-start.31 = (bf16[8,128,128]{2,1,0:T(8,128)(2,1)S(1)}, bf16[8,128,128]{2,1,0:T(8,128)(2,1)S(1)}, u32[]{:S(2)}, u32[]{:S(2)}) collective-permute-start(bf16[8,128,128]{2,1,0:T(8,128)(2,1)S(1)} %get-tuple-element.254), channel_id=1, source_target_pairs={{0,16},{8,24},{16,0},{24,8},{32,48},{40,56},{48,32},{56,40},{64,80... | collective-permute-start | bytes 786440 | tf_op jit(solution)/shard_map/ppermute | solution.py:339
  112.0 11.9 %collective-permute-start.35 = (bf16[6,128,128]{2,1,0:T(8,128)(2,1)S(1)}, bf16[6,128,128]{2,1,0:T(8,128)(2,1)S(1)}, u32[]{:S(2)}, u32[]{:S(2)}) collective-permute-start(bf16[6,128,128]{2,1,0:T(8,128)(2,1)S(1)} %get-tuple-element.260), channel_id=1, source_target_pairs={{0,32},{8,40},{16,48},{24,56},{32,0},{40,8},{48,16},{56,24},{64,96... | collective-permute-start | bytes 589832 | tf_op jit(solution)/shard_map/ppermute | solution.py:339
  112.9 11.2 %collective-permute-start.34 = (bf16[6,128,128]{2,1,0:T(8,128)(2,1)S(1)}, bf16[6,128,128]{2,1,0:T(8,128)(2,1)S(1)}, u32[]{:S(2)}, u32[]{:S(2)}) collective-permute-start(bf16[6,128,128]{2,1,0:T(8,128)(2,1)S(1)} %get-tuple-element.259), channel_id=1, source_target_pairs={{0,16},{8,24},{16,0},{24,8},{32,48},{40,56},{48,32},{56,40},{64,80... | collective-permute-start | bytes 589832 | tf_op jit(solution)/shard_map/ppermute | solution.py:339
  119.4 6.9 %collective-permute-start.33 = (bf16[6,128,128]{2,1,0:T(8,128)(2,1)S(1)}, bf16[6,128,128]{2,1,0:T(8,128)(2,1)S(1)}, u32[]{:S(2)}, u32[]{:S(2)}) collective-permute-start(bf16[6,128,128]{2,1,0:T(8,128)(2,1)S(1)} %get-tuple-element.258), channel_id=1, source_target_pairs={{0,96},{8,104},{16,112},{24,120},{32,64},{40,72},{48,80},{56,88},{... | collective-permute-start | bytes 589832 | tf_op jit(solution)/shard_map/ppermute | solution.py:339
  120.6 7.4 %collective-permute-start.28 = (bf16[5,128,128]{2,1,0:T(8,128)(2,1)S(1)}, bf16[5,128,128]{2,1,0:T(8,128)(2,1)S(1)}, u32[]{:S(2)}, u32[]{:S(2)}) collective-permute-start(bf16[5,128,128]{2,1,0:T(8,128)(2,1)S(1)} %get-tuple-element.248), channel_id=1, source_target_pairs={{0,96},{8,104},{16,112},{24,120},{32,64},{40,72},{48,80},{56,88},{... | collective-permute-start | bytes 491528 | tf_op jit(solution)/shard_map/ppermute | solution.py:339
  122.9 5.9 %collective-permute-start.30 = (bf16[5,128,128]{2,1,0:T(8,128)(2,1)S(1)}, bf16[5,128,128]{2,1,0:T(8,128)(2,1)S(1)}, u32[]{:S(2)}, u32[]{:S(2)}) collective-permute-start(bf16[5,128,128]{2,1,0:T(8,128)(2,1)S(1)} %get-tuple-element.252), channel_id=1, source_target_pairs={{0,16},{8,24},{16,0},{24,8},{32,48},{40,56},{48,32},{56,40},{64,80... | collective-permute-start | bytes 491528 | tf_op jit(solution)/shard_map/ppermute | solution.py:339
  123.8 5.0 %collective-permute-start.32 = (bf16[4,128,128]{2,1,0:T(8,128)(2,1)S(1)}, bf16[4,128,128]{2,1,0:T(8,128)(2,1)S(1)}, u32[]{:S(2)}, u32[]{:S(2)}) collective-permute-start(bf16[4,128,128]{2,1,0:T(8,128)(2,1)S(1)} %get-tuple-element.256), channel_id=1, source_target_pairs={{0,32},{8,40},{16,48},{24,56},{32,0},{40,8},{48,16},{56,24},{64,96... | collective-permute-start | bytes 393224 | tf_op jit(solution)/shard_map/ppermute | solution.py:339
  (2 other events, 2.7 us)

commit v4 on v3

--- a/solution.py
+++ b/solution.py
@@ -25,10 +25,12 @@
 
 
 def plan_kernel(early, own_ref, count_ref, tiles_ref, request_ref, table_ref):
-    slots = tiles_ref.shape[0]
+    slots = tiles_ref.shape[1]
     own = own_ref[0]
-    r = tiles_ref[:, 0:1]
-    c = tiles_ref[:, 1:2]
+    both = jnp.concatenate([tiles_ref[...].astype(F32), jnp.zeros((6, slots), F32)], axis=0)
+    both = both.T.astype(I32)
+    r = both[:, 0:1]
+    c = both[:, 1:2]
     k = iota((slots, 1), 0)
     src = c >> 7
     within = c & (BLK - 1)
@@ -94,7 +96,7 @@
         ],
         compiler_params=pltpu.CompilerParams(vmem_limit_bytes=16 * 2**20),
         name="plan",
-    )(own, counts, tile_list)
+    )(own, counts, tile_list.T)
 
 
 STEP = 16
@@ -191,7 +193,7 @@
     )
 
 
-def pack_kernel(asked_ref, em_ref, out_ref, sems):
+def pack_kernel(own_ref, asked_ref, em_ref, out_ref, sems):
     count = out_ref.shape[0]
 
     def copy(i):
@@ -200,22 +202,30 @@
         return pltpu.make_async_copy(em_ref.at[:, cols], out_ref.at[i], sems.at[i])
 
     for i in range(count):
-        copy(i).start()
+
+        @pl.when(i // CAP != own_ref[0])
+        def _():
+            copy(i).start()
+
     for i in range(count):
-        copy(i).wait()
-
-
-def pack(asked, emission):
+
+        @pl.when(i // CAP != own_ref[0])
+        def _():
+            copy(i).wait()
+
+
+def pack(own, asked, emission):
     owners = asked.shape[0]
     return pl.pallas_call(
         pack_kernel,
-        in_specs=[pl.BlockSpec(memory_space=pltpu.SMEM), pl.BlockSpec(memory_space=pl.ANY)],
+        in_specs=[pl.BlockSpec(memory_space=pltpu.SMEM)] * 2
+        + [pl.BlockSpec(memory_space=pl.ANY)],
         out_specs=pl.BlockSpec(memory_space=pltpu.VMEM),
         out_shape=jax.ShapeDtypeStruct((owners * CAP, emission.shape[0], BLK), BF16),
         scratch_shapes=[pltpu.SemaphoreType.DMA((owners * CAP,))],
         compiler_params=pltpu.CompilerParams(vmem_limit_bytes=8 * 2**20),
         name="pack",
-    )(asked, in_hbm(emission))
+    )(own, asked, in_hbm(emission))
 
 
 def tiles_kernel(first, per, with_add, rolled, *refs):
@@ -357,7 +367,7 @@
     split = sum(cuts[0])
     request, table = plan(own, counts, tile_list, owners, split)
     asked = lax.all_to_all(request, "tile", split_axis=0, concat_axis=0, tiled=True)
-    outgoing = pack(asked, emission)
+    outgoing = pack(own, asked, emission)
     far = lax.all_to_all(outgoing, "tile", split_axis=0, concat_axis=0, tiled=True)
     crowded = jnp.any(asked[:, CAP] > 0)
     weights = step_weights[:, None]

time: 132 us -> 132 us (level)
  transfers between devices with their start and end apart: 26 -> 26, of which waited for: 11 -> 11; matrix products, arithmetic and copies ran while one was open for 1% -> 1% of each run, Pallas kernels for 37% -> 38%
where the time goes in v4:
time: 132 us
  Pallas kernels  57.9 us (44%)
  starting transfers between devices  35.8 us (27%)
  waiting for transfers between devices  32.7 us (25%)
  local copies, waits for them, and re-layouts  2.69 us (2%)
    pallas_call x12, Pallas kernels, tiles(): pl.pallas_call(functools.partial(tiles_kernel, first, per, with_add, roll...  25.5 us
    ppermute x24, starting transfers between devices, swap(): return lax.ppermute(a, 'tm', [(i, i ^ mask) for i in range(n)])  23.6 us
    ppermute x24, waiting for transfers between devices, swap(): return lax.ppermute(a, 'tm', [(i, i ^ mask) for i in range(n)])  22.3 us
    pallas_call x2, Pallas kernels, prep(): pl.pallas_call(functools.partial(prep_kernel, with_far), in_specs=[vmem]...  18.4 us
    all_to_all x1, starting transfers between devices, body(): lax.all_to_all(request, 'tile', split_axis=0, concat_axis=0, tiled=True)  7.86 us
    all_to_all x1, waiting for transfers between devices, body(): lax.all_to_all(request, 'tile', split_axis=0, concat_axis=0, tiled=True)  6.9 us
    all_to_all x1, starting transfers between devices, body(): lax.all_to_all(outgoing, 'tile', split_axis=0, concat_axis=0, tiled=True)  4.41 us
    pallas_call x1, Pallas kernels, pack(): pl.pallas_call(pack_kernel, in_specs=[pl.BlockSpec(memory_space=pltpu.SME...  4.13 us
  transfers between devices with their start and end apart: 26, of which 11 were waited for; matrix products, arithmetic and copies ran while one was open for 1% of the time, Pallas kernels for 38%

profile of v4, /device:TPU:0, one launch (start us, length us, event | category | flops | bytes accessed | tf_op | source)
XLA Modules:
  0.0 131.8 jit_solution(8102766539474287028)
XLA Ops:
  1.3 2.2 %plan.1 = (s32[8,128]{1,0:T(8,128)}, s32[16,128]{1,0:T(8,128)S(1)}) custom-call(s32[1]{0:T(128)} %bitcast.own_ref, s32[1]{0:T(128)S(6)} %copy.42.count_ref, s32[2,512]{1,0:T(2,128)S(1)} %bitcast.12), custom_call_target="tpu_custom_call" | custom-call | tf_op jit(solution)/shard_map/plan/pallas_call | solution.py:89
  3.5 7.9 %all-to-all-start = ((s32[8,1,128]{2,1,0:T(1,128)}), s32[8,1,128]{2,1,0:T(1,128)S(1)}, u32[]{:S(2)}, u32[]{:S(2)}) async-start(s32[8,1,128]{2,1,0:T(1,128)} %bitcast.3), calls=%async_computation | async-start | bytes 8192 | tf_op jit(solution)/shard_map/all_to_all | solution.py:369
  12.1 6.9 %all-to-all-done = s32[8,1,128]{2,1,0:T(1,128)S(1)} async-done(((s32[8,1,128]{2,1,0:T(1,128)}), s32[8,1,128]{2,1,0:T(1,128)S(1)}, u32[]{:S(2)}, u32[]{:S(2)}) %all-to-all-start) | async-done | bytes 4128 | tf_op jit(solution)/shard_map/all_to_all | solution.py:369
  19.0 4.1 %pack.1 = bf16[32,320,128]{2,1,0:T(8,128)(2,1)} custom-call(s32[1]{0:T(128)} %bitcast.own_ref, s32[8,128]{1,0:T(8,128)S(1)} %bitcast.10, bf16[320,16384]{1,0:T(8,128)(2,1)} %em_ref.5), custom_call_target="tpu_custom_call" | custom-call | tf_op jit(solution)/shard_map/pack/pallas_call | solution.py:219
  23.1 4.4 %all-to-all-start.1 = ((bf16[32,320,128]{2,1,0:T(8,128)(2,1)}), bf16[32,320,128]{2,1,0:T(8,128)(2,1)}, u32[]{:S(2)}, u32[]{:S(2)}) async-start(bf16[32,320,128]{2,1,0:T(8,128)(2,1)} %pack.1), calls=%async_computation.1 | async-start | bytes 5242880 | tf_op jit(solution)/shard_map/all_to_all | solution.py:371
  27.7 8.9 %prep.3 = (bf16[128,128,384]{2,1,0:T(8,128)(2,1)S(1)}, bf16[128,384,128]{2,1,0:T(8,128)(2,1)S(1)}) custom-call(f32[320,1]{1,0:T(8,128)S(1)} %copy.30.weights_ref, bf16[320,16384]{1,0:T(8,128)(2,1)} %adj_ref.3, bf16[320,16384]{1,0:T(8,128)(2,1)} %em_ref.5), custom_call_target="tpu_custom_call" | custom-call | tf_op jit(solution)/shard_map/prep/pallas_call | solution.py:171
  36.6 2.1 %tiles.18 = bf16[48,128,128]{2,1,0:T(8,128)(2,1)S(1)} custom-call(s32[8]{0:T(128)S(1)} %multiply_xor_fusion.1.refs_0_.refs_1_, s32[8]{0:T(128)S(1)} %multiply_xor_fusion.1.refs_0_.refs_1_, s32[16,128]{1,0:T(8,128)S(1)} %get-tuple-element.487.refs_2_.table_ref, bf16[128,128,384]{2,1,0:T(8,128)(2,1)S(1)} %get-tuple-element.195.refs_3_, ...), custom_call_target="tpu_custom_call" | custom-call | tf_op jit(solution)/shard_map/tiles/pallas_call | solution.py:263
  38.8 2.1 %tiles.19 = bf16[48,128,128]{2,1,0:T(8,128)(2,1)S(1)} custom-call(s32[8]{0:T(128)S(1)} %multiply_xor_fusion.1.refs_0_.refs_1_, s32[8]{0:T(128)S(1)} %multiply_xor_fusion.1.refs_0_.refs_1_, s32[16,128]{1,0:T(8,128)S(1)} %get-tuple-element.487.refs_2_.table_ref, bf16[128,128,384]{2,1,0:T(8,128)(2,1)S(1)} %get-tuple-element.195.refs_3_, ...), custom_call_target="tpu_custom_call" | custom-call | tf_op jit(solution)/shard_map/tiles/pallas_call | solution.py:263
  41.5 2.1 %tiles.20 = bf16[48,128,128]{2,1,0:T(8,128)(2,1)S(1)} custom-call(s32[8]{0:T(128)S(1)} %multiply_xor_fusion.1.refs_0_.refs_1_, s32[8]{0:T(128)S(1)} %multiply_xor_fusion.1.refs_0_.refs_1_, s32[16,128]{1,0:T(8,128)S(1)} %get-tuple-element.487.refs_2_.table_ref, bf16[128,128,384]{2,1,0:T(8,128)(2,1)S(1)} %get-tuple-element.195.refs_3_, ...), custom_call_target="tpu_custom_call" | custom-call | tf_op jit(solution)/shard_map/tiles/pallas_call | solution.py:263
  43.7 2.8 %tiles.21 = (bf16[24,128,128]{2,1,0:T(8,128)(2,1)}, bf16[24,128,128]{2,1,0:T(8,128)(2,1)S(1)}) custom-call(s32[8]{0:T(128)S(1)} %broadcast_xor_fusion.5.refs_0_, s32[8]{0:T(128)S(1)} %copy-done.8, s32[16,128]{1,0:T(8,128)S(1)} %get-tuple-element.487.refs_2_.table_ref, bf16[128,128,384]{2,1,0:T(8,128)(2,1)S(1)} %get-tuple-element.195.refs_3_, ...), custom_call_target="tpu_custom_call" | custom-call | tf_op jit(solution)/shard_map/tiles/pallas_call | solution.py:263
  47.1 2.8 %tiles.22 = (bf16[24,128,128]{2,1,0:T(8,128)(2,1)}, bf16[24,128,128]{2,1,0:T(8,128)(2,1)S(1)}) custom-call(s32[8]{0:T(128)S(1)} %broadcast_xor_fusion.3.refs_0_, s32[8]{0:T(128)S(1)} %copy-done.7, s32[16,128]{1,0:T(8,128)S(1)} %get-tuple-element.487.refs_2_.table_ref, bf16[128,128,384]{2,1,0:T(8,128)(2,1)S(1)} %get-tuple-element.195.refs_3_, ...), custom_call_target="tpu_custom_call" | custom-call | tf_op jit(solution)/shard_map/tiles/pallas_call | solution.py:263
  49.9 1.6 %collective-permute-start.16 = (bf16[24,128,128]{2,1,0:T(8,128)(2,1)}, bf16[24,128,128]{2,1,0:T(8,128)(2,1)}, u32[]{:S(2)}, u32[]{:S(2)}) collective-permute-start(bf16[24,128,128]{2,1,0:T(8,128)(2,1)} %get-tuple-element.215), channel_id=1, source_target_pairs={{0,32},{8,40},{16,48},{24,56},{32,0},{40,8},{48,16},{56,24},{64,96... | collective-permute-start | bytes 2359304 | tf_op jit(solution)/shard_map/ppermute | solution.py:349
  51.5 2.8 %tiles.23 = (bf16[24,128,128]{2,1,0:T(8,128)(2,1)}, bf16[24,128,128]{2,1,0:T(8,128)(2,1)S(1)}) custom-call(s32[8]{0:T(128)S(1)} %broadcast_xor_fusion.4.refs_0_, s32[8]{0:T(128)S(1)} %copy-done.6, s32[16,128]{1,0:T(8,128)S(1)} %get-tuple-element.487.refs_2_.table_ref, bf16[128,128,384]{2,1,0:T(8,128)(2,1)S(1)} %get-tuple-element.195.refs_3_, ...), custom_call_target="tpu_custom_call" | custom-call | tf_op jit(solution)/shard_map/tiles/pallas_call | solution.py:263
  55.2 2.2 %collective-permute-start.17 = (bf16[24,128,128]{2,1,0:T(8,128)(2,1)}, bf16[24,128,128]{2,1,0:T(8,128)(2,1)S(1)}, u32[]{:S(2)}, u32[]{:S(2)}) collective-permute-start(bf16[24,128,128]{2,1,0:T(8,128)(2,1)} %get-tuple-element.218), channel_id=1, source_target_pairs={{0,96},{8,104},{16,112},{24,120},{32,64},{40,72},{48,80},{56,88},{... | collective-permute-start | bytes 2359304 | tf_op jit(solution)/shard_map/ppermute | solution.py:349
  57.5 3.5 %all-to-all-done.1.refs_0_ = bf16[32,320,128]{2,1,0:T(8,128)(2,1)} async-done(((bf16[32,320,128]{2,1,0:T(8,128)(2,1)}), bf16[32,320,128]{2,1,0:T(8,128)(2,1)}, u32[]{:S(2)}, u32[]{:S(2)}) %all-to-all-start.1) | async-done | bytes 2621472 | tf_op jit(solution)/shard_map/all_to_all | solution.py:371
  61.0 9.5 %prep.4 = (bf16[128,128,384]{2,1,0:T(8,128)(2,1)S(1)}, bf16[160,384,128]{2,1,0:T(8,128)(2,1)S(1)}) custom-call(f32[320,1]{1,0:T(8,128)S(1)} %copy.31.weights_ref, bf16[320,16384]{1,0:T(8,128)(2,1)} %adj_ref.3, bf16[320,16384]{1,0:T(8,128)(2,1)} %em_ref.5, bf16[32,320,128]{2,1,0:T(8,128)(2,1)} %all-to-all-done.1.refs_0_), custom_call_target="tpu_custom_call" | custom-call | tf_op jit(solution)/shard_map/prep/pallas_call | solution.py:171
  70.5 1.9 %tiles.24 = bf16[40,128,128]{2,1,0:T(8,128)(2,1)S(1)} custom-call(s32[8]{0:T(128)S(1)} %multiply_xor_fusion.1.refs_0_.refs_1_, s32[8]{0:T(128)S(1)} %multiply_xor_fusion.1.refs_0_.refs_1_, s32[16,128]{1,0:T(8,128)S(1)} %get-tuple-element.487.refs_2_.table_ref, bf16[128,128,384]{2,1,0:T(8,128)(2,1)S(1)} %get-tuple-element.207.refs_3_, ...), custom_call_target="tpu_custom_call" | custom-call | tf_op jit(solution)/shard_map/tiles/pallas_call | solution.py:263
  73.9 1.9 %tiles.25 = bf16[40,128,128]{2,1,0:T(8,128)(2,1)S(1)} custom-call(s32[8]{0:T(128)S(1)} %multiply_xor_fusion.1.refs_0_.refs_1_, s32[8]{0:T(128)S(1)} %multiply_xor_fusion.1.refs_0_.refs_1_, s32[16,128]{1,0:T(8,128)S(1)} %get-tuple-element.487.refs_2_.table_ref, bf16[128,128,384]{2,1,0:T(8,128)(2,1)S(1)} %get-tuple-element.207.refs_3_, ...), custom_call_target="tpu_custom_call" | custom-call | tf_op jit(solution)/shard_map/tiles/pallas_call | solution.py:263
  77.9 1.7 %tiles.26 = bf16[32,128,128]{2,1,0:T(8,128)(2,1)S(1)} custom-call(s32[8]{0:T(128)S(1)} %multiply_xor_fusion.1.refs_0_.refs_1_, s32[8]{0:T(128)S(1)} %multiply_xor_fusion.1.refs_0_.refs_1_, s32[16,128]{1,0:T(8,128)S(1)} %get-tuple-element.487.refs_2_.table_ref, bf16[128,128,384]{2,1,0:T(8,128)(2,1)S(1)} %get-tuple-element.207.refs_3_, ...), custom_call_target="tpu_custom_call" | custom-call | tf_op jit(solution)/shard_map/tiles/pallas_call | solution.py:263
  79.8 1.6 %collective-permute-start.20 = (bf16[12,128,128]{2,1,0:T(8,128)(2,1)S(1)}, bf16[12,128,128]{2,1,0:T(8,128)(2,1)S(1)}, u32[]{:S(2)}, u32[]{:S(2)}) collective-permute-start(bf16[12,128,128]{2,1,0:T(8,128)(2,1)S(1)} %get-tuple-element.226), channel_id=1, source_target_pairs={{0,32},{8,40},{16,48},{24,56},{32,0},{40,8},{48,16},{56,24},{64,96... | collective-permute-start | bytes 1179656 | tf_op jit(solution)/shard_map/ppermute | solution.py:349
  81.3 2.2 %collective-permute-start.21 = (bf16[12,128,128]{2,1,0:T(8,128)(2,1)S(1)}, bf16[12,128,128]{2,1,0:T(8,128)(2,1)S(1)}, u32[]{:S(2)}, u32[]{:S(2)}) collective-permute-start(bf16[12,128,128]{2,1,0:T(8,128)(2,1)S(1)} %get-tuple-element.229), channel_id=1, source_target_pairs={{0,96},{8,104},{16,112},{24,120},{32,64},{40,72},{48,80},{56,88},{... | collective-permute-start | bytes 1179656 | tf_op jit(solution)/shard_map/ppermute | solution.py:349
  84.9 1.9 %tiles.27 = (bf16[20,128,128]{2,1,0:T(8,128)(2,1)S(1)}, bf16[20,128,128]{2,1,0:T(8,128)(2,1)S(1)}) custom-call(s32[8]{0:T(128)S(1)} %broadcast_xor_fusion.5.refs_0_, s32[8]{0:T(128)S(1)} %copy-done.8, s32[16,128]{1,0:T(8,128)S(1)} %get-tuple-element.487.refs_2_.table_ref, bf16[128,128,384]{2,1,0:T(8,128)(2,1)S(1)} %get-tuple-element.207.refs_3_, ...), custom_call_target="tpu_custom_call" | custom-call | tf_op jit(solution)/shard_map/tiles/pallas_call | solution.py:263
  87.5 1.9 %tiles.28 = (bf16[20,128,128]{2,1,0:T(8,128)(2,1)S(1)}, bf16[20,128,128]{2,1,0:T(8,128)(2,1)S(1)}) custom-call(s32[8]{0:T(128)S(1)} %broadcast_xor_fusion.3.refs_0_, s32[8]{0:T(128)S(1)} %copy-done.7, s32[16,128]{1,0:T(8,128)S(1)} %get-tuple-element.487.refs_2_.table_ref, bf16[128,128,384]{2,1,0:T(8,128)(2,1)S(1)} %get-tuple-element.207.refs_3_, ...), custom_call_target="tpu_custom_call" | custom-call | tf_op jit(solution)/shard_map/tiles/pallas_call | solution.py:263
  89.4 1.7 %collective-permute-done.20.refs_1_ = bf16[12,128,128]{2,1,0:T(8,128)(2,1)S(1)} collective-permute-done((bf16[12,128,128]{2,1,0:T(8,128)(2,1)S(1)}, bf16[12,128,128]{2,1,0:T(8,128)(2,1)S(1)}, u32[]{:S(2)}, u32[]{:S(2)}) %collective-permute-start.20) | collective-permute-done | bytes 393248 | tf_op jit(solution)/shard_map/ppermute | solution.py:349
  93.7 1.8 %collective-permute-done.22.refs_1_ = bf16[12,128,128]{2,1,0:T(8,128)(2,1)S(1)} collective-permute-done((bf16[12,128,128]{2,1,0:T(8,128)(2,1)S(1)}, bf16[12,128,128]{2,1,0:T(8,128)(2,1)S(1)}, u32[]{:S(2)}, u32[]{:S(2)}) %collective-permute-start.22) | collective-permute-done | bytes 393248 | tf_op jit(solution)/shard_map/ppermute | solution.py:349
  95.7 1.7 %tiles.29 = (bf16[16,128,128]{2,1,0:T(8,128)(2,1)S(1)}, bf16[16,128,128]{2,1,0:T(8,128)(2,1)S(1)}) custom-call(s32[8]{0:T(128)S(1)} %broadcast_xor_fusion.4.refs_0_, s32[8]{0:T(128)S(1)} %copy-done.6, s32[16,128]{1,0:T(8,128)S(1)} %get-tuple-element.487.refs_2_.table_ref, bf16[128,128,384]{2,1,0:T(8,128)(2,1)S(1)} %get-tuple-element.207.refs_3_, ...), custom_call_target="tpu_custom_call" | custom-call | tf_op jit(solution)/shard_map/tiles/pallas_call | solution.py:263
  99.4 9.0 %collective-permute-done.24.refs_1_ = bf16[20,128,128]{2,1,0:T(8,128)(2,1)S(1)} collective-permute-done((bf16[20,128,128]{2,1,0:T(8,128)(2,1)S(1)}, bf16[20,128,128]{2,1,0:T(8,128)(2,1)S(1)}, u32[]{:S(2)}, u32[]{:S(2)}) %collective-permute-start.24) | collective-permute-done | bytes 655392 | tf_op jit(solution)/shard_map/ppermute | solution.py:349
  113.6 5.7 %collective-permute-done.27.refs_1_ = bf16[10,128,128]{2,1,0:T(8,128)(2,1)S(1)} collective-permute-done((bf16[10,128,128]{2,1,0:T(8,128)(2,1)S(1)}, bf16[10,128,128]{2,1,0:T(8,128)(2,1)S(1)}, u32[]{:S(2)}, u32[]{:S(2)}) %collective-permute-start.27) | collective-permute-done | bytes 327712 | tf_op jit(solution)/shard_map/ppermute | solution.py:349
  120.5 2.3 %collective-permute-start.28 = (bf16[5,128,128]{2,1,0:T(8,128)(2,1)S(1)}, bf16[5,128,128]{2,1,0:T(8,128)(2,1)S(1)}, u32[]{:S(2)}, u32[]{:S(2)}) collective-permute-start(bf16[5,128,128]{2,1,0:T(8,128)(2,1)S(1)} %get-tuple-element.248), channel_id=1, source_target_pairs={{0,96},{8,104},{16,112},{24,120},{32,64},{40,72},{48,80},{56,88},{... | collective-permute-start | bytes 491528 | tf_op jit(solution)/shard_map/ppermute | solution.py:349
  124.0 2.2 %collective-permute-done.33.refs_1_ = bf16[6,128,128]{2,1,0:T(8,128)(2,1)S(1)} collective-permute-done((bf16[6,128,128]{2,1,0:T(8,128)(2,1)S(1)}, bf16[6,128,128]{2,1,0:T(8,128)(2,1)S(1)}, u32[]{:S(2)}, u32[]{:S(2)}) %collective-permute-start.33) | collective-permute-done | bytes 196640 | tf_op jit(solution)/shard_map/ppermute | solution.py:349
  126.2 1.7 %finish.3 = (f32[32,128,128]{2,1,0:T(8,128)}, f32[8,128]{1,0:T(8,128)S(1)}) custom-call(s32[1]{0:T(128)} %bitcast.5.me_ref, s32[1]{0:T(128)S(6)} %copy.42.count_ref, s32[16,128]{1,0:T(8,128)S(1)} %get-tuple-element.487.refs_2_.table_ref, bf16[6,128,128]{2,1,0:T(8,128)(2,1)S(1)} %get-tuple-element.227.refs_0_, ...), custom_call_target="tpu_custom_call" | custom-call | tf_op jit(solution)/shard_map/finish/pallas_call | solution.py:326
  128.8 2.2 %finish.4 = (f32[32,128,128]{2,1,0:T(8,128)}, f32[8,128]{1,0:T(8,128)}) custom-call(s32[1]{0:T(128)} %bitcast.5.me_ref, s32[1]{0:T(128)S(6)} %copy.42.count_ref, s32[16,128]{1,0:T(8,128)S(1)} %get-tuple-element.487.refs_2_.table_ref, bf16[5,128,128]{2,1,0:T(8,128)(2,1)S(1)} %get-tuple-element.247.refs_0_, ...), custom_call_target="tpu_custom_call", output_to_operand_aliasing={{0}: (9, {})} | custom-call | tf_op jit(solution)/shard_map/finish/pallas_call | solution.py:326
  (78 shorter events, 23.5 us)
Async XLA Ops:
  3.5 15.4 %all-to-all-start = ((s32[8,1,128]{2,1,0:T(1,128)}), s32[8,1,128]{2,1,0:T(1,128)S(1)}, u32[]{:S(2)}, u32[]{:S(2)}) async-start(s32[8,1,128]{2,1,0:T(1,128)} %bitcast.3), calls=%async_computation | async-start | bytes 8192 | tf_op jit(solution)/shard_map/all_to_all | solution.py:369
  23.1 37.9 %all-to-all-start.1 = ((bf16[32,320,128]{2,1,0:T(8,128)(2,1)}), bf16[32,320,128]{2,1,0:T(8,128)(2,1)}, u32[]{:S(2)}, u32[]{:S(2)}) async-start(bf16[32,320,128]{2,1,0:T(8,128)(2,1)} %pack.1), calls=%async_computation.1 | async-start | bytes 5242880 | tf_op jit(solution)/shard_map/all_to_all | solution.py:371
  38.7 5.0 %collective-permute-start.12 = (bf16[48,128,128]{2,1,0:T(8,128)(2,1)S(1)}, bf16[48,128,128]{2,1,0:T(8,128)(2,1)S(1)}, u32[]{:S(2)}, u32[]{:S(2)}) collective-permute-start(bf16[48,128,128]{2,1,0:T(8,128)(2,1)S(1)} %tiles.18), channel_id=1, source_target_pairs={{0,8},{8,0},{16,24},{24,16},{32,40},{40,32},{48,56},{56,48},{64,72... | collective-permute-start | bytes 4718600 | tf_op jit(solution)/shard_map/ppermute | solution.py:349
  40.9 2.8 %copy-start.11 = (s32[8]{0:T(128)S(1)}, s32[8]{0:T(128)}, u32[]{:S(2)}) copy-start(s32[8]{0:T(128)} %constant.31.clone) | copy-start | bytes 100
  40.9 2.8 %copy-start.8 = (s32[8]{0:T(128)S(1)}, s32[8]{0:T(128)}, u32[]{:S(2)}) copy-start(s32[8]{0:T(128)} %constant.32.clone.refs_1_) | copy-start | bytes 100
  40.9 6.2 %collective-permute-start.13 = (bf16[48,128,128]{2,1,0:T(8,128)(2,1)S(1)}, bf16[48,128,128]{2,1,0:T(8,128)(2,1)S(1)}, u32[]{:S(2)}, u32[]{:S(2)}) collective-permute-start(bf16[48,128,128]{2,1,0:T(8,128)(2,1)S(1)} %tiles.19), channel_id=1, source_target_pairs={{0,8},{8,0},{16,24},{24,16},{32,40},{40,32},{48,56},{56,48},{64,72... | collective-permute-start | bytes 4718600 | tf_op jit(solution)/shard_map/ppermute | solution.py:349
  43.6 7.9 %collective-permute-start.14 = (bf16[48,128,128]{2,1,0:T(8,128)(2,1)S(1)}, bf16[48,128,128]{2,1,0:T(8,128)(2,1)S(1)}, u32[]{:S(2)}, u32[]{:S(2)}) collective-permute-start(bf16[48,128,128]{2,1,0:T(8,128)(2,1)S(1)} %tiles.20), channel_id=1, source_target_pairs={{0,8},{8,0},{16,24},{24,16},{32,40},{40,32},{48,56},{56,48},{64,72... | collective-permute-start | bytes 4718600 | tf_op jit(solution)/shard_map/ppermute | solution.py:349
  43.7 3.4 %copy-start.10 = (s32[8]{0:T(128)S(1)}, s32[8]{0:T(128)}, u32[]{:S(2)}) copy-start(s32[8]{0:T(128)} %constant.33.clone) | copy-start | bytes 100
  43.7 3.4 %copy-start.9 = (s32[8]{0:T(128)S(1)}, s32[8]{0:T(128)}, u32[]{:S(2)}) copy-start(s32[8]{0:T(128)} %constant.35.clone) | copy-start | bytes 100
  43.7 3.4 %copy-start.7 = (s32[8]{0:T(128)S(1)}, s32[8]{0:T(128)}, u32[]{:S(2)}) copy-start(s32[8]{0:T(128)} %constant.34.clone.refs_1_) | copy-start | bytes 100
  46.5 26.1 %collective-permute-start.15 = (bf16[24,128,128]{2,1,0:T(8,128)(2,1)}, bf16[24,128,128]{2,1,0:T(8,128)(2,1)}, u32[]{:S(2)}, u32[]{:S(2)}) collective-permute-start(bf16[24,128,128]{2,1,0:T(8,128)(2,1)} %get-tuple-element.211), channel_id=1, source_target_pairs={{0,16},{8,24},{16,0},{24,8},{32,48},{40,56},{48,32},{56,40},{64,80... | collective-permute-start | bytes 2359304 | tf_op jit(solution)/shard_map/ppermute | solution.py:349
  47.1 4.4 %copy-start.6 = (s32[8]{0:T(128)S(1)}, s32[8]{0:T(128)}, u32[]{:S(2)}) copy-start(s32[8]{0:T(128)} %constant.36.clone.refs_1_) | copy-start | bytes 100
  49.9 26.4 %collective-permute-start.16 = (bf16[24,128,128]{2,1,0:T(8,128)(2,1)}, bf16[24,128,128]{2,1,0:T(8,128)(2,1)}, u32[]{:S(2)}, u32[]{:S(2)}) collective-permute-start(bf16[24,128,128]{2,1,0:T(8,128)(2,1)} %get-tuple-element.215), channel_id=1, source_target_pairs={{0,32},{8,40},{16,48},{24,56},{32,0},{40,8},{48,16},{56,24},{64,96... | collective-permute-start | bytes 2359304 | tf_op jit(solution)/shard_map/ppermute | solution.py:349
  55.2 22.4 %collective-permute-start.17 = (bf16[24,128,128]{2,1,0:T(8,128)(2,1)}, bf16[24,128,128]{2,1,0:T(8,128)(2,1)S(1)}, u32[]{:S(2)}, u32[]{:S(2)}) collective-permute-start(bf16[24,128,128]{2,1,0:T(8,128)(2,1)} %get-tuple-element.218), channel_id=1, source_target_pairs={{0,96},{8,104},{16,112},{24,120},{32,64},{40,72},{48,80},{56,88},{... | collective-permute-start | bytes 2359304 | tf_op jit(solution)/shard_map/ppermute | solution.py:349
  72.4 11.1 %collective-permute-start.18 = (bf16[40,128,128]{2,1,0:T(8,128)(2,1)S(1)}, bf16[40,128,128]{2,1,0:T(8,128)(2,1)S(1)}, u32[]{:S(2)}, u32[]{:S(2)}) collective-permute-start(bf16[40,128,128]{2,1,0:T(8,128)(2,1)S(1)} %tiles.24), channel_id=1, source_target_pairs={{0,8},{8,0},{16,24},{24,16},{32,40},{40,32},{48,56},{56,48},{64,72... | collective-permute-start | bytes 3932168 | tf_op jit(solution)/shard_map/ppermute | solution.py:349
  75.8 11.0 %collective-permute-start.19 = (bf16[40,128,128]{2,1,0:T(8,128)(2,1)S(1)}, bf16[40,128,128]{2,1,0:T(8,128)(2,1)S(1)}, u32[]{:S(2)}, u32[]{:S(2)}) collective-permute-start(bf16[40,128,128]{2,1,0:T(8,128)(2,1)S(1)} %tiles.25), channel_id=1, source_target_pairs={{0,8},{8,0},{16,24},{24,16},{32,40},{40,32},{48,56},{56,48},{64,72... | collective-permute-start | bytes 3932168 | tf_op jit(solution)/shard_map/ppermute | solution.py:349
  79.6 16.1 %collective-permute-start.23 = (bf16[32,128,128]{2,1,0:T(8,128)(2,1)S(1)}, bf16[32,128,128]{2,1,0:T(8,128)(2,1)S(1)}, u32[]{:S(2)}, u32[]{:S(2)}) collective-permute-start(bf16[32,128,128]{2,1,0:T(8,128)(2,1)S(1)} %tiles.26), channel_id=1, source_target_pairs={{0,8},{8,0},{16,24},{24,16},{32,40},{40,32},{48,56},{56,48},{64,72... | collective-permute-start | bytes 3145736 | tf_op jit(solution)/shard_map/ppermute | solution.py:349
  79.8 11.4 %collective-permute-start.20 = (bf16[12,128,128]{2,1,0:T(8,128)(2,1)S(1)}, bf16[12,128,128]{2,1,0:T(8,128)(2,1)S(1)}, u32[]{:S(2)}, u32[]{:S(2)}) collective-permute-start(bf16[12,128,128]{2,1,0:T(8,128)(2,1)S(1)} %get-tuple-element.226), channel_id=1, source_target_pairs={{0,32},{8,40},{16,48},{24,56},{32,0},{40,8},{48,16},{56,24},{64,96... | collective-permute-start | bytes 1179656 | tf_op jit(solution)/shard_map/ppermute | solution.py:349
  81.3 12.3 %collective-permute-start.21 = (bf16[12,128,128]{2,1,0:T(8,128)(2,1)S(1)}, bf16[12,128,128]{2,1,0:T(8,128)(2,1)S(1)}, u32[]{:S(2)}, u32[]{:S(2)}) collective-permute-start(bf16[12,128,128]{2,1,0:T(8,128)(2,1)S(1)} %get-tuple-element.229), channel_id=1, source_target_pairs={{0,96},{8,104},{16,112},{24,120},{32,64},{40,72},{48,80},{56,88},{... | collective-permute-start | bytes 1179656 | tf_op jit(solution)/shard_map/ppermute | solution.py:349
  83.5 12.0 %collective-permute-start.22 = (bf16[12,128,128]{2,1,0:T(8,128)(2,1)S(1)}, bf16[12,128,128]{2,1,0:T(8,128)(2,1)S(1)}, u32[]{:S(2)}, u32[]{:S(2)}) collective-permute-start(bf16[12,128,128]{2,1,0:T(8,128)(2,1)S(1)} %get-tuple-element.232), channel_id=1, source_target_pairs={{0,16},{8,24},{16,0},{24,8},{32,48},{40,56},{48,32},{56,40},{64,80... | collective-permute-start | bytes 1179656 | tf_op jit(solution)/shard_map/ppermute | solution.py:349
  86.8 21.6 %collective-permute-start.24 = (bf16[20,128,128]{2,1,0:T(8,128)(2,1)S(1)}, bf16[20,128,128]{2,1,0:T(8,128)(2,1)S(1)}, u32[]{:S(2)}, u32[]{:S(2)}) collective-permute-start(bf16[20,128,128]{2,1,0:T(8,128)(2,1)S(1)} %get-tuple-element.237), channel_id=1, source_target_pairs={{0,16},{8,24},{16,0},{24,8},{32,48},{40,56},{48,32},{56,40},{64,80... | collective-permute-start | bytes 1966088 | tf_op jit(solution)/shard_map/ppermute | solution.py:349
  91.2 18.2 %collective-permute-start.25 = (bf16[20,128,128]{2,1,0:T(8,128)(2,1)S(1)}, bf16[20,128,128]{2,1,0:T(8,128)(2,1)S(1)}, u32[]{:S(2)}, u32[]{:S(2)}) collective-permute-start(bf16[20,128,128]{2,1,0:T(8,128)(2,1)S(1)} %get-tuple-element.240), channel_id=1, source_target_pairs={{0,32},{8,40},{16,48},{24,56},{32,0},{40,8},{48,16},{56,24},{64,96... | collective-permute-start | bytes 1966088 | tf_op jit(solution)/shard_map/ppermute | solution.py:349
  97.3 13.3 %collective-permute-start.26 = (bf16[16,128,128]{2,1,0:T(8,128)(2,1)S(1)}, bf16[16,128,128]{2,1,0:T(8,128)(2,1)S(1)}, u32[]{:S(2)}, u32[]{:S(2)}) collective-permute-start(bf16[16,128,128]{2,1,0:T(8,128)(2,1)S(1)} %get-tuple-element.243), channel_id=1, source_target_pairs={{0,96},{8,104},{16,112},{24,120},{32,64},{40,72},{48,80},{56,88},{... | collective-permute-start | bytes 1572872 | tf_op jit(solution)/shard_map/ppermute | solution.py:349
  108.6 10.7 %collective-permute-start.27 = (bf16[10,128,128]{2,1,0:T(8,128)(2,1)S(1)}, bf16[10,128,128]{2,1,0:T(8,128)(2,1)S(1)}, u32[]{:S(2)}, u32[]{:S(2)}) collective-permute-start(bf16[10,128,128]{2,1,0:T(8,128)(2,1)S(1)} %get-tuple-element.246), channel_id=1, source_target_pairs={{0,32},{8,40},{16,48},{24,56},{32,0},{40,8},{48,16},{56,24},{64,96... | collective-permute-start | bytes 983048 | tf_op jit(solution)/shard_map/ppermute | solution.py:349
  109.5 10.9 %collective-permute-start.29 = (bf16[10,128,128]{2,1,0:T(8,128)(2,1)S(1)}, bf16[10,128,128]{2,1,0:T(8,128)(2,1)S(1)}, u32[]{:S(2)}, u32[]{:S(2)}) collective-permute-start(bf16[10,128,128]{2,1,0:T(8,128)(2,1)S(1)} %get-tuple-element.250), channel_id=1, source_target_pairs={{0,96},{8,104},{16,112},{24,120},{32,64},{40,72},{48,80},{56,88},{... | collective-permute-start | bytes 983048 | tf_op jit(solution)/shard_map/ppermute | solution.py:349
  110.8 12.0 %collective-permute-start.31 = (bf16[8,128,128]{2,1,0:T(8,128)(2,1)S(1)}, bf16[8,128,128]{2,1,0:T(8,128)(2,1)S(1)}, u32[]{:S(2)}, u32[]{:S(2)}) collective-permute-start(bf16[8,128,128]{2,1,0:T(8,128)(2,1)S(1)} %get-tuple-element.254), channel_id=1, source_target_pairs={{0,16},{8,24},{16,0},{24,8},{32,48},{40,56},{48,32},{56,40},{64,80... | collective-permute-start | bytes 786440 | tf_op jit(solution)/shard_map/ppermute | solution.py:349
  111.8 11.9 %collective-permute-start.35 = (bf16[6,128,128]{2,1,0:T(8,128)(2,1)S(1)}, bf16[6,128,128]{2,1,0:T(8,128)(2,1)S(1)}, u32[]{:S(2)}, u32[]{:S(2)}) collective-permute-start(bf16[6,128,128]{2,1,0:T(8,128)(2,1)S(1)} %get-tuple-element.260), channel_id=1, source_target_pairs={{0,32},{8,40},{16,48},{24,56},{32,0},{40,8},{48,16},{56,24},{64,96... | collective-permute-start | bytes 589832 | tf_op jit(solution)/shard_map/ppermute | solution.py:349
  112.7 11.2 %collective-permute-start.34 = (bf16[6,128,128]{2,1,0:T(8,128)(2,1)S(1)}, bf16[6,128,128]{2,1,0:T(8,128)(2,1)S(1)}, u32[]{:S(2)}, u32[]{:S(2)}) collective-permute-start(bf16[6,128,128]{2,1,0:T(8,128)(2,1)S(1)} %get-tuple-element.259), channel_id=1, source_target_pairs={{0,16},{8,24},{16,0},{24,8},{32,48},{40,56},{48,32},{56,40},{64,80... | collective-permute-start | bytes 589832 | tf_op jit(solution)/shard_map/ppermute | solution.py:349
  119.3 6.9 %collective-permute-start.33 = (bf16[6,128,128]{2,1,0:T(8,128)(2,1)S(1)}, bf16[6,128,128]{2,1,0:T(8,128)(2,1)S(1)}, u32[]{:S(2)}, u32[]{:S(2)}) collective-permute-start(bf16[6,128,128]{2,1,0:T(8,128)(2,1)S(1)} %get-tuple-element.258), channel_id=1, source_target_pairs={{0,96},{8,104},{16,112},{24,120},{32,64},{40,72},{48,80},{56,88},{... | collective-permute-start | bytes 589832 | tf_op jit(solution)/shard_map/ppermute | solution.py:349
  120.5 7.4 %collective-permute-start.28 = (bf16[5,128,128]{2,1,0:T(8,128)(2,1)S(1)}, bf16[5,128,128]{2,1,0:T(8,128)(2,1)S(1)}, u32[]{:S(2)}, u32[]{:S(2)}) collective-permute-start(bf16[5,128,128]{2,1,0:T(8,128)(2,1)S(1)} %get-tuple-element.248), channel_id=1, source_target_pairs={{0,96},{8,104},{16,112},{24,120},{32,64},{40,72},{48,80},{56,88},{... | collective-permute-start | bytes 491528 | tf_op jit(solution)/shard_map/ppermute | solution.py:349
  122.8 5.9 %collective-permute-start.30 = (bf16[5,128,128]{2,1,0:T(8,128)(2,1)S(1)}, bf16[5,128,128]{2,1,0:T(8,128)(2,1)S(1)}, u32[]{:S(2)}, u32[]{:S(2)}) collective-permute-start(bf16[5,128,128]{2,1,0:T(8,128)(2,1)S(1)} %get-tuple-element.252), channel_id=1, source_target_pairs={{0,16},{8,24},{16,0},{24,8},{32,48},{40,56},{48,32},{56,40},{64,80... | collective-permute-start | bytes 491528 | tf_op jit(solution)/shard_map/ppermute | solution.py:349
  123.7 5.0 %collective-permute-start.32 = (bf16[4,128,128]{2,1,0:T(8,128)(2,1)S(1)}, bf16[4,128,128]{2,1,0:T(8,128)(2,1)S(1)}, u32[]{:S(2)}, u32[]{:S(2)}) collective-permute-start(bf16[4,128,128]{2,1,0:T(8,128)(2,1)S(1)} %get-tuple-element.256), channel_id=1, source_target_pairs={{0,32},{8,40},{16,48},{24,56},{32,0},{40,8},{48,16},{56,24},{64,96... | collective-permute-start | bytes 393224 | tf_op jit(solution)/shard_map/ppermute | solution.py:349
  (3 other events, 3.4 us)

commit v5 on v4

--- a/solution.py
+++ b/solution.py
@@ -342,6 +342,7 @@
     (UP_Y, DOWN_Y, ALONG_X),
     (DOWN_Y, ALONG_X, UP_Y),
 )
+TURNS = (ORDERS, ORDERS[1:] + ORDERS[:1])
 
 
 def swap(a, mask):
@@ -381,15 +382,15 @@
         )[0]
 
     def kept(c, i, wt, e_blocks, last, core, rolled=False):
-        masks = [m for lead in (1, 0) for m in order_masks(ORDERS[i], lead)]
+        masks = [m for lead in (1, 0) for m in order_masks(TURNS[c][i], lead)]
         mine = me ^ jnp.array(masks, I32)
         places = jnp.array([m // 2 for m in masks], I32)
         return tiles(
             after(mine, last), places, table, wt, e_blocks, offsets[c][i], cuts[c][i], 2, rolled, core
         )
 
-    def exchange(outs, step):
-        return [(out[1], swap(out[0], order[step])) for out, order in zip(outs, ORDERS)]
+    def exchange(c, outs, step):
+        return [(out[1], swap(out[0], order[step])) for out, order in zip(outs, TURNS[c])]
 
     def halve(pairs, last):
         outs = []
@@ -407,7 +408,7 @@
     for i in range(3):
         early.append(kept(0, i, wt, e_blocks, last, cores[i]))
         last = early[i][1]
-    early = exchange(early, 0)
+    early = exchange(0, early, 0)
     wt, e_blocks = prep(after(weights, last), adjoint, emission, far)
     last, cores, late = wt, [], []
     halved = []
@@ -417,17 +418,17 @@
         for j in ((0,), (1, 2), ())[i]:
             some, last = halve(early[j : j + 1], last)
             halved += some
-    early = exchange(halved, 1)
+    early = exchange(0, halved, 1)
     for i in range(3):
         if i == 2:
             early, last = halve(early, last)
-            early = exchange(early, 2)
+            early = exchange(0, early, 2)
         late.append(kept(1, i, wt, e_blocks, last, cores[i]))
         last = late[i][1]
-    late = exchange(late, 0)
+    late = exchange(1, late, 0)
     late, last = halve(late, (last, crowded))
-    late, last = halve(exchange(late, 1), last)
-    late = exchange(late, 2)
+    late, last = halve(exchange(1, late, 1), last)
+    late = exchange(1, late, 2)
     out, done = finish(after(me, last), counts, table, early, tuple(offsets[0]))
     out, _ = finish(me, counts, table, late, tuple(offsets[1]), (out, done))
 
@@ -442,8 +443,8 @@
             again.append(kept(0, i, wt, e_blocks, last, cores[i], True))
             last = again[i][1]
         for step in range(2):
-            again, last = halve(exchange(again, step), last)
-        out, _ = finish(me, counts, table, exchange(again, 2), tuple(offsets[0]), (out, counts))
+            again, last = halve(exchange(0, again, step), last)
+        out, _ = finish(me, counts, table, exchange(0, again, 2), tuple(offsets[0]), (out, counts))
         return jnp.zeros((), bool), out
 
     return lax.while_loop(lambda state: state[0], crowded_group, (crowded, out))[1][None]

time: 132 us -> 132 us (level)
  waiting for transfers between devices: 32.7 us -> 25.3 us
  starting transfers between devices: 35.8 us -> 42.6 us
    ppermute x24, waiting for transfers between devices: 22.3 us -> 14.9 us  [swap(): return lax.ppermute(a, 'tm', [(i, i ^ mask) for i in range(n)])]
    ppermute x24, starting transfers between devices: 23.6 us -> 30.4 us  [swap(): return lax.ppermute(a, 'tm', [(i, i ^ mask) for i in range(n)])]
  transfers between devices with their start and end apart: 26 -> 26, of which waited for: 11 -> 10; matrix products, arithmetic and copies ran while one was open for 1% -> 1% of each run, Pallas kernels for 38% -> 38%
where the time goes in v5:
time: 132 us; the launch traced here: 131 us
  Pallas kernels  57.9 us (44%)
  starting transfers between devices  42.6 us (32%)
  waiting for transfers between devices  25.3 us (19%)
  local copies, waits for them, and re-layouts  2.69 us (2%)
    ppermute x24, starting transfers between devices, swap(): return lax.ppermute(a, 'tm', [(i, i ^ mask) for i in range(n)])  30.4 us
    pallas_call x12, Pallas kernels, tiles(): pl.pallas_call(functools.partial(tiles_kernel, first, per, with_add, roll...  25.5 us
    pallas_call x2, Pallas kernels, prep(): pl.pallas_call(functools.partial(prep_kernel, with_far), in_specs=[vmem]...  18.4 us
    ppermute x24, waiting for transfers between devices, swap(): return lax.ppermute(a, 'tm', [(i, i ^ mask) for i in range(n)])  14.9 us
    all_to_all x1, starting transfers between devices, body(): lax.all_to_all(request, 'tile', split_axis=0, concat_axis=0, tiled=True)  7.86 us
    all_to_all x1, waiting for transfers between devices, body(): lax.all_to_all(request, 'tile', split_axis=0, concat_axis=0, tiled=True)  6.9 us
    all_to_all x1, starting transfers between devices, body(): lax.all_to_all(outgoing, 'tile', split_axis=0, concat_axis=0, tiled=True)  4.41 us
    pallas_call x1, Pallas kernels, pack(): pl.pallas_call(pack_kernel, in_specs=[pl.BlockSpec(memory_space=pltpu.SME...  4.13 us
  transfers between devices with their start and end apart: 26, of which 10 were waited for; matrix products, arithmetic and copies ran while one was open for 1% of the time, Pallas kernels for 38%

profile of v5, /device:TPU:0, one launch (start us, length us, event | category | flops | bytes accessed | tf_op | source)
XLA Modules:
  0.0 131.2 jit_solution(5967229356521659622)
XLA Ops:
  1.3 2.2 %plan.1 = (s32[8,128]{1,0:T(8,128)}, s32[16,128]{1,0:T(8,128)S(1)}) custom-call(s32[1]{0:T(128)} %bitcast.own_ref, s32[1]{0:T(128)S(6)} %copy.42.count_ref, s32[2,512]{1,0:T(2,128)S(1)} %bitcast.12), custom_call_target="tpu_custom_call" | custom-call | tf_op jit(solution)/shard_map/plan/pallas_call | solution.py:89
  3.5 7.9 %all-to-all-start = ((s32[8,1,128]{2,1,0:T(1,128)}), s32[8,1,128]{2,1,0:T(1,128)S(1)}, u32[]{:S(2)}, u32[]{:S(2)}) async-start(s32[8,1,128]{2,1,0:T(1,128)} %bitcast.3), calls=%async_computation | async-start | bytes 8192 | tf_op jit(solution)/shard_map/all_to_all | solution.py:370
  12.1 6.9 %all-to-all-done = s32[8,1,128]{2,1,0:T(1,128)S(1)} async-done(((s32[8,1,128]{2,1,0:T(1,128)}), s32[8,1,128]{2,1,0:T(1,128)S(1)}, u32[]{:S(2)}, u32[]{:S(2)}) %all-to-all-start) | async-done | bytes 4128 | tf_op jit(solution)/shard_map/all_to_all | solution.py:370
  19.0 4.1 %pack.1 = bf16[32,320,128]{2,1,0:T(8,128)(2,1)} custom-call(s32[1]{0:T(128)} %bitcast.own_ref, s32[8,128]{1,0:T(8,128)S(1)} %bitcast.10, bf16[320,16384]{1,0:T(8,128)(2,1)} %em_ref.5), custom_call_target="tpu_custom_call" | custom-call | tf_op jit(solution)/shard_map/pack/pallas_call | solution.py:219
  23.1 4.4 %all-to-all-start.1 = ((bf16[32,320,128]{2,1,0:T(8,128)(2,1)}), bf16[32,320,128]{2,1,0:T(8,128)(2,1)}, u32[]{:S(2)}, u32[]{:S(2)}) async-start(bf16[32,320,128]{2,1,0:T(8,128)(2,1)} %pack.1), calls=%async_computation.1 | async-start | bytes 5242880 | tf_op jit(solution)/shard_map/all_to_all | solution.py:372
  27.7 8.9 %prep.3 = (bf16[128,128,384]{2,1,0:T(8,128)(2,1)S(1)}, bf16[128,384,128]{2,1,0:T(8,128)(2,1)S(1)}) custom-call(f32[320,1]{1,0:T(8,128)S(1)} %copy.30.weights_ref, bf16[320,16384]{1,0:T(8,128)(2,1)} %adj_ref.3, bf16[320,16384]{1,0:T(8,128)(2,1)} %em_ref.5), custom_call_target="tpu_custom_call" | custom-call | tf_op jit(solution)/shard_map/prep/pallas_call | solution.py:171
  36.6 2.1 %tiles.18 = bf16[48,128,128]{2,1,0:T(8,128)(2,1)S(1)} custom-call(s32[8]{0:T(128)S(1)} %multiply_xor_fusion.1.refs_0_.refs_1_, s32[8]{0:T(128)S(1)} %multiply_xor_fusion.1.refs_0_.refs_1_, s32[16,128]{1,0:T(8,128)S(1)} %get-tuple-element.487.refs_2_.table_ref, bf16[128,128,384]{2,1,0:T(8,128)(2,1)S(1)} %get-tuple-element.195.refs_3_, ...), custom_call_target="tpu_custom_call" | custom-call | tf_op jit(solution)/shard_map/tiles/pallas_call | solution.py:263
  38.8 2.1 %tiles.19 = bf16[48,128,128]{2,1,0:T(8,128)(2,1)S(1)} custom-call(s32[8]{0:T(128)S(1)} %multiply_xor_fusion.1.refs_0_.refs_1_, s32[8]{0:T(128)S(1)} %multiply_xor_fusion.1.refs_0_.refs_1_, s32[16,128]{1,0:T(8,128)S(1)} %get-tuple-element.487.refs_2_.table_ref, bf16[128,128,384]{2,1,0:T(8,128)(2,1)S(1)} %get-tuple-element.195.refs_3_, ...), custom_call_target="tpu_custom_call" | custom-call | tf_op jit(solution)/shard_map/tiles/pallas_call | solution.py:263
  41.5 2.1 %tiles.20 = bf16[48,128,128]{2,1,0:T(8,128)(2,1)S(1)} custom-call(s32[8]{0:T(128)S(1)} %multiply_xor_fusion.1.refs_0_.refs_1_, s32[8]{0:T(128)S(1)} %multiply_xor_fusion.1.refs_0_.refs_1_, s32[16,128]{1,0:T(8,128)S(1)} %get-tuple-element.487.refs_2_.table_ref, bf16[128,128,384]{2,1,0:T(8,128)(2,1)S(1)} %get-tuple-element.195.refs_3_, ...), custom_call_target="tpu_custom_call" | custom-call | tf_op jit(solution)/shard_map/tiles/pallas_call | solution.py:263
  43.7 2.8 %tiles.21 = (bf16[24,128,128]{2,1,0:T(8,128)(2,1)}, bf16[24,128,128]{2,1,0:T(8,128)(2,1)S(1)}) custom-call(s32[8]{0:T(128)S(1)} %broadcast_xor_fusion.3.refs_0_, s32[8]{0:T(128)S(1)} %copy-done.6, s32[16,128]{1,0:T(8,128)S(1)} %get-tuple-element.487.refs_2_.table_ref, bf16[128,128,384]{2,1,0:T(8,128)(2,1)S(1)} %get-tuple-element.195.refs_3_, ...), custom_call_target="tpu_custom_call" | custom-call | tf_op jit(solution)/shard_map/tiles/pallas_call | solution.py:263
  47.1 2.8 %tiles.22 = (bf16[24,128,128]{2,1,0:T(8,128)(2,1)}, bf16[24,128,128]{2,1,0:T(8,128)(2,1)S(1)}) custom-call(s32[8]{0:T(128)S(1)} %broadcast_xor_fusion.5.refs_0_, s32[8]{0:T(128)S(1)} %copy-done.8, s32[16,128]{1,0:T(8,128)S(1)} %get-tuple-element.487.refs_2_.table_ref, bf16[128,128,384]{2,1,0:T(8,128)(2,1)S(1)} %get-tuple-element.195.refs_3_, ...), custom_call_target="tpu_custom_call" | custom-call | tf_op jit(solution)/shard_map/tiles/pallas_call | solution.py:263
  51.5 2.8 %tiles.23 = (bf16[24,128,128]{2,1,0:T(8,128)(2,1)}, bf16[24,128,128]{2,1,0:T(8,128)(2,1)S(1)}) custom-call(s32[8]{0:T(128)S(1)} %broadcast_xor_fusion.4.refs_0_, s32[8]{0:T(128)S(1)} %copy-done.7, s32[16,128]{1,0:T(8,128)S(1)} %get-tuple-element.487.refs_2_.table_ref, bf16[128,128,384]{2,1,0:T(8,128)(2,1)S(1)} %get-tuple-element.195.refs_3_, ...), custom_call_target="tpu_custom_call" | custom-call | tf_op jit(solution)/shard_map/tiles/pallas_call | solution.py:263
  55.2 2.2 %collective-permute-start.17 = (bf16[24,128,128]{2,1,0:T(8,128)(2,1)}, bf16[24,128,128]{2,1,0:T(8,128)(2,1)S(1)}, u32[]{:S(2)}, u32[]{:S(2)}) collective-permute-start(bf16[24,128,128]{2,1,0:T(8,128)(2,1)} %get-tuple-element.218), channel_id=1, source_target_pairs={{0,96},{8,104},{16,112},{24,120},{32,64},{40,72},{48,80},{56,88},{... | collective-permute-start | bytes 2359304 | tf_op jit(solution)/shard_map/ppermute | solution.py:350
  57.5 3.5 %all-to-all-done.1.refs_0_ = bf16[32,320,128]{2,1,0:T(8,128)(2,1)} async-done(((bf16[32,320,128]{2,1,0:T(8,128)(2,1)}), bf16[32,320,128]{2,1,0:T(8,128)(2,1)}, u32[]{:S(2)}, u32[]{:S(2)}) %all-to-all-start.1) | async-done | bytes 2621472 | tf_op jit(solution)/shard_map/all_to_all | solution.py:372
  61.0 9.5 %prep.4 = (bf16[128,128,384]{2,1,0:T(8,128)(2,1)S(1)}, bf16[160,384,128]{2,1,0:T(8,128)(2,1)S(1)}) custom-call(f32[320,1]{1,0:T(8,128)S(1)} %copy.31.weights_ref, bf16[320,16384]{1,0:T(8,128)(2,1)} %adj_ref.3, bf16[320,16384]{1,0:T(8,128)(2,1)} %em_ref.5, bf16[32,320,128]{2,1,0:T(8,128)(2,1)} %all-to-all-done.1.refs_0_), custom_call_target="tpu_custom_call" | custom-call | tf_op jit(solution)/shard_map/prep/pallas_call | solution.py:171
  70.5 1.9 %tiles.24 = bf16[40,128,128]{2,1,0:T(8,128)(2,1)S(1)} custom-call(s32[8]{0:T(128)S(1)} %multiply_xor_fusion.1.refs_0_.refs_1_, s32[8]{0:T(128)S(1)} %multiply_xor_fusion.1.refs_0_.refs_1_, s32[16,128]{1,0:T(8,128)S(1)} %get-tuple-element.487.refs_2_.table_ref, bf16[128,128,384]{2,1,0:T(8,128)(2,1)S(1)} %get-tuple-element.207.refs_3_, ...), custom_call_target="tpu_custom_call" | custom-call | tf_op jit(solution)/shard_map/tiles/pallas_call | solution.py:263
  73.9 1.9 %tiles.25 = bf16[40,128,128]{2,1,0:T(8,128)(2,1)S(1)} custom-call(s32[8]{0:T(128)S(1)} %multiply_xor_fusion.1.refs_0_.refs_1_, s32[8]{0:T(128)S(1)} %multiply_xor_fusion.1.refs_0_.refs_1_, s32[16,128]{1,0:T(8,128)S(1)} %get-tuple-element.487.refs_2_.table_ref, bf16[128,128,384]{2,1,0:T(8,128)(2,1)S(1)} %get-tuple-element.207.refs_3_, ...), custom_call_target="tpu_custom_call" | custom-call | tf_op jit(solution)/shard_map/tiles/pallas_call | solution.py:263
  81.3 2.2 %collective-permute-start.21 = (bf16[12,128,128]{2,1,0:T(8,128)(2,1)S(1)}, bf16[12,128,128]{2,1,0:T(8,128)(2,1)S(1)}, u32[]{:S(2)}, u32[]{:S(2)}) collective-permute-start(bf16[12,128,128]{2,1,0:T(8,128)(2,1)S(1)} %get-tuple-element.229), channel_id=1, source_target_pairs={{0,96},{8,104},{16,112},{24,120},{32,64},{40,72},{48,80},{56,88},{... | collective-permute-start | bytes 1179656 | tf_op jit(solution)/shard_map/ppermute | solution.py:350
  84.9 1.9 %tiles.27 = (bf16[20,128,128]{2,1,0:T(8,128)(2,1)S(1)}, bf16[20,128,128]{2,1,0:T(8,128)(2,1)S(1)}) custom-call(s32[8]{0:T(128)S(1)} %broadcast_xor_fusion.5.refs_0_, s32[8]{0:T(128)S(1)} %copy-done.8, s32[16,128]{1,0:T(8,128)S(1)} %get-tuple-element.487.refs_2_.table_ref, bf16[128,128,384]{2,1,0:T(8,128)(2,1)S(1)} %get-tuple-element.207.refs_3_, ...), custom_call_target="tpu_custom_call" | custom-call | tf_op jit(solution)/shard_map/tiles/pallas_call | solution.py:263
  87.6 1.9 %tiles.28 = (bf16[20,128,128]{2,1,0:T(8,128)(2,1)S(1)}, bf16[20,128,128]{2,1,0:T(8,128)(2,1)S(1)}) custom-call(s32[8]{0:T(128)S(1)} %broadcast_xor_fusion.4.refs_0_, s32[8]{0:T(128)S(1)} %copy-done.7, s32[16,128]{1,0:T(8,128)S(1)} %get-tuple-element.487.refs_2_.table_ref, bf16[128,128,384]{2,1,0:T(8,128)(2,1)S(1)} %get-tuple-element.207.refs_3_, ...), custom_call_target="tpu_custom_call" | custom-call | tf_op jit(solution)/shard_map/tiles/pallas_call | solution.py:263
  89.5 2.2 %collective-permute-done.20.refs_1_ = bf16[12,128,128]{2,1,0:T(8,128)(2,1)S(1)} collective-permute-done((bf16[12,128,128]{2,1,0:T(8,128)(2,1)S(1)}, bf16[12,128,128]{2,1,0:T(8,128)(2,1)S(1)}, u32[]{:S(2)}, u32[]{:S(2)}) %collective-permute-start.20) | collective-permute-done | bytes 393248 | tf_op jit(solution)/shard_map/ppermute | solution.py:350
  91.7 3.0 %collective-permute-start.25 = (bf16[20,128,128]{2,1,0:T(8,128)(2,1)S(1)}, bf16[20,128,128]{2,1,0:T(8,128)(2,1)S(1)}, u32[]{:S(2)}, u32[]{:S(2)}) collective-permute-start(bf16[20,128,128]{2,1,0:T(8,128)(2,1)S(1)} %get-tuple-element.240), channel_id=1, source_target_pairs={{0,96},{8,104},{16,112},{24,120},{32,64},{40,72},{48,80},{56,88},{... | collective-permute-start | bytes 1966088 | tf_op jit(solution)/shard_map/ppermute | solution.py:350
  96.8 1.7 %collective-permute-start.26 = (bf16[16,128,128]{2,1,0:T(8,128)(2,1)S(1)}, bf16[16,128,128]{2,1,0:T(8,128)(2,1)S(1)}, u32[]{:S(2)}, u32[]{:S(2)}) collective-permute-start(bf16[16,128,128]{2,1,0:T(8,128)(2,1)S(1)} %get-tuple-element.243), channel_id=1, source_target_pairs={{0,16},{8,24},{16,0},{24,8},{32,48},{40,56},{48,32},{56,40},{64,80... | collective-permute-start | bytes 1572872 | tf_op jit(solution)/shard_map/ppermute | solution.py:350
  99.2 6.0 %collective-permute-done.24.refs_1_ = bf16[20,128,128]{2,1,0:T(8,128)(2,1)S(1)} collective-permute-done((bf16[20,128,128]{2,1,0:T(8,128)(2,1)S(1)}, bf16[20,128,128]{2,1,0:T(8,128)(2,1)S(1)}, u32[]{:S(2)}, u32[]{:S(2)}) %collective-permute-start.24) | collective-permute-done | bytes 655392 | tf_op jit(solution)/shard_map/ppermute | solution.py:350
  105.4 3.1 %collective-permute-start.27 = (bf16[10,128,128]{2,1,0:T(8,128)(2,1)S(1)}, bf16[10,128,128]{2,1,0:T(8,128)(2,1)S(1)}, u32[]{:S(2)}, u32[]{:S(2)}) collective-permute-start(bf16[10,128,128]{2,1,0:T(8,128)(2,1)S(1)} %get-tuple-element.246), channel_id=1, source_target_pairs={{0,96},{8,104},{16,112},{24,120},{32,64},{40,72},{48,80},{56,88},{... | collective-permute-start | bytes 983048 | tf_op jit(solution)/shard_map/ppermute | solution.py:350
  110.2 1.9 %collective-permute-start.35 = (bf16[6,128,128]{2,1,0:T(8,128)(2,1)S(1)}, bf16[6,128,128]{2,1,0:T(8,128)(2,1)S(1)}, u32[]{:S(2)}, u32[]{:S(2)}) collective-permute-start(bf16[6,128,128]{2,1,0:T(8,128)(2,1)S(1)} %get-tuple-element.260), channel_id=1, source_target_pairs={{0,32},{8,40},{16,48},{24,56},{32,0},{40,8},{48,16},{56,24},{64,96... | collective-permute-start | bytes 589832 | tf_op jit(solution)/shard_map/ppermute | solution.py:350
  113.2 2.7 %collective-permute-done.27.refs_1_ = bf16[10,128,128]{2,1,0:T(8,128)(2,1)S(1)} collective-permute-done((bf16[10,128,128]{2,1,0:T(8,128)(2,1)S(1)}, bf16[10,128,128]{2,1,0:T(8,128)(2,1)S(1)}, u32[]{:S(2)}, u32[]{:S(2)}) %collective-permute-start.27) | collective-permute-done | bytes 327712 | tf_op jit(solution)/shard_map/ppermute | solution.py:350
  115.9 3.0 %collective-permute-start.33 = (bf16[6,128,128]{2,1,0:T(8,128)(2,1)S(1)}, bf16[6,128,128]{2,1,0:T(8,128)(2,1)S(1)}, u32[]{:S(2)}, u32[]{:S(2)}) collective-permute-start(bf16[6,128,128]{2,1,0:T(8,128)(2,1)S(1)} %get-tuple-element.258), channel_id=1, source_target_pairs={{0,96},{8,104},{16,112},{24,120},{32,64},{40,72},{48,80},{56,88},{... | collective-permute-start | bytes 589832 | tf_op jit(solution)/shard_map/ppermute | solution.py:350
  122.0 2.4 %collective-permute-start.32 = (bf16[4,128,128]{2,1,0:T(8,128)(2,1)S(1)}, bf16[4,128,128]{2,1,0:T(8,128)(2,1)S(1)}, u32[]{:S(2)}, u32[]{:S(2)}) collective-permute-start(bf16[4,128,128]{2,1,0:T(8,128)(2,1)S(1)} %get-tuple-element.256), channel_id=1, source_target_pairs={{0,96},{8,104},{16,112},{24,120},{32,64},{40,72},{48,80},{56,88},{... | collective-permute-start | bytes 393224 | tf_op jit(solution)/shard_map/ppermute | solution.py:350
  124.5 1.7 %finish.3 = (f32[32,128,128]{2,1,0:T(8,128)}, f32[8,128]{1,0:T(8,128)S(1)}) custom-call(s32[1]{0:T(128)} %bitcast.5.me_ref, s32[1]{0:T(128)S(6)} %copy.42.count_ref, s32[16,128]{1,0:T(8,128)S(1)} %get-tuple-element.487.refs_2_.table_ref, bf16[6,128,128]{2,1,0:T(8,128)(2,1)S(1)} %get-tuple-element.227.refs_0_, ...), custom_call_target="tpu_custom_call" | custom-call | tf_op jit(solution)/shard_map/finish/pallas_call | solution.py:326
  126.2 2.0 %collective-permute-done.32.refs_5_ = bf16[4,128,128]{2,1,0:T(8,128)(2,1)S(1)} collective-permute-done((bf16[4,128,128]{2,1,0:T(8,128)(2,1)S(1)}, bf16[4,128,128]{2,1,0:T(8,128)(2,1)S(1)}, u32[]{:S(2)}, u32[]{:S(2)}) %collective-permute-start.32) | collective-permute-done | bytes 131104 | tf_op jit(solution)/shard_map/ppermute | solution.py:350
  128.2 2.2 %finish.4 = (f32[32,128,128]{2,1,0:T(8,128)}, f32[8,128]{1,0:T(8,128)}) custom-call(s32[1]{0:T(128)} %bitcast.5.me_ref, s32[1]{0:T(128)S(6)} %copy.42.count_ref, s32[16,128]{1,0:T(8,128)S(1)} %get-tuple-element.487.refs_2_.table_ref, bf16[5,128,128]{2,1,0:T(8,128)(2,1)S(1)} %get-tuple-element.247.refs_0_, ...), custom_call_target="tpu_custom_call", output_to_operand_aliasing={{0}: (9, {})} | custom-call | tf_op jit(solution)/shard_map/finish/pallas_call | solution.py:326
  (78 shorter events, 24.3 us)
Async XLA Ops:
  3.5 15.4 %all-to-all-start = ((s32[8,1,128]{2,1,0:T(1,128)}), s32[8,1,128]{2,1,0:T(1,128)S(1)}, u32[]{:S(2)}, u32[]{:S(2)}) async-start(s32[8,1,128]{2,1,0:T(1,128)} %bitcast.3), calls=%async_computation | async-start | bytes 8192 | tf_op jit(solution)/shard_map/all_to_all | solution.py:370
  23.1 37.9 %all-to-all-start.1 = ((bf16[32,320,128]{2,1,0:T(8,128)(2,1)}), bf16[32,320,128]{2,1,0:T(8,128)(2,1)}, u32[]{:S(2)}, u32[]{:S(2)}) async-start(bf16[32,320,128]{2,1,0:T(8,128)(2,1)} %pack.1), calls=%async_computation.1 | async-start | bytes 5242880 | tf_op jit(solution)/shard_map/all_to_all | solution.py:372
  38.7 5.0 %collective-permute-start.12 = (bf16[48,128,128]{2,1,0:T(8,128)(2,1)S(1)}, bf16[48,128,128]{2,1,0:T(8,128)(2,1)S(1)}, u32[]{:S(2)}, u32[]{:S(2)}) collective-permute-start(bf16[48,128,128]{2,1,0:T(8,128)(2,1)S(1)} %tiles.18), channel_id=1, source_target_pairs={{0,8},{8,0},{16,24},{24,16},{32,40},{40,32},{48,56},{56,48},{64,72... | collective-permute-start | bytes 4718600 | tf_op jit(solution)/shard_map/ppermute | solution.py:350
  40.9 2.8 %copy-start.11 = (s32[8]{0:T(128)S(1)}, s32[8]{0:T(128)}, u32[]{:S(2)}) copy-start(s32[8]{0:T(128)} %constant.31.clone) | copy-start | bytes 100
  40.9 2.8 %copy-start.6 = (s32[8]{0:T(128)S(1)}, s32[8]{0:T(128)}, u32[]{:S(2)}) copy-start(s32[8]{0:T(128)} %constant.32.clone.refs_1_) | copy-start | bytes 100
  40.9 6.2 %collective-permute-start.13 = (bf16[48,128,128]{2,1,0:T(8,128)(2,1)S(1)}, bf16[48,128,128]{2,1,0:T(8,128)(2,1)S(1)}, u32[]{:S(2)}, u32[]{:S(2)}) collective-permute-start(bf16[48,128,128]{2,1,0:T(8,128)(2,1)S(1)} %tiles.19), channel_id=1, source_target_pairs={{0,8},{8,0},{16,24},{24,16},{32,40},{40,32},{48,56},{56,48},{64,72... | collective-permute-start | bytes 4718600 | tf_op jit(solution)/shard_map/ppermute | solution.py:350
  43.6 7.9 %collective-permute-start.14 = (bf16[48,128,128]{2,1,0:T(8,128)(2,1)S(1)}, bf16[48,128,128]{2,1,0:T(8,128)(2,1)S(1)}, u32[]{:S(2)}, u32[]{:S(2)}) collective-permute-start(bf16[48,128,128]{2,1,0:T(8,128)(2,1)S(1)} %tiles.20), channel_id=1, source_target_pairs={{0,8},{8,0},{16,24},{24,16},{32,40},{40,32},{48,56},{56,48},{64,72... | collective-permute-start | bytes 4718600 | tf_op jit(solution)/shard_map/ppermute | solution.py:350
  43.7 3.4 %copy-start.10 = (s32[8]{0:T(128)S(1)}, s32[8]{0:T(128)}, u32[]{:S(2)}) copy-start(s32[8]{0:T(128)} %constant.33.clone) | copy-start | bytes 100
  43.7 3.4 %copy-start.9 = (s32[8]{0:T(128)S(1)}, s32[8]{0:T(128)}, u32[]{:S(2)}) copy-start(s32[8]{0:T(128)} %constant.35.clone) | copy-start | bytes 100
  43.7 3.4 %copy-start.8 = (s32[8]{0:T(128)S(1)}, s32[8]{0:T(128)}, u32[]{:S(2)}) copy-start(s32[8]{0:T(128)} %constant.34.clone.refs_1_) | copy-start | bytes 100
  46.5 26.1 %collective-permute-start.15 = (bf16[24,128,128]{2,1,0:T(8,128)(2,1)}, bf16[24,128,128]{2,1,0:T(8,128)(2,1)}, u32[]{:S(2)}, u32[]{:S(2)}) collective-permute-start(bf16[24,128,128]{2,1,0:T(8,128)(2,1)} %get-tuple-element.211), channel_id=1, source_target_pairs={{0,16},{8,24},{16,0},{24,8},{32,48},{40,56},{48,32},{56,40},{64,80... | collective-permute-start | bytes 2359304 | tf_op jit(solution)/shard_map/ppermute | solution.py:350
  47.1 4.4 %copy-start.7 = (s32[8]{0:T(128)S(1)}, s32[8]{0:T(128)}, u32[]{:S(2)}) copy-start(s32[8]{0:T(128)} %constant.36.clone.refs_1_) | copy-start | bytes 100
  49.9 26.4 %collective-permute-start.16 = (bf16[24,128,128]{2,1,0:T(8,128)(2,1)}, bf16[24,128,128]{2,1,0:T(8,128)(2,1)}, u32[]{:S(2)}, u32[]{:S(2)}) collective-permute-start(bf16[24,128,128]{2,1,0:T(8,128)(2,1)} %get-tuple-element.215), channel_id=1, source_target_pairs={{0,32},{8,40},{16,48},{24,56},{32,0},{40,8},{48,16},{56,24},{64,96... | collective-permute-start | bytes 2359304 | tf_op jit(solution)/shard_map/ppermute | solution.py:350
  55.2 22.4 %collective-permute-start.17 = (bf16[24,128,128]{2,1,0:T(8,128)(2,1)}, bf16[24,128,128]{2,1,0:T(8,128)(2,1)S(1)}, u32[]{:S(2)}, u32[]{:S(2)}) collective-permute-start(bf16[24,128,128]{2,1,0:T(8,128)(2,1)} %get-tuple-element.218), channel_id=1, source_target_pairs={{0,96},{8,104},{16,112},{24,120},{32,64},{40,72},{48,80},{56,88},{... | collective-permute-start | bytes 2359304 | tf_op jit(solution)/shard_map/ppermute | solution.py:350
  72.4 11.1 %collective-permute-start.18 = (bf16[40,128,128]{2,1,0:T(8,128)(2,1)S(1)}, bf16[40,128,128]{2,1,0:T(8,128)(2,1)S(1)}, u32[]{:S(2)}, u32[]{:S(2)}) collective-permute-start(bf16[40,128,128]{2,1,0:T(8,128)(2,1)S(1)} %tiles.24), channel_id=1, source_target_pairs={{0,8},{8,0},{16,24},{24,16},{32,40},{40,32},{48,56},{56,48},{64,72... | collective-permute-start | bytes 3932168 | tf_op jit(solution)/shard_map/ppermute | solution.py:350
  75.8 11.0 %collective-permute-start.19 = (bf16[40,128,128]{2,1,0:T(8,128)(2,1)S(1)}, bf16[40,128,128]{2,1,0:T(8,128)(2,1)S(1)}, u32[]{:S(2)}, u32[]{:S(2)}) collective-permute-start(bf16[40,128,128]{2,1,0:T(8,128)(2,1)S(1)} %tiles.25), channel_id=1, source_target_pairs={{0,8},{8,0},{16,24},{24,16},{32,40},{40,32},{48,56},{56,48},{64,72... | collective-permute-start | bytes 3932168 | tf_op jit(solution)/shard_map/ppermute | solution.py:350
  79.6 15.5 %collective-permute-start.23 = (bf16[32,128,128]{2,1,0:T(8,128)(2,1)S(1)}, bf16[32,128,128]{2,1,0:T(8,128)(2,1)S(1)}, u32[]{:S(2)}, u32[]{:S(2)}) collective-permute-start(bf16[32,128,128]{2,1,0:T(8,128)(2,1)S(1)} %tiles.26), channel_id=1, source_target_pairs={{0,8},{8,0},{16,24},{24,16},{32,40},{40,32},{48,56},{56,48},{64,72... | collective-permute-start | bytes 3145736 | tf_op jit(solution)/shard_map/ppermute | solution.py:350
  79.8 11.9 %collective-permute-start.20 = (bf16[12,128,128]{2,1,0:T(8,128)(2,1)S(1)}, bf16[12,128,128]{2,1,0:T(8,128)(2,1)S(1)}, u32[]{:S(2)}, u32[]{:S(2)}) collective-permute-start(bf16[12,128,128]{2,1,0:T(8,128)(2,1)S(1)} %get-tuple-element.226), channel_id=1, source_target_pairs={{0,32},{8,40},{16,48},{24,56},{32,0},{40,8},{48,16},{56,24},{64,96... | collective-permute-start | bytes 1179656 | tf_op jit(solution)/shard_map/ppermute | solution.py:350
  81.3 13.5 %collective-permute-start.21 = (bf16[12,128,128]{2,1,0:T(8,128)(2,1)S(1)}, bf16[12,128,128]{2,1,0:T(8,128)(2,1)S(1)}, u32[]{:S(2)}, u32[]{:S(2)}) collective-permute-start(bf16[12,128,128]{2,1,0:T(8,128)(2,1)S(1)} %get-tuple-element.229), channel_id=1, source_target_pairs={{0,96},{8,104},{16,112},{24,120},{32,64},{40,72},{48,80},{56,88},{... | collective-permute-start | bytes 1179656 | tf_op jit(solution)/shard_map/ppermute | solution.py:350
  83.5 11.4 %collective-permute-start.22 = (bf16[12,128,128]{2,1,0:T(8,128)(2,1)S(1)}, bf16[12,128,128]{2,1,0:T(8,128)(2,1)S(1)}, u32[]{:S(2)}, u32[]{:S(2)}) collective-permute-start(bf16[12,128,128]{2,1,0:T(8,128)(2,1)S(1)} %get-tuple-element.232), channel_id=1, source_target_pairs={{0,16},{8,24},{16,0},{24,8},{32,48},{40,56},{48,32},{56,40},{64,80... | collective-permute-start | bytes 1179656 | tf_op jit(solution)/shard_map/ppermute | solution.py:350
  86.8 18.4 %collective-permute-start.24 = (bf16[20,128,128]{2,1,0:T(8,128)(2,1)S(1)}, bf16[20,128,128]{2,1,0:T(8,128)(2,1)S(1)}, u32[]{:S(2)}, u32[]{:S(2)}) collective-permute-start(bf16[20,128,128]{2,1,0:T(8,128)(2,1)S(1)} %get-tuple-element.237), channel_id=1, source_target_pairs={{0,32},{8,40},{16,48},{24,56},{32,0},{40,8},{48,16},{56,24},{64,96... | collective-permute-start | bytes 1966088 | tf_op jit(solution)/shard_map/ppermute | solution.py:350
  91.7 16.9 %collective-permute-start.25 = (bf16[20,128,128]{2,1,0:T(8,128)(2,1)S(1)}, bf16[20,128,128]{2,1,0:T(8,128)(2,1)S(1)}, u32[]{:S(2)}, u32[]{:S(2)}) collective-permute-start(bf16[20,128,128]{2,1,0:T(8,128)(2,1)S(1)} %get-tuple-element.240), channel_id=1, source_target_pairs={{0,96},{8,104},{16,112},{24,120},{32,64},{40,72},{48,80},{56,88},{... | collective-permute-start | bytes 1966088 | tf_op jit(solution)/shard_map/ppermute | solution.py:350
  96.8 13.1 %collective-permute-start.26 = (bf16[16,128,128]{2,1,0:T(8,128)(2,1)S(1)}, bf16[16,128,128]{2,1,0:T(8,128)(2,1)S(1)}, u32[]{:S(2)}, u32[]{:S(2)}) collective-permute-start(bf16[16,128,128]{2,1,0:T(8,128)(2,1)S(1)} %get-tuple-element.243), channel_id=1, source_target_pairs={{0,16},{8,24},{16,0},{24,8},{32,48},{40,56},{48,32},{56,40},{64,80... | collective-permute-start | bytes 1572872 | tf_op jit(solution)/shard_map/ppermute | solution.py:350
  105.4 10.5 %collective-permute-start.27 = (bf16[10,128,128]{2,1,0:T(8,128)(2,1)S(1)}, bf16[10,128,128]{2,1,0:T(8,128)(2,1)S(1)}, u32[]{:S(2)}, u32[]{:S(2)}) collective-permute-start(bf16[10,128,128]{2,1,0:T(8,128)(2,1)S(1)} %get-tuple-element.246), channel_id=1, source_target_pairs={{0,96},{8,104},{16,112},{24,120},{32,64},{40,72},{48,80},{56,88},{... | collective-permute-start | bytes 983048 | tf_op jit(solution)/shard_map/ppermute | solution.py:350
  108.8 10.7 %collective-permute-start.29 = (bf16[10,128,128]{2,1,0:T(8,128)(2,1)S(1)}, bf16[10,128,128]{2,1,0:T(8,128)(2,1)S(1)}, u32[]{:S(2)}, u32[]{:S(2)}) collective-permute-start(bf16[10,128,128]{2,1,0:T(8,128)(2,1)S(1)} %get-tuple-element.250), channel_id=1, source_target_pairs={{0,16},{8,24},{16,0},{24,8},{32,48},{40,56},{48,32},{56,40},{64,80... | collective-permute-start | bytes 983048 | tf_op jit(solution)/shard_map/ppermute | solution.py:350
  110.0 10.7 %collective-permute-start.31 = (bf16[8,128,128]{2,1,0:T(8,128)(2,1)S(1)}, bf16[8,128,128]{2,1,0:T(8,128)(2,1)S(1)}, u32[]{:S(2)}, u32[]{:S(2)}) collective-permute-start(bf16[8,128,128]{2,1,0:T(8,128)(2,1)S(1)} %get-tuple-element.254), channel_id=1, source_target_pairs={{0,32},{8,40},{16,48},{24,56},{32,0},{40,8},{48,16},{56,24},{64,96... | collective-permute-start | bytes 786440 | tf_op jit(solution)/shard_map/ppermute | solution.py:350
  110.2 11.8 %collective-permute-start.35 = (bf16[6,128,128]{2,1,0:T(8,128)(2,1)S(1)}, bf16[6,128,128]{2,1,0:T(8,128)(2,1)S(1)}, u32[]{:S(2)}, u32[]{:S(2)}) collective-permute-start(bf16[6,128,128]{2,1,0:T(8,128)(2,1)S(1)} %get-tuple-element.260), channel_id=1, source_target_pairs={{0,32},{8,40},{16,48},{24,56},{32,0},{40,8},{48,16},{56,24},{64,96... | collective-permute-start | bytes 589832 | tf_op jit(solution)/shard_map/ppermute | solution.py:350
  112.1 12.4 %collective-permute-start.34 = (bf16[6,128,128]{2,1,0:T(8,128)(2,1)S(1)}, bf16[6,128,128]{2,1,0:T(8,128)(2,1)S(1)}, u32[]{:S(2)}, u32[]{:S(2)}) collective-permute-start(bf16[6,128,128]{2,1,0:T(8,128)(2,1)S(1)} %get-tuple-element.259), channel_id=1, source_target_pairs={{0,16},{8,24},{16,0},{24,8},{32,48},{40,56},{48,32},{56,40},{64,80... | collective-permute-start | bytes 589832 | tf_op jit(solution)/shard_map/ppermute | solution.py:350
  115.9 8.6 %collective-permute-start.33 = (bf16[6,128,128]{2,1,0:T(8,128)(2,1)S(1)}, bf16[6,128,128]{2,1,0:T(8,128)(2,1)S(1)}, u32[]{:S(2)}, u32[]{:S(2)}) collective-permute-start(bf16[6,128,128]{2,1,0:T(8,128)(2,1)S(1)} %get-tuple-element.258), channel_id=1, source_target_pairs={{0,96},{8,104},{16,112},{24,120},{32,64},{40,72},{48,80},{56,88},{... | collective-permute-start | bytes 589832 | tf_op jit(solution)/shard_map/ppermute | solution.py:350
  119.6 6.6 %collective-permute-start.28 = (bf16[5,128,128]{2,1,0:T(8,128)(2,1)S(1)}, bf16[5,128,128]{2,1,0:T(8,128)(2,1)S(1)}, u32[]{:S(2)}, u32[]{:S(2)}) collective-permute-start(bf16[5,128,128]{2,1,0:T(8,128)(2,1)S(1)} %get-tuple-element.248), channel_id=1, source_target_pairs={{0,16},{8,24},{16,0},{24,8},{32,48},{40,56},{48,32},{56,40},{64,80... | collective-permute-start | bytes 491528 | tf_op jit(solution)/shard_map/ppermute | solution.py:350
  120.7 7.5 %collective-permute-start.30 = (bf16[5,128,128]{2,1,0:T(8,128)(2,1)S(1)}, bf16[5,128,128]{2,1,0:T(8,128)(2,1)S(1)}, u32[]{:S(2)}, u32[]{:S(2)}) collective-permute-start(bf16[5,128,128]{2,1,0:T(8,128)(2,1)S(1)} %get-tuple-element.252), channel_id=1, source_target_pairs={{0,32},{8,40},{16,48},{24,56},{32,0},{40,8},{48,16},{56,24},{64,96... | collective-permute-start | bytes 491528 | tf_op jit(solution)/shard_map/ppermute | solution.py:350
  122.0 6.2 %collective-permute-start.32 = (bf16[4,128,128]{2,1,0:T(8,128)(2,1)S(1)}, bf16[4,128,128]{2,1,0:T(8,128)(2,1)S(1)}, u32[]{:S(2)}, u32[]{:S(2)}) collective-permute-start(bf16[4,128,128]{2,1,0:T(8,128)(2,1)S(1)} %get-tuple-element.256), channel_id=1, source_target_pairs={{0,96},{8,104},{16,112},{24,120},{32,64},{40,72},{48,80},{56,88},{... | collective-permute-start | bytes 393224 | tf_op jit(solution)/shard_map/ppermute | solution.py:350
  (3 other events, 3.4 us)

commit v6 on v5

--- a/solution.py
+++ b/solution.py
@@ -101,6 +101,7 @@
 
 STEP = 16
 DEPTH = 3
+PARTS = 2
 
 
 def prep_kernel(with_far, weights_ref, adj_ref, em_ref, *refs):
@@ -111,19 +112,25 @@
     steps = adj_ref.shape[0]
     blocks = wt_ref.shape[0]
     chunks = blocks // STEP
+    part = STEP // PARTS * BLK
+
+    def copies(j, h):
+        slot = lax.rem(j, DEPTH)
+        cols = pl.ds(pl.multiple_of(j * (STEP * BLK) + h * part, part), part)
+        here = pl.ds(h * part, part)
+        return (
+            pltpu.make_async_copy(adj_ref.at[:, cols], abuf.at[slot, :, here], asem.at[slot, h]),
+            pltpu.make_async_copy(em_ref.at[:, cols], ebuf.at[slot, :, here], esem.at[slot, h]),
+        )
+
+    def start(j):
+        for h in range(PARTS):
+            for copy in copies(j, h):
+                copy.start()
+
+    for j in range(DEPTH - 1):
+        start(j)
     wide[...] = jnp.broadcast_to(weights_ref[...], wide.shape)
-
-    def copies(j):
-        slot = lax.rem(j, DEPTH)
-        cols = pl.ds(pl.multiple_of(j * (STEP * BLK), STEP * BLK), STEP * BLK)
-        return (
-            pltpu.make_async_copy(adj_ref.at[:, cols], abuf.at[slot], asem.at[slot]),
-            pltpu.make_async_copy(em_ref.at[:, cols], ebuf.at[slot], esem.at[slot]),
-        )
-
-    for j in range(DEPTH - 1):
-        for copy in copies(j):
-            copy.start()
     if with_far:
         rest = pl.ds(blocks, e_ref.shape[0] - blocks)
         far_copy = pltpu.make_async_copy(far_ref, e_ref.at[rest, pl.ds(0, steps)], fsem)
@@ -136,12 +143,12 @@
 
         @pl.when(j + DEPTH - 1 < chunks)
         def _():
-            for copy in copies(j + DEPTH - 1):
-                copy.start()
-
-        for copy in copies(j):
-            copy.wait()
+            start(j + DEPTH - 1)
+
         for b in range(STEP):
+            if b % (STEP // PARTS) == 0:
+                for copy in copies(j, b // (STEP // PARTS)):
+                    copy.wait()
             at = j * STEP + b
             w = (wide[...] * abuf[slot, :, b * BLK : (b + 1) * BLK].astype(F32)).astype(BF16)
             e = ebuf[slot, :, b * BLK : (b + 1) * BLK]
@@ -180,8 +187,8 @@
             pltpu.VMEM((DEPTH, steps, STEP * BLK), BF16),
             pltpu.VMEM((DEPTH, steps, STEP * BLK), BF16),
             pltpu.VMEM((steps, BLK), F32),
-            pltpu.SemaphoreType.DMA((DEPTH,)),
-            pltpu.SemaphoreType.DMA((DEPTH,)),
+            pltpu.SemaphoreType.DMA((DEPTH, PARTS)),
+            pltpu.SemaphoreType.DMA((DEPTH, PARTS)),
         ]
         + ([pltpu.SemaphoreType.DMA] if with_far else []),
         compiler_params=pltpu.CompilerParams(vmem_limit_bytes=14 * 2**20),
@@ -255,16 +262,16 @@
         n += size
 
 
-def tiles(groups, places, table, wt, e_blocks, first, per, outs, rolled, add=None):
+def tiles(groups, places, table, wt, e_blocks, first, per, outs, rolled, add=None, to_hbm=False):
     smem = pl.BlockSpec(memory_space=pltpu.SMEM)
     vmem = pl.BlockSpec(memory_space=pltpu.VMEM)
-    count = groups.shape[0] * per
+    shape = (groups.shape[0] * per // outs, BLK, BLK)
     with_add = add is not None
     return pl.pallas_call(
         functools.partial(tiles_kernel, first, per, with_add, rolled),
         in_specs=[smem, smem, smem, vmem, vmem] + ([vmem] if with_add else []),
         out_specs=[vmem] * outs,
-        out_shape=[jax.ShapeDtypeStruct((count // outs, BLK, BLK), BF16)] * outs,
+        out_shape=[(pltpu.HBM if to_hbm else jax.ShapeDtypeStruct)(shape, BF16)] * outs,
         compiler_params=pltpu.CompilerParams(vmem_limit_bytes=10 * 2**20),
         name="tiles",
     )(groups, places, table, wt, e_blocks, *([add] if with_add else []))
@@ -386,7 +393,7 @@
         mine = me ^ jnp.array(masks, I32)
         places = jnp.array([m // 2 for m in masks], I32)
         return tiles(
-            after(mine, last), places, table, wt, e_blocks, offsets[c][i], cuts[c][i], 2, rolled, core
+            after(mine, last), places, table, wt, e_blocks, offsets[c][i], cuts[c][i], 2, rolled, core, c == 0
         )
 
     def exchange(c, outs, step):

time: 132 us -> 131 us (level)
  Pallas kernels: 57.9 us -> 56.5 us
    pallas_call x12, Pallas kernels: 3.86 us -> 1.59 us  [add_pairs(): pl.pallas_call(functools.partial(add_kernel, len(pairs)), in_specs=[vmem]...]
  transfers between devices with their start and end apart: 26 -> 26, of which waited for: 10 -> 11; matrix products, arithmetic and copies ran while one was open for 1% -> 1% of each run, Pallas kernels for 38% -> 37%
where the time goes in v6:
time: 131 us; the launch traced here: 130 us
  Pallas kernels  56.5 us (43%)
  starting transfers between devices  42.9 us (33%)
  waiting for transfers between devices  25.9 us (20%)
  local copies, waits for them, and re-layouts  1.82 us (1%)
    ppermute x24, starting transfers between devices, swap(): return lax.ppermute(a, 'tm', [(i, i ^ mask) for i in range(n)])  30.6 us
    pallas_call x12, Pallas kernels, tiles(): pl.pallas_call(functools.partial(tiles_kernel, first, per, with_add, roll...  26.5 us
    pallas_call x2, Pallas kernels, prep(): pl.pallas_call(functools.partial(prep_kernel, with_far), in_specs=[vmem]...  18.2 us
    ppermute x24, waiting for transfers between devices, swap(): return lax.ppermute(a, 'tm', [(i, i ^ mask) for i in range(n)])  15.6 us
    all_to_all x1, starting transfers between devices, body(): lax.all_to_all(request, 'tile', split_axis=0, concat_axis=0, tiled=True)  7.86 us
    all_to_all x1, waiting for transfers between devices, body(): lax.all_to_all(request, 'tile', split_axis=0, concat_axis=0, tiled=True)  6.9 us
    all_to_all x1, starting transfers between devices, body(): lax.all_to_all(outgoing, 'tile', split_axis=0, concat_axis=0, tiled=True)  4.41 us
    pallas_call x1, Pallas kernels, pack(): pl.pallas_call(pack_kernel, in_specs=[pl.BlockSpec(memory_space=pltpu.SME...  4.15 us
  transfers between devices with their start and end apart: 26, of which 11 were waited for; matrix products, arithmetic and copies ran while one was open for 1% of the time, Pallas kernels for 37%

profile of v6, /device:TPU:0, one launch (start us, length us, event | category | flops | bytes accessed | tf_op | source)
XLA Modules:
  0.0 129.8 jit_solution(8138471062518359029)
XLA Ops:
  1.3 2.2 %plan.1 = (s32[8,128]{1,0:T(8,128)}, s32[16,128]{1,0:T(8,128)S(1)}) custom-call(s32[1]{0:T(128)} %bitcast.own_ref, s32[1]{0:T(128)S(6)} %copy.42.count_ref, s32[2,512]{1,0:T(2,128)S(1)} %bitcast.12), custom_call_target="tpu_custom_call" | custom-call | tf_op jit(solution)/shard_map/plan/pallas_call | solution.py:89
  3.5 7.9 %all-to-all-start = ((s32[8,1,128]{2,1,0:T(1,128)}), s32[8,1,128]{2,1,0:T(1,128)S(1)}, u32[]{:S(2)}, u32[]{:S(2)}) async-start(s32[8,1,128]{2,1,0:T(1,128)} %bitcast.3), calls=%async_computation | async-start | bytes 8192 | tf_op jit(solution)/shard_map/all_to_all | solution.py:377
  12.1 6.9 %all-to-all-done = s32[8,1,128]{2,1,0:T(1,128)S(1)} async-done(((s32[8,1,128]{2,1,0:T(1,128)}), s32[8,1,128]{2,1,0:T(1,128)S(1)}, u32[]{:S(2)}, u32[]{:S(2)}) %all-to-all-start) | async-done | bytes 4128 | tf_op jit(solution)/shard_map/all_to_all | solution.py:377
  19.0 4.1 %pack.1 = bf16[32,320,128]{2,1,0:T(8,128)(2,1)} custom-call(s32[1]{0:T(128)} %bitcast.own_ref, s32[8,128]{1,0:T(8,128)S(1)} %bitcast.10, bf16[320,16384]{1,0:T(8,128)(2,1)} %em_ref.5), custom_call_target="tpu_custom_call" | custom-call | tf_op jit(solution)/shard_map/pack/pallas_call | solution.py:226
  23.1 4.4 %all-to-all-start.1 = ((bf16[32,320,128]{2,1,0:T(8,128)(2,1)}), bf16[32,320,128]{2,1,0:T(8,128)(2,1)}, u32[]{:S(2)}, u32[]{:S(2)}) async-start(bf16[32,320,128]{2,1,0:T(8,128)(2,1)} %pack.1), calls=%async_computation.1 | async-start | bytes 5242880 | tf_op jit(solution)/shard_map/all_to_all | solution.py:379
  27.7 8.9 %prep.3 = (bf16[128,128,384]{2,1,0:T(8,128)(2,1)S(1)}, bf16[128,384,128]{2,1,0:T(8,128)(2,1)S(1)}) custom-call(f32[320,1]{1,0:T(8,128)S(1)} %copy.30.weights_ref, bf16[320,16384]{1,0:T(8,128)(2,1)} %adj_ref.3, bf16[320,16384]{1,0:T(8,128)(2,1)} %em_ref.5), custom_call_target="tpu_custom_call" | custom-call | tf_op jit(solution)/shard_map/prep/pallas_call | solution.py:178
  36.6 2.1 %tiles.18 = bf16[48,128,128]{2,1,0:T(8,128)(2,1)S(1)} custom-call(s32[8]{0:T(128)S(1)} %multiply_xor_fusion.1.refs_0_.refs_1_, s32[8]{0:T(128)S(1)} %multiply_xor_fusion.1.refs_0_.refs_1_, s32[16,128]{1,0:T(8,128)S(1)} %get-tuple-element.487.refs_2_.table_ref, bf16[128,128,384]{2,1,0:T(8,128)(2,1)S(1)} %get-tuple-element.195.refs_3_, ...), custom_call_target="tpu_custom_call" | custom-call | tf_op jit(solution)/shard_map/tiles/pallas_call | solution.py:270
  38.7 2.1 %tiles.19 = bf16[48,128,128]{2,1,0:T(8,128)(2,1)S(1)} custom-call(s32[8]{0:T(128)S(1)} %multiply_xor_fusion.1.refs_0_.refs_1_, s32[8]{0:T(128)S(1)} %multiply_xor_fusion.1.refs_0_.refs_1_, s32[16,128]{1,0:T(8,128)S(1)} %get-tuple-element.487.refs_2_.table_ref, bf16[128,128,384]{2,1,0:T(8,128)(2,1)S(1)} %get-tuple-element.195.refs_3_, ...), custom_call_target="tpu_custom_call" | custom-call | tf_op jit(solution)/shard_map/tiles/pallas_call | solution.py:270
  41.4 2.1 %tiles.20 = bf16[48,128,128]{2,1,0:T(8,128)(2,1)S(1)} custom-call(s32[8]{0:T(128)S(1)} %multiply_xor_fusion.1.refs_0_.refs_1_, s32[8]{0:T(128)S(1)} %multiply_xor_fusion.1.refs_0_.refs_1_, s32[16,128]{1,0:T(8,128)S(1)} %get-tuple-element.487.refs_2_.table_ref, bf16[128,128,384]{2,1,0:T(8,128)(2,1)S(1)} %get-tuple-element.195.refs_3_, ...), custom_call_target="tpu_custom_call" | custom-call | tf_op jit(solution)/shard_map/tiles/pallas_call | solution.py:270
  43.7 3.1 %tiles.21 = (bf16[24,128,128]{2,1,0:T(8,128)(2,1)}, bf16[24,128,128]{2,1,0:T(8,128)(2,1)}) custom-call(s32[8]{0:T(128)S(1)} %broadcast_xor_fusion.3.refs_0_, s32[8]{0:T(128)S(1)} %copy-done.10, s32[16,128]{1,0:T(8,128)S(1)} %get-tuple-element.487.refs_2_.table_ref, bf16[128,128,384]{2,1,0:T(8,128)(2,1)S(1)} %get-tuple-element.195.refs_3_, ...), custom_call_target="tpu_custom_call" | custom-call | tf_op jit(solution)/shard_map/tiles/pallas_call | solution.py:270
  47.4 3.2 %tiles.22 = (bf16[24,128,128]{2,1,0:T(8,128)(2,1)}, bf16[24,128,128]{2,1,0:T(8,128)(2,1)}) custom-call(s32[8]{0:T(128)S(1)} %broadcast_xor_fusion.5.refs_0_, s32[8]{0:T(128)S(1)} %copy-done.12, s32[16,128]{1,0:T(8,128)S(1)} %get-tuple-element.487.refs_2_.table_ref, bf16[128,128,384]{2,1,0:T(8,128)(2,1)S(1)} %get-tuple-element.195.refs_3_, ...), custom_call_target="tpu_custom_call" | custom-call | tf_op jit(solution)/shard_map/tiles/pallas_call | solution.py:270
  52.2 3.1 %tiles.23 = (bf16[24,128,128]{2,1,0:T(8,128)(2,1)}, bf16[24,128,128]{2,1,0:T(8,128)(2,1)}) custom-call(s32[8]{0:T(128)S(1)} %broadcast_xor_fusion.4.refs_0_, s32[8]{0:T(128)S(1)} %copy-done.11, s32[16,128]{1,0:T(8,128)S(1)} %get-tuple-element.487.refs_2_.table_ref, bf16[128,128,384]{2,1,0:T(8,128)(2,1)S(1)} %get-tuple-element.195.refs_3_, ...), custom_call_target="tpu_custom_call" | custom-call | tf_op jit(solution)/shard_map/tiles/pallas_call | solution.py:270
  55.3 2.2 %collective-permute-start.17 = (bf16[24,128,128]{2,1,0:T(8,128)(2,1)}, bf16[24,128,128]{2,1,0:T(8,128)(2,1)S(1)}, u32[]{:S(2)}, u32[]{:S(2)}) collective-permute-start(bf16[24,128,128]{2,1,0:T(8,128)(2,1)} %get-tuple-element.218), channel_id=1, source_target_pairs={{0,96},{8,104},{16,112},{24,120},{32,64},{40,72},{48,80},{56,88},{... | collective-permute-start | bytes 2359304 | tf_op jit(solution)/shard_map/ppermute | solution.py:357
  57.6 3.4 %all-to-all-done.1.refs_0_ = bf16[32,320,128]{2,1,0:T(8,128)(2,1)} async-done(((bf16[32,320,128]{2,1,0:T(8,128)(2,1)}), bf16[32,320,128]{2,1,0:T(8,128)(2,1)}, u32[]{:S(2)}, u32[]{:S(2)}) %all-to-all-start.1) | async-done | bytes 2621472 | tf_op jit(solution)/shard_map/all_to_all | solution.py:379
  61.0 9.4 %prep.4 = (bf16[128,128,384]{2,1,0:T(8,128)(2,1)S(1)}, bf16[160,384,128]{2,1,0:T(8,128)(2,1)S(1)}) custom-call(f32[320,1]{1,0:T(8,128)S(1)} %copy.31.weights_ref, bf16[320,16384]{1,0:T(8,128)(2,1)} %adj_ref.3, bf16[320,16384]{1,0:T(8,128)(2,1)} %em_ref.5, bf16[32,320,128]{2,1,0:T(8,128)(2,1)} %all-to-all-done.1.refs_0_), custom_call_target="tpu_custom_call" | custom-call | tf_op jit(solution)/shard_map/prep/pallas_call | solution.py:178
  70.4 1.9 %tiles.24 = bf16[40,128,128]{2,1,0:T(8,128)(2,1)S(1)} custom-call(s32[8]{0:T(128)S(1)} %multiply_xor_fusion.1.refs_0_.refs_1_, s32[8]{0:T(128)S(1)} %multiply_xor_fusion.1.refs_0_.refs_1_, s32[16,128]{1,0:T(8,128)S(1)} %get-tuple-element.487.refs_2_.table_ref, bf16[128,128,384]{2,1,0:T(8,128)(2,1)S(1)} %get-tuple-element.207.refs_3_, ...), custom_call_target="tpu_custom_call" | custom-call | tf_op jit(solution)/shard_map/tiles/pallas_call | solution.py:270
  72.7 1.9 %tiles.25 = bf16[40,128,128]{2,1,0:T(8,128)(2,1)S(1)} custom-call(s32[8]{0:T(128)S(1)} %multiply_xor_fusion.1.refs_0_.refs_1_, s32[8]{0:T(128)S(1)} %multiply_xor_fusion.1.refs_0_.refs_1_, s32[16,128]{1,0:T(8,128)S(1)} %get-tuple-element.487.refs_2_.table_ref, bf16[128,128,384]{2,1,0:T(8,128)(2,1)S(1)} %get-tuple-element.207.refs_3_, ...), custom_call_target="tpu_custom_call" | custom-call | tf_op jit(solution)/shard_map/tiles/pallas_call | solution.py:270
  79.7 2.2 %collective-permute-start.21 = (bf16[12,128,128]{2,1,0:T(8,128)(2,1)S(1)}, bf16[12,128,128]{2,1,0:T(8,128)(2,1)S(1)}, u32[]{:S(2)}, u32[]{:S(2)}) collective-permute-start(bf16[12,128,128]{2,1,0:T(8,128)(2,1)S(1)} %get-tuple-element.229), channel_id=1, source_target_pairs={{0,96},{8,104},{16,112},{24,120},{32,64},{40,72},{48,80},{56,88},{... | collective-permute-start | bytes 1179656 | tf_op jit(solution)/shard_map/ppermute | solution.py:357
  83.0 1.9 %tiles.27 = (bf16[20,128,128]{2,1,0:T(8,128)(2,1)S(1)}, bf16[20,128,128]{2,1,0:T(8,128)(2,1)S(1)}) custom-call(s32[8]{0:T(128)S(1)} %broadcast_xor_fusion.5.refs_0_, s32[8]{0:T(128)S(1)} %copy-done.12, s32[16,128]{1,0:T(8,128)S(1)} %get-tuple-element.487.refs_2_.table_ref, bf16[128,128,384]{2,1,0:T(8,128)(2,1)S(1)} %get-tuple-element.207.refs_3_, ...), custom_call_target="tpu_custom_call" | custom-call | tf_op jit(solution)/shard_map/tiles/pallas_call | solution.py:270
  85.6 1.9 %tiles.28 = (bf16[20,128,128]{2,1,0:T(8,128)(2,1)S(1)}, bf16[20,128,128]{2,1,0:T(8,128)(2,1)S(1)}) custom-call(s32[8]{0:T(128)S(1)} %broadcast_xor_fusion.4.refs_0_, s32[8]{0:T(128)S(1)} %copy-done.11, s32[16,128]{1,0:T(8,128)S(1)} %get-tuple-element.487.refs_2_.table_ref, bf16[128,128,384]{2,1,0:T(8,128)(2,1)S(1)} %get-tuple-element.207.refs_3_, ...), custom_call_target="tpu_custom_call" | custom-call | tf_op jit(solution)/shard_map/tiles/pallas_call | solution.py:270
  87.5 2.5 %collective-permute-done.20.refs_1_ = bf16[12,128,128]{2,1,0:T(8,128)(2,1)S(1)} collective-permute-done((bf16[12,128,128]{2,1,0:T(8,128)(2,1)S(1)}, bf16[12,128,128]{2,1,0:T(8,128)(2,1)S(1)}, u32[]{:S(2)}, u32[]{:S(2)}) %collective-permute-start.20) | collective-permute-done | bytes 393248 | tf_op jit(solution)/shard_map/ppermute | solution.py:357
  90.0 3.0 %collective-permute-start.25 = (bf16[20,128,128]{2,1,0:T(8,128)(2,1)S(1)}, bf16[20,128,128]{2,1,0:T(8,128)(2,1)S(1)}, u32[]{:S(2)}, u32[]{:S(2)}) collective-permute-start(bf16[20,128,128]{2,1,0:T(8,128)(2,1)S(1)} %get-tuple-element.240), channel_id=1, source_target_pairs={{0,96},{8,104},{16,112},{24,120},{32,64},{40,72},{48,80},{56,88},{... | collective-permute-start | bytes 1966088 | tf_op jit(solution)/shard_map/ppermute | solution.py:357
  93.4 1.7 %tiles.29 = (bf16[16,128,128]{2,1,0:T(8,128)(2,1)S(1)}, bf16[16,128,128]{2,1,0:T(8,128)(2,1)S(1)}) custom-call(s32[8]{0:T(128)S(1)} %broadcast_xor_fusion.3.refs_0_, s32[8]{0:T(128)S(1)} %copy-done.10, s32[16,128]{1,0:T(8,128)S(1)} %get-tuple-element.487.refs_2_.table_ref, bf16[128,128,384]{2,1,0:T(8,128)(2,1)S(1)} %get-tuple-element.207.refs_3_, ...), custom_call_target="tpu_custom_call" | custom-call | tf_op jit(solution)/shard_map/tiles/pallas_call | solution.py:270
  97.3 6.3 %collective-permute-done.24.refs_1_ = bf16[20,128,128]{2,1,0:T(8,128)(2,1)S(1)} collective-permute-done((bf16[20,128,128]{2,1,0:T(8,128)(2,1)S(1)}, bf16[20,128,128]{2,1,0:T(8,128)(2,1)S(1)}, u32[]{:S(2)}, u32[]{:S(2)}) %collective-permute-start.24) | collective-permute-done | bytes 655392 | tf_op jit(solution)/shard_map/ppermute | solution.py:357
  103.8 2.8 %collective-permute-start.27 = (bf16[10,128,128]{2,1,0:T(8,128)(2,1)S(1)}, bf16[10,128,128]{2,1,0:T(8,128)(2,1)S(1)}, u32[]{:S(2)}, u32[]{:S(2)}) collective-permute-start(bf16[10,128,128]{2,1,0:T(8,128)(2,1)S(1)} %get-tuple-element.246), channel_id=1, source_target_pairs={{0,96},{8,104},{16,112},{24,120},{32,64},{40,72},{48,80},{56,88},{... | collective-permute-start | bytes 983048 | tf_op jit(solution)/shard_map/ppermute | solution.py:357
  109.0 2.0 %collective-permute-start.35 = (bf16[6,128,128]{2,1,0:T(8,128)(2,1)S(1)}, bf16[6,128,128]{2,1,0:T(8,128)(2,1)S(1)}, u32[]{:S(2)}, u32[]{:S(2)}) collective-permute-start(bf16[6,128,128]{2,1,0:T(8,128)(2,1)S(1)} %get-tuple-element.260), channel_id=1, source_target_pairs={{0,32},{8,40},{16,48},{24,56},{32,0},{40,8},{48,16},{56,24},{64,96... | collective-permute-start | bytes 589832 | tf_op jit(solution)/shard_map/ppermute | solution.py:357
  111.6 2.7 %collective-permute-done.27.refs_1_ = bf16[10,128,128]{2,1,0:T(8,128)(2,1)S(1)} collective-permute-done((bf16[10,128,128]{2,1,0:T(8,128)(2,1)S(1)}, bf16[10,128,128]{2,1,0:T(8,128)(2,1)S(1)}, u32[]{:S(2)}, u32[]{:S(2)}) %collective-permute-start.27) | collective-permute-done | bytes 327712 | tf_op jit(solution)/shard_map/ppermute | solution.py:357
  114.3 2.4 %collective-permute-start.33 = (bf16[6,128,128]{2,1,0:T(8,128)(2,1)S(1)}, bf16[6,128,128]{2,1,0:T(8,128)(2,1)S(1)}, u32[]{:S(2)}, u32[]{:S(2)}) collective-permute-start(bf16[6,128,128]{2,1,0:T(8,128)(2,1)S(1)} %get-tuple-element.258), channel_id=1, source_target_pairs={{0,96},{8,104},{16,112},{24,120},{32,64},{40,72},{48,80},{56,88},{... | collective-permute-start | bytes 589832 | tf_op jit(solution)/shard_map/ppermute | solution.py:357
  117.7 1.8 %collective-permute-start.28 = (bf16[5,128,128]{2,1,0:T(8,128)(2,1)S(1)}, bf16[5,128,128]{2,1,0:T(8,128)(2,1)S(1)}, u32[]{:S(2)}, u32[]{:S(2)}) collective-permute-start(bf16[5,128,128]{2,1,0:T(8,128)(2,1)S(1)} %get-tuple-element.248), channel_id=1, source_target_pairs={{0,16},{8,24},{16,0},{24,8},{32,48},{40,56},{48,32},{56,40},{64,80... | collective-permute-start | bytes 491528 | tf_op jit(solution)/shard_map/ppermute | solution.py:357
  120.4 3.4 %collective-permute-start.32 = (bf16[4,128,128]{2,1,0:T(8,128)(2,1)S(1)}, bf16[4,128,128]{2,1,0:T(8,128)(2,1)S(1)}, u32[]{:S(2)}, u32[]{:S(2)}) collective-permute-start(bf16[4,128,128]{2,1,0:T(8,128)(2,1)S(1)} %get-tuple-element.256), channel_id=1, source_target_pairs={{0,96},{8,104},{16,112},{24,120},{32,64},{40,72},{48,80},{56,88},{... | collective-permute-start | bytes 393224 | tf_op jit(solution)/shard_map/ppermute | solution.py:357
  124.0 1.7 %finish.3 = (f32[32,128,128]{2,1,0:T(8,128)}, f32[8,128]{1,0:T(8,128)S(1)}) custom-call(s32[1]{0:T(128)} %bitcast.5.me_ref, s32[1]{0:T(128)S(6)} %copy.42.count_ref, s32[16,128]{1,0:T(8,128)S(1)} %get-tuple-element.487.refs_2_.table_ref, bf16[6,128,128]{2,1,0:T(8,128)(2,1)S(1)} %get-tuple-element.227.refs_0_, ...), custom_call_target="tpu_custom_call" | custom-call | tf_op jit(solution)/shard_map/finish/pallas_call | solution.py:333
  126.7 2.2 %finish.4 = (f32[32,128,128]{2,1,0:T(8,128)}, f32[8,128]{1,0:T(8,128)}) custom-call(s32[1]{0:T(128)} %bitcast.5.me_ref, s32[1]{0:T(128)S(6)} %copy.42.count_ref, s32[16,128]{1,0:T(8,128)S(1)} %get-tuple-element.487.refs_2_.table_ref, bf16[5,128,128]{2,1,0:T(8,128)(2,1)S(1)} %get-tuple-element.247.refs_0_, ...), custom_call_target="tpu_custom_call", output_to_operand_aliasing={{0}: (9, {})} | custom-call | tf_op jit(solution)/shard_map/finish/pallas_call | solution.py:333
  (80 shorter events, 21.5 us)
Async XLA Ops:
  3.5 15.4 %all-to-all-start = ((s32[8,1,128]{2,1,0:T(1,128)}), s32[8,1,128]{2,1,0:T(1,128)S(1)}, u32[]{:S(2)}, u32[]{:S(2)}) async-start(s32[8,1,128]{2,1,0:T(1,128)} %bitcast.3), calls=%async_computation | async-start | bytes 8192 | tf_op jit(solution)/shard_map/all_to_all | solution.py:377
  23.1 37.9 %all-to-all-start.1 = ((bf16[32,320,128]{2,1,0:T(8,128)(2,1)}), bf16[32,320,128]{2,1,0:T(8,128)(2,1)}, u32[]{:S(2)}, u32[]{:S(2)}) async-start(bf16[32,320,128]{2,1,0:T(8,128)(2,1)} %pack.1), calls=%async_computation.1 | async-start | bytes 5242880 | tf_op jit(solution)/shard_map/all_to_all | solution.py:379
  38.6 5.0 %collective-permute-start.12 = (bf16[48,128,128]{2,1,0:T(8,128)(2,1)S(1)}, bf16[48,128,128]{2,1,0:T(8,128)(2,1)S(1)}, u32[]{:S(2)}, u32[]{:S(2)}) collective-permute-start(bf16[48,128,128]{2,1,0:T(8,128)(2,1)S(1)} %tiles.18), channel_id=1, source_target_pairs={{0,8},{8,0},{16,24},{24,16},{32,40},{40,32},{48,56},{56,48},{64,72... | collective-permute-start | bytes 4718600 | tf_op jit(solution)/shard_map/ppermute | solution.py:357
  40.8 2.8 %copy-start.15 = (s32[8]{0:T(128)S(1)}, s32[8]{0:T(128)}, u32[]{:S(2)}) copy-start(s32[8]{0:T(128)} %constant.31.clone) | copy-start | bytes 100
  40.8 2.8 %copy-start.10 = (s32[8]{0:T(128)S(1)}, s32[8]{0:T(128)}, u32[]{:S(2)}) copy-start(s32[8]{0:T(128)} %constant.32.clone.refs_1_) | copy-start | bytes 100
  40.8 6.5 %collective-permute-start.13 = (bf16[48,128,128]{2,1,0:T(8,128)(2,1)S(1)}, bf16[48,128,128]{2,1,0:T(8,128)(2,1)S(1)}, u32[]{:S(2)}, u32[]{:S(2)}) collective-permute-start(bf16[48,128,128]{2,1,0:T(8,128)(2,1)S(1)} %tiles.19), channel_id=1, source_target_pairs={{0,8},{8,0},{16,24},{24,16},{32,40},{40,32},{48,56},{56,48},{64,72... | collective-permute-start | bytes 4718600 | tf_op jit(solution)/shard_map/ppermute | solution.py:357
  43.5 8.7 %collective-permute-start.14 = (bf16[48,128,128]{2,1,0:T(8,128)(2,1)S(1)}, bf16[48,128,128]{2,1,0:T(8,128)(2,1)S(1)}, u32[]{:S(2)}, u32[]{:S(2)}) collective-permute-start(bf16[48,128,128]{2,1,0:T(8,128)(2,1)S(1)} %tiles.20), channel_id=1, source_target_pairs={{0,8},{8,0},{16,24},{24,16},{32,40},{40,32},{48,56},{56,48},{64,72... | collective-permute-start | bytes 4718600 | tf_op jit(solution)/shard_map/ppermute | solution.py:357
  43.6 3.7 %copy-start.14 = (s32[8]{0:T(128)S(1)}, s32[8]{0:T(128)}, u32[]{:S(2)}) copy-start(s32[8]{0:T(128)} %constant.33.clone) | copy-start | bytes 100
  43.6 3.7 %copy-start.13 = (s32[8]{0:T(128)S(1)}, s32[8]{0:T(128)}, u32[]{:S(2)}) copy-start(s32[8]{0:T(128)} %constant.35.clone) | copy-start | bytes 100
  43.7 3.7 %copy-start.12 = (s32[8]{0:T(128)S(1)}, s32[8]{0:T(128)}, u32[]{:S(2)}) copy-start(s32[8]{0:T(128)} %constant.34.clone.refs_1_) | copy-start | bytes 100
  46.8 25.7 %collective-permute-start.15 = (bf16[24,128,128]{2,1,0:T(8,128)(2,1)}, bf16[24,128,128]{2,1,0:T(8,128)(2,1)S(1)}, u32[]{:S(2)}, u32[]{:S(2)}) collective-permute-start(bf16[24,128,128]{2,1,0:T(8,128)(2,1)} %get-tuple-element.211), channel_id=1, source_target_pairs={{0,16},{8,24},{16,0},{24,8},{32,48},{40,56},{48,32},{56,40},{64,80... | collective-permute-start | bytes 2359304 | tf_op jit(solution)/shard_map/ppermute | solution.py:357
  47.4 4.8 %copy-start.11 = (s32[8]{0:T(128)S(1)}, s32[8]{0:T(128)}, u32[]{:S(2)}) copy-start(s32[8]{0:T(128)} %constant.36.clone.refs_1_) | copy-start | bytes 100
  50.6 24.5 %collective-permute-start.16 = (bf16[24,128,128]{2,1,0:T(8,128)(2,1)}, bf16[24,128,128]{2,1,0:T(8,128)(2,1)S(1)}, u32[]{:S(2)}, u32[]{:S(2)}) collective-permute-start(bf16[24,128,128]{2,1,0:T(8,128)(2,1)} %get-tuple-element.215), channel_id=1, source_target_pairs={{0,32},{8,40},{16,48},{24,56},{32,0},{40,8},{48,16},{56,24},{64,96... | collective-permute-start | bytes 2359304 | tf_op jit(solution)/shard_map/ppermute | solution.py:357
  55.3 20.7 %collective-permute-start.17 = (bf16[24,128,128]{2,1,0:T(8,128)(2,1)}, bf16[24,128,128]{2,1,0:T(8,128)(2,1)S(1)}, u32[]{:S(2)}, u32[]{:S(2)}) collective-permute-start(bf16[24,128,128]{2,1,0:T(8,128)(2,1)} %get-tuple-element.218), channel_id=1, source_target_pairs={{0,96},{8,104},{16,112},{24,120},{32,64},{40,72},{48,80},{56,88},{... | collective-permute-start | bytes 2359304 | tf_op jit(solution)/shard_map/ppermute | solution.py:357
  72.3 9.5 %collective-permute-start.18 = (bf16[40,128,128]{2,1,0:T(8,128)(2,1)S(1)}, bf16[40,128,128]{2,1,0:T(8,128)(2,1)S(1)}, u32[]{:S(2)}, u32[]{:S(2)}) collective-permute-start(bf16[40,128,128]{2,1,0:T(8,128)(2,1)S(1)} %tiles.24), channel_id=1, source_target_pairs={{0,8},{8,0},{16,24},{24,16},{32,40},{40,32},{48,56},{56,48},{64,72... | collective-permute-start | bytes 3932168 | tf_op jit(solution)/shard_map/ppermute | solution.py:357
  74.6 10.3 %collective-permute-start.19 = (bf16[40,128,128]{2,1,0:T(8,128)(2,1)S(1)}, bf16[40,128,128]{2,1,0:T(8,128)(2,1)S(1)}, u32[]{:S(2)}, u32[]{:S(2)}) collective-permute-start(bf16[40,128,128]{2,1,0:T(8,128)(2,1)S(1)} %tiles.25), channel_id=1, source_target_pairs={{0,8},{8,0},{16,24},{24,16},{32,40},{40,32},{48,56},{56,48},{64,72... | collective-permute-start | bytes 3932168 | tf_op jit(solution)/shard_map/ppermute | solution.py:357
  77.9 15.5 %collective-permute-start.23 = (bf16[32,128,128]{2,1,0:T(8,128)(2,1)S(1)}, bf16[32,128,128]{2,1,0:T(8,128)(2,1)S(1)}, u32[]{:S(2)}, u32[]{:S(2)}) collective-permute-start(bf16[32,128,128]{2,1,0:T(8,128)(2,1)S(1)} %tiles.26), channel_id=1, source_target_pairs={{0,8},{8,0},{16,24},{24,16},{32,40},{40,32},{48,56},{56,48},{64,72... | collective-permute-start | bytes 3145736 | tf_op jit(solution)/shard_map/ppermute | solution.py:357
  78.1 11.9 %collective-permute-start.20 = (bf16[12,128,128]{2,1,0:T(8,128)(2,1)S(1)}, bf16[12,128,128]{2,1,0:T(8,128)(2,1)S(1)}, u32[]{:S(2)}, u32[]{:S(2)}) collective-permute-start(bf16[12,128,128]{2,1,0:T(8,128)(2,1)S(1)} %get-tuple-element.226), channel_id=1, source_target_pairs={{0,32},{8,40},{16,48},{24,56},{32,0},{40,8},{48,16},{56,24},{64,96... | collective-permute-start | bytes 1179656 | tf_op jit(solution)/shard_map/ppermute | solution.py:357
  79.7 13.5 %collective-permute-start.21 = (bf16[12,128,128]{2,1,0:T(8,128)(2,1)S(1)}, bf16[12,128,128]{2,1,0:T(8,128)(2,1)S(1)}, u32[]{:S(2)}, u32[]{:S(2)}) collective-permute-start(bf16[12,128,128]{2,1,0:T(8,128)(2,1)S(1)} %get-tuple-element.229), channel_id=1, source_target_pairs={{0,96},{8,104},{16,112},{24,120},{32,64},{40,72},{48,80},{56,88},{... | collective-permute-start | bytes 1179656 | tf_op jit(solution)/shard_map/ppermute | solution.py:357
  81.8 11.4 %collective-permute-start.22 = (bf16[12,128,128]{2,1,0:T(8,128)(2,1)S(1)}, bf16[12,128,128]{2,1,0:T(8,128)(2,1)S(1)}, u32[]{:S(2)}, u32[]{:S(2)}) collective-permute-start(bf16[12,128,128]{2,1,0:T(8,128)(2,1)S(1)} %get-tuple-element.232), channel_id=1, source_target_pairs={{0,16},{8,24},{16,0},{24,8},{32,48},{40,56},{48,32},{56,40},{64,80... | collective-permute-start | bytes 1179656 | tf_op jit(solution)/shard_map/ppermute | solution.py:357
  84.9 18.7 %collective-permute-start.24 = (bf16[20,128,128]{2,1,0:T(8,128)(2,1)S(1)}, bf16[20,128,128]{2,1,0:T(8,128)(2,1)S(1)}, u32[]{:S(2)}, u32[]{:S(2)}) collective-permute-start(bf16[20,128,128]{2,1,0:T(8,128)(2,1)S(1)} %get-tuple-element.237), channel_id=1, source_target_pairs={{0,32},{8,40},{16,48},{24,56},{32,0},{40,8},{48,16},{56,24},{64,96... | collective-permute-start | bytes 1966088 | tf_op jit(solution)/shard_map/ppermute | solution.py:357
  90.0 17.0 %collective-permute-start.25 = (bf16[20,128,128]{2,1,0:T(8,128)(2,1)S(1)}, bf16[20,128,128]{2,1,0:T(8,128)(2,1)S(1)}, u32[]{:S(2)}, u32[]{:S(2)}) collective-permute-start(bf16[20,128,128]{2,1,0:T(8,128)(2,1)S(1)} %get-tuple-element.240), channel_id=1, source_target_pairs={{0,96},{8,104},{16,112},{24,120},{32,64},{40,72},{48,80},{56,88},{... | collective-permute-start | bytes 1966088 | tf_op jit(solution)/shard_map/ppermute | solution.py:357
  95.1 13.6 %collective-permute-start.26 = (bf16[16,128,128]{2,1,0:T(8,128)(2,1)S(1)}, bf16[16,128,128]{2,1,0:T(8,128)(2,1)S(1)}, u32[]{:S(2)}, u32[]{:S(2)}) collective-permute-start(bf16[16,128,128]{2,1,0:T(8,128)(2,1)S(1)} %get-tuple-element.243), channel_id=1, source_target_pairs={{0,16},{8,24},{16,0},{24,8},{32,48},{40,56},{48,32},{56,40},{64,80... | collective-permute-start | bytes 1572872 | tf_op jit(solution)/shard_map/ppermute | solution.py:357
  103.8 10.5 %collective-permute-start.27 = (bf16[10,128,128]{2,1,0:T(8,128)(2,1)S(1)}, bf16[10,128,128]{2,1,0:T(8,128)(2,1)S(1)}, u32[]{:S(2)}, u32[]{:S(2)}) collective-permute-start(bf16[10,128,128]{2,1,0:T(8,128)(2,1)S(1)} %get-tuple-element.246), channel_id=1, source_target_pairs={{0,96},{8,104},{16,112},{24,120},{32,64},{40,72},{48,80},{56,88},{... | collective-permute-start | bytes 983048 | tf_op jit(solution)/shard_map/ppermute | solution.py:357
  107.2 10.4 %collective-permute-start.29 = (bf16[10,128,128]{2,1,0:T(8,128)(2,1)S(1)}, bf16[10,128,128]{2,1,0:T(8,128)(2,1)S(1)}, u32[]{:S(2)}, u32[]{:S(2)}) collective-permute-start(bf16[10,128,128]{2,1,0:T(8,128)(2,1)S(1)} %get-tuple-element.250), channel_id=1, source_target_pairs={{0,16},{8,24},{16,0},{24,8},{32,48},{40,56},{48,32},{56,40},{64,80... | collective-permute-start | bytes 983048 | tf_op jit(solution)/shard_map/ppermute | solution.py:357
  108.8 10.6 %collective-permute-start.31 = (bf16[8,128,128]{2,1,0:T(8,128)(2,1)S(1)}, bf16[8,128,128]{2,1,0:T(8,128)(2,1)S(1)}, u32[]{:S(2)}, u32[]{:S(2)}) collective-permute-start(bf16[8,128,128]{2,1,0:T(8,128)(2,1)S(1)} %get-tuple-element.254), channel_id=1, source_target_pairs={{0,32},{8,40},{16,48},{24,56},{32,0},{40,8},{48,16},{56,24},{64,96... | collective-permute-start | bytes 786440 | tf_op jit(solution)/shard_map/ppermute | solution.py:357
  109.0 11.4 %collective-permute-start.35 = (bf16[6,128,128]{2,1,0:T(8,128)(2,1)S(1)}, bf16[6,128,128]{2,1,0:T(8,128)(2,1)S(1)}, u32[]{:S(2)}, u32[]{:S(2)}) collective-permute-start(bf16[6,128,128]{2,1,0:T(8,128)(2,1)S(1)} %get-tuple-element.260), channel_id=1, source_target_pairs={{0,32},{8,40},{16,48},{24,56},{32,0},{40,8},{48,16},{56,24},{64,96... | collective-permute-start | bytes 589832 | tf_op jit(solution)/shard_map/ppermute | solution.py:357
  111.0 13.0 %collective-permute-start.34 = (bf16[6,128,128]{2,1,0:T(8,128)(2,1)S(1)}, bf16[6,128,128]{2,1,0:T(8,128)(2,1)S(1)}, u32[]{:S(2)}, u32[]{:S(2)}) collective-permute-start(bf16[6,128,128]{2,1,0:T(8,128)(2,1)S(1)} %get-tuple-element.259), channel_id=1, source_target_pairs={{0,16},{8,24},{16,0},{24,8},{32,48},{40,56},{48,32},{56,40},{64,80... | collective-permute-start | bytes 589832 | tf_op jit(solution)/shard_map/ppermute | solution.py:357
  114.3 9.6 %collective-permute-start.33 = (bf16[6,128,128]{2,1,0:T(8,128)(2,1)S(1)}, bf16[6,128,128]{2,1,0:T(8,128)(2,1)S(1)}, u32[]{:S(2)}, u32[]{:S(2)}) collective-permute-start(bf16[6,128,128]{2,1,0:T(8,128)(2,1)S(1)} %get-tuple-element.258), channel_id=1, source_target_pairs={{0,96},{8,104},{16,112},{24,120},{32,64},{40,72},{48,80},{56,88},{... | collective-permute-start | bytes 589832 | tf_op jit(solution)/shard_map/ppermute | solution.py:357
  117.7 8.0 %collective-permute-start.28 = (bf16[5,128,128]{2,1,0:T(8,128)(2,1)S(1)}, bf16[5,128,128]{2,1,0:T(8,128)(2,1)S(1)}, u32[]{:S(2)}, u32[]{:S(2)}) collective-permute-start(bf16[5,128,128]{2,1,0:T(8,128)(2,1)S(1)} %get-tuple-element.248), channel_id=1, source_target_pairs={{0,16},{8,24},{16,0},{24,8},{32,48},{40,56},{48,32},{56,40},{64,80... | collective-permute-start | bytes 491528 | tf_op jit(solution)/shard_map/ppermute | solution.py:357
  119.5 7.3 %collective-permute-start.30 = (bf16[5,128,128]{2,1,0:T(8,128)(2,1)S(1)}, bf16[5,128,128]{2,1,0:T(8,128)(2,1)S(1)}, u32[]{:S(2)}, u32[]{:S(2)}) collective-permute-start(bf16[5,128,128]{2,1,0:T(8,128)(2,1)S(1)} %get-tuple-element.252), channel_id=1, source_target_pairs={{0,32},{8,40},{16,48},{24,56},{32,0},{40,8},{48,16},{56,24},{64,96... | collective-permute-start | bytes 491528 | tf_op jit(solution)/shard_map/ppermute | solution.py:357
  120.4 6.4 %collective-permute-start.32 = (bf16[4,128,128]{2,1,0:T(8,128)(2,1)S(1)}, bf16[4,128,128]{2,1,0:T(8,128)(2,1)S(1)}, u32[]{:S(2)}, u32[]{:S(2)}) collective-permute-start(bf16[4,128,128]{2,1,0:T(8,128)(2,1)S(1)} %get-tuple-element.256), channel_id=1, source_target_pairs={{0,96},{8,104},{16,112},{24,120},{32,64},{40,72},{48,80},{56,88},{... | collective-permute-start | bytes 393224 | tf_op jit(solution)/shard_map/ppermute | solution.py:357
  (4 other events, 6.6 us)

commit v7 on v6

--- a/solution.py
+++ b/solution.py
@@ -393,7 +393,7 @@
         mine = me ^ jnp.array(masks, I32)
         places = jnp.array([m // 2 for m in masks], I32)
         return tiles(
-            after(mine, last), places, table, wt, e_blocks, offsets[c][i], cuts[c][i], 2, rolled, core, c == 0
+            after(mine, last), places, table, wt, e_blocks, offsets[c][i], cuts[c][i], 2, rolled, core, (c, i) == (0, 2)
         )
 
     def exchange(c, outs, step):

time: 131 us -> 132 us (level)
  Pallas kernels: 56.5 us -> 58 us
    pallas_call x12, Pallas kernels: 1.59 us -> 3.86 us  [add_pairs(): pl.pallas_call(functools.partial(add_kernel, len(pairs)), in_specs=[vmem]...]
  transfers between devices with their start and end apart: 26 -> 26, of which waited for: 11 -> 10; matrix products, arithmetic and copies ran while one was open for 1% -> 1% of each run, Pallas kernels for 37% -> 38%
where the time goes in v7:
time: 132 us; the launch traced here: 131 us
  Pallas kernels  58 us (44%)
  starting transfers between devices  42.8 us (32%)
  waiting for transfers between devices  25.9 us (20%)
  local copies, waits for them, and re-layouts  1.81 us (1%)
    ppermute x24, starting transfers between devices, swap(): return lax.ppermute(a, 'tm', [(i, i ^ mask) for i in range(n)])  30.6 us
    pallas_call x12, Pallas kernels, tiles(): pl.pallas_call(functools.partial(tiles_kernel, first, per, with_add, roll...  25.7 us
    pallas_call x2, Pallas kernels, prep(): pl.pallas_call(functools.partial(prep_kernel, with_far), in_specs=[vmem]...  18.2 us
    ppermute x24, waiting for transfers between devices, swap(): return lax.ppermute(a, 'tm', [(i, i ^ mask) for i in range(n)])  14.9 us
    all_to_all x1, starting transfers between devices, body(): lax.all_to_all(request, 'tile', split_axis=0, concat_axis=0, tiled=True)  7.86 us
    all_to_all x1, waiting for transfers between devices, body(): lax.all_to_all(request, 'tile', split_axis=0, concat_axis=0, tiled=True)  6.9 us
    all_to_all x1, starting transfers between devices, body(): lax.all_to_all(outgoing, 'tile', split_axis=0, concat_axis=0, tiled=True)  4.41 us
    pallas_call x1, Pallas kernels, pack(): pl.pallas_call(pack_kernel, in_specs=[pl.BlockSpec(memory_space=pltpu.SME...  4.13 us
  transfers between devices with their start and end apart: 26, of which 10 were waited for; matrix products, arithmetic and copies ran while one was open for 1% of the time, Pallas kernels for 38%

profile of v7, /device:TPU:0, one launch (start us, length us, event | category | flops | bytes accessed | tf_op | source)
XLA Modules:
  0.0 131.2 jit_solution(11551636323842904650)
XLA Ops:
  1.3 2.2 %plan.1 = (s32[8,128]{1,0:T(8,128)}, s32[16,128]{1,0:T(8,128)S(1)}) custom-call(s32[1]{0:T(128)} %bitcast.own_ref, s32[1]{0:T(128)S(6)} %copy.42.count_ref, s32[2,512]{1,0:T(2,128)S(1)} %bitcast.12), custom_call_target="tpu_custom_call" | custom-call | tf_op jit(solution)/shard_map/plan/pallas_call | solution.py:89
  3.5 7.9 %all-to-all-start = ((s32[8,1,128]{2,1,0:T(1,128)}), s32[8,1,128]{2,1,0:T(1,128)S(1)}, u32[]{:S(2)}, u32[]{:S(2)}) async-start(s32[8,1,128]{2,1,0:T(1,128)} %bitcast.3), calls=%async_computation | async-start | bytes 8192 | tf_op jit(solution)/shard_map/all_to_all | solution.py:377
  12.1 6.9 %all-to-all-done = s32[8,1,128]{2,1,0:T(1,128)S(1)} async-done(((s32[8,1,128]{2,1,0:T(1,128)}), s32[8,1,128]{2,1,0:T(1,128)S(1)}, u32[]{:S(2)}, u32[]{:S(2)}) %all-to-all-start) | async-done | bytes 4128 | tf_op jit(solution)/shard_map/all_to_all | solution.py:377
  19.0 4.1 %pack.1 = bf16[32,320,128]{2,1,0:T(8,128)(2,1)} custom-call(s32[1]{0:T(128)} %bitcast.own_ref, s32[8,128]{1,0:T(8,128)S(1)} %bitcast.10, bf16[320,16384]{1,0:T(8,128)(2,1)} %em_ref.5), custom_call_target="tpu_custom_call" | custom-call | tf_op jit(solution)/shard_map/pack/pallas_call | solution.py:226
  23.1 4.4 %all-to-all-start.1 = ((bf16[32,320,128]{2,1,0:T(8,128)(2,1)}), bf16[32,320,128]{2,1,0:T(8,128)(2,1)}, u32[]{:S(2)}, u32[]{:S(2)}) async-start(bf16[32,320,128]{2,1,0:T(8,128)(2,1)} %pack.1), calls=%async_computation.1 | async-start | bytes 5242880 | tf_op jit(solution)/shard_map/all_to_all | solution.py:379
  27.7 8.9 %prep.3 = (bf16[128,128,384]{2,1,0:T(8,128)(2,1)S(1)}, bf16[128,384,128]{2,1,0:T(8,128)(2,1)S(1)}) custom-call(f32[320,1]{1,0:T(8,128)S(1)} %copy.30.weights_ref, bf16[320,16384]{1,0:T(8,128)(2,1)} %adj_ref.3, bf16[320,16384]{1,0:T(8,128)(2,1)} %em_ref.5), custom_call_target="tpu_custom_call" | custom-call | tf_op jit(solution)/shard_map/prep/pallas_call | solution.py:178
  36.5 2.1 %tiles.18 = bf16[48,128,128]{2,1,0:T(8,128)(2,1)S(1)} custom-call(s32[8]{0:T(128)S(1)} %multiply_xor_fusion.1.refs_0_.refs_1_, s32[8]{0:T(128)S(1)} %multiply_xor_fusion.1.refs_0_.refs_1_, s32[16,128]{1,0:T(8,128)S(1)} %get-tuple-element.487.refs_2_.table_ref, bf16[128,128,384]{2,1,0:T(8,128)(2,1)S(1)} %get-tuple-element.195.refs_3_, ...), custom_call_target="tpu_custom_call" | custom-call | tf_op jit(solution)/shard_map/tiles/pallas_call | solution.py:270
  38.7 2.1 %tiles.19 = bf16[48,128,128]{2,1,0:T(8,128)(2,1)S(1)} custom-call(s32[8]{0:T(128)S(1)} %multiply_xor_fusion.1.refs_0_.refs_1_, s32[8]{0:T(128)S(1)} %multiply_xor_fusion.1.refs_0_.refs_1_, s32[16,128]{1,0:T(8,128)S(1)} %get-tuple-element.487.refs_2_.table_ref, bf16[128,128,384]{2,1,0:T(8,128)(2,1)S(1)} %get-tuple-element.195.refs_3_, ...), custom_call_target="tpu_custom_call" | custom-call | tf_op jit(solution)/shard_map/tiles/pallas_call | solution.py:270
  41.4 2.1 %tiles.20 = bf16[48,128,128]{2,1,0:T(8,128)(2,1)S(1)} custom-call(s32[8]{0:T(128)S(1)} %multiply_xor_fusion.1.refs_0_.refs_1_, s32[8]{0:T(128)S(1)} %multiply_xor_fusion.1.refs_0_.refs_1_, s32[16,128]{1,0:T(8,128)S(1)} %get-tuple-element.487.refs_2_.table_ref, bf16[128,128,384]{2,1,0:T(8,128)(2,1)S(1)} %get-tuple-element.195.refs_3_, ...), custom_call_target="tpu_custom_call" | custom-call | tf_op jit(solution)/shard_map/tiles/pallas_call | solution.py:270
  43.7 2.8 %tiles.21 = (bf16[24,128,128]{2,1,0:T(8,128)(2,1)}, bf16[24,128,128]{2,1,0:T(8,128)(2,1)S(1)}) custom-call(s32[8]{0:T(128)S(1)} %broadcast_xor_fusion.3.refs_0_, s32[8]{0:T(128)S(1)} %copy-done.6, s32[16,128]{1,0:T(8,128)S(1)} %get-tuple-element.487.refs_2_.table_ref, bf16[128,128,384]{2,1,0:T(8,128)(2,1)S(1)} %get-tuple-element.195.refs_3_, ...), custom_call_target="tpu_custom_call" | custom-call | tf_op jit(solution)/shard_map/tiles/pallas_call | solution.py:270
  47.1 2.8 %tiles.22 = (bf16[24,128,128]{2,1,0:T(8,128)(2,1)}, bf16[24,128,128]{2,1,0:T(8,128)(2,1)S(1)}) custom-call(s32[8]{0:T(128)S(1)} %broadcast_xor_fusion.5.refs_0_, s32[8]{0:T(128)S(1)} %copy-done.8, s32[16,128]{1,0:T(8,128)S(1)} %get-tuple-element.487.refs_2_.table_ref, bf16[128,128,384]{2,1,0:T(8,128)(2,1)S(1)} %get-tuple-element.195.refs_3_, ...), custom_call_target="tpu_custom_call" | custom-call | tf_op jit(solution)/shard_map/tiles/pallas_call | solution.py:270
  51.4 3.1 %tiles.23 = (bf16[24,128,128]{2,1,0:T(8,128)(2,1)}, bf16[24,128,128]{2,1,0:T(8,128)(2,1)}) custom-call(s32[8]{0:T(128)S(1)} %broadcast_xor_fusion.4.refs_0_, s32[8]{0:T(128)S(1)} %copy-done.7, s32[16,128]{1,0:T(8,128)S(1)} %get-tuple-element.487.refs_2_.table_ref, bf16[128,128,384]{2,1,0:T(8,128)(2,1)S(1)} %get-tuple-element.195.refs_3_, ...), custom_call_target="tpu_custom_call" | custom-call | tf_op jit(solution)/shard_map/tiles/pallas_call | solution.py:270
  54.5 2.2 %collective-permute-start.17 = (bf16[24,128,128]{2,1,0:T(8,128)(2,1)}, bf16[24,128,128]{2,1,0:T(8,128)(2,1)S(1)}, u32[]{:S(2)}, u32[]{:S(2)}) collective-permute-start(bf16[24,128,128]{2,1,0:T(8,128)(2,1)} %get-tuple-element.218), channel_id=1, source_target_pairs={{0,96},{8,104},{16,112},{24,120},{32,64},{40,72},{48,80},{56,88},{... | collective-permute-start | bytes 2359304 | tf_op jit(solution)/shard_map/ppermute | solution.py:357
  56.9 4.1 %all-to-all-done.1.refs_0_ = bf16[32,320,128]{2,1,0:T(8,128)(2,1)} async-done(((bf16[32,320,128]{2,1,0:T(8,128)(2,1)}), bf16[32,320,128]{2,1,0:T(8,128)(2,1)}, u32[]{:S(2)}, u32[]{:S(2)}) %all-to-all-start.1) | async-done | bytes 2621472 | tf_op jit(solution)/shard_map/all_to_all | solution.py:379
  61.0 9.4 %prep.4 = (bf16[128,128,384]{2,1,0:T(8,128)(2,1)S(1)}, bf16[160,384,128]{2,1,0:T(8,128)(2,1)S(1)}) custom-call(f32[320,1]{1,0:T(8,128)S(1)} %copy.31.weights_ref, bf16[320,16384]{1,0:T(8,128)(2,1)} %adj_ref.3, bf16[320,16384]{1,0:T(8,128)(2,1)} %em_ref.5, bf16[32,320,128]{2,1,0:T(8,128)(2,1)} %all-to-all-done.1.refs_0_), custom_call_target="tpu_custom_call" | custom-call | tf_op jit(solution)/shard_map/prep/pallas_call | solution.py:178
  70.4 1.9 %tiles.24 = bf16[40,128,128]{2,1,0:T(8,128)(2,1)S(1)} custom-call(s32[8]{0:T(128)S(1)} %multiply_xor_fusion.1.refs_0_.refs_1_, s32[8]{0:T(128)S(1)} %multiply_xor_fusion.1.refs_0_.refs_1_, s32[16,128]{1,0:T(8,128)S(1)} %get-tuple-element.487.refs_2_.table_ref, bf16[128,128,384]{2,1,0:T(8,128)(2,1)S(1)} %get-tuple-element.207.refs_3_, ...), custom_call_target="tpu_custom_call" | custom-call | tf_op jit(solution)/shard_map/tiles/pallas_call | solution.py:270
  73.9 1.9 %tiles.25 = bf16[40,128,128]{2,1,0:T(8,128)(2,1)S(1)} custom-call(s32[8]{0:T(128)S(1)} %multiply_xor_fusion.1.refs_0_.refs_1_, s32[8]{0:T(128)S(1)} %multiply_xor_fusion.1.refs_0_.refs_1_, s32[16,128]{1,0:T(8,128)S(1)} %get-tuple-element.487.refs_2_.table_ref, bf16[128,128,384]{2,1,0:T(8,128)(2,1)S(1)} %get-tuple-element.207.refs_3_, ...), custom_call_target="tpu_custom_call" | custom-call | tf_op jit(solution)/shard_map/tiles/pallas_call | solution.py:270
  81.3 2.2 %collective-permute-start.21 = (bf16[12,128,128]{2,1,0:T(8,128)(2,1)S(1)}, bf16[12,128,128]{2,1,0:T(8,128)(2,1)S(1)}, u32[]{:S(2)}, u32[]{:S(2)}) collective-permute-start(bf16[12,128,128]{2,1,0:T(8,128)(2,1)S(1)} %get-tuple-element.229), channel_id=1, source_target_pairs={{0,96},{8,104},{16,112},{24,120},{32,64},{40,72},{48,80},{56,88},{... | collective-permute-start | bytes 1179656 | tf_op jit(solution)/shard_map/ppermute | solution.py:357
  84.9 1.9 %tiles.27 = (bf16[20,128,128]{2,1,0:T(8,128)(2,1)S(1)}, bf16[20,128,128]{2,1,0:T(8,128)(2,1)S(1)}) custom-call(s32[8]{0:T(128)S(1)} %broadcast_xor_fusion.5.refs_0_, s32[8]{0:T(128)S(1)} %copy-done.8, s32[16,128]{1,0:T(8,128)S(1)} %get-tuple-element.487.refs_2_.table_ref, bf16[128,128,384]{2,1,0:T(8,128)(2,1)S(1)} %get-tuple-element.207.refs_3_, ...), custom_call_target="tpu_custom_call" | custom-call | tf_op jit(solution)/shard_map/tiles/pallas_call | solution.py:270
  87.6 1.9 %tiles.28 = (bf16[20,128,128]{2,1,0:T(8,128)(2,1)S(1)}, bf16[20,128,128]{2,1,0:T(8,128)(2,1)S(1)}) custom-call(s32[8]{0:T(128)S(1)} %broadcast_xor_fusion.4.refs_0_, s32[8]{0:T(128)S(1)} %copy-done.7, s32[16,128]{1,0:T(8,128)S(1)} %get-tuple-element.487.refs_2_.table_ref, bf16[128,128,384]{2,1,0:T(8,128)(2,1)S(1)} %get-tuple-element.207.refs_3_, ...), custom_call_target="tpu_custom_call" | custom-call | tf_op jit(solution)/shard_map/tiles/pallas_call | solution.py:270
  89.5 2.2 %collective-permute-done.20.refs_1_ = bf16[12,128,128]{2,1,0:T(8,128)(2,1)S(1)} collective-permute-done((bf16[12,128,128]{2,1,0:T(8,128)(2,1)S(1)}, bf16[12,128,128]{2,1,0:T(8,128)(2,1)S(1)}, u32[]{:S(2)}, u32[]{:S(2)}) %collective-permute-start.20) | collective-permute-done | bytes 393248 | tf_op jit(solution)/shard_map/ppermute | solution.py:357
  91.7 3.0 %collective-permute-start.25 = (bf16[20,128,128]{2,1,0:T(8,128)(2,1)S(1)}, bf16[20,128,128]{2,1,0:T(8,128)(2,1)S(1)}, u32[]{:S(2)}, u32[]{:S(2)}) collective-permute-start(bf16[20,128,128]{2,1,0:T(8,128)(2,1)S(1)} %get-tuple-element.240), channel_id=1, source_target_pairs={{0,96},{8,104},{16,112},{24,120},{32,64},{40,72},{48,80},{56,88},{... | collective-permute-start | bytes 1966088 | tf_op jit(solution)/shard_map/ppermute | solution.py:357
  96.7 1.8 %collective-permute-start.26 = (bf16[16,128,128]{2,1,0:T(8,128)(2,1)S(1)}, bf16[16,128,128]{2,1,0:T(8,128)(2,1)S(1)}, u32[]{:S(2)}, u32[]{:S(2)}) collective-permute-start(bf16[16,128,128]{2,1,0:T(8,128)(2,1)S(1)} %get-tuple-element.243), channel_id=1, source_target_pairs={{0,16},{8,24},{16,0},{24,8},{32,48},{40,56},{48,32},{56,40},{64,80... | collective-permute-start | bytes 1572872 | tf_op jit(solution)/shard_map/ppermute | solution.py:357
  99.2 5.9 %collective-permute-done.24.refs_1_ = bf16[20,128,128]{2,1,0:T(8,128)(2,1)S(1)} collective-permute-done((bf16[20,128,128]{2,1,0:T(8,128)(2,1)S(1)}, bf16[20,128,128]{2,1,0:T(8,128)(2,1)S(1)}, u32[]{:S(2)}, u32[]{:S(2)}) %collective-permute-start.24) | collective-permute-done | bytes 655392 | tf_op jit(solution)/shard_map/ppermute | solution.py:357
  105.2 3.1 %collective-permute-start.27 = (bf16[10,128,128]{2,1,0:T(8,128)(2,1)S(1)}, bf16[10,128,128]{2,1,0:T(8,128)(2,1)S(1)}, u32[]{:S(2)}, u32[]{:S(2)}) collective-permute-start(bf16[10,128,128]{2,1,0:T(8,128)(2,1)S(1)} %get-tuple-element.246), channel_id=1, source_target_pairs={{0,96},{8,104},{16,112},{24,120},{32,64},{40,72},{48,80},{56,88},{... | collective-permute-start | bytes 983048 | tf_op jit(solution)/shard_map/ppermute | solution.py:357
  110.2 1.9 %collective-permute-start.35 = (bf16[6,128,128]{2,1,0:T(8,128)(2,1)S(1)}, bf16[6,128,128]{2,1,0:T(8,128)(2,1)S(1)}, u32[]{:S(2)}, u32[]{:S(2)}) collective-permute-start(bf16[6,128,128]{2,1,0:T(8,128)(2,1)S(1)} %get-tuple-element.260), channel_id=1, source_target_pairs={{0,32},{8,40},{16,48},{24,56},{32,0},{40,8},{48,16},{56,24},{64,96... | collective-permute-start | bytes 589832 | tf_op jit(solution)/shard_map/ppermute | solution.py:357
  112.9 2.7 %collective-permute-done.27.refs_1_ = bf16[10,128,128]{2,1,0:T(8,128)(2,1)S(1)} collective-permute-done((bf16[10,128,128]{2,1,0:T(8,128)(2,1)S(1)}, bf16[10,128,128]{2,1,0:T(8,128)(2,1)S(1)}, u32[]{:S(2)}, u32[]{:S(2)}) %collective-permute-start.27) | collective-permute-done | bytes 327712 | tf_op jit(solution)/shard_map/ppermute | solution.py:357
  115.7 3.0 %collective-permute-start.33 = (bf16[6,128,128]{2,1,0:T(8,128)(2,1)S(1)}, bf16[6,128,128]{2,1,0:T(8,128)(2,1)S(1)}, u32[]{:S(2)}, u32[]{:S(2)}) collective-permute-start(bf16[6,128,128]{2,1,0:T(8,128)(2,1)S(1)} %get-tuple-element.258), channel_id=1, source_target_pairs={{0,96},{8,104},{16,112},{24,120},{32,64},{40,72},{48,80},{56,88},{... | collective-permute-start | bytes 589832 | tf_op jit(solution)/shard_map/ppermute | solution.py:357
  122.0 2.3 %collective-permute-start.32 = (bf16[4,128,128]{2,1,0:T(8,128)(2,1)S(1)}, bf16[4,128,128]{2,1,0:T(8,128)(2,1)S(1)}, u32[]{:S(2)}, u32[]{:S(2)}) collective-permute-start(bf16[4,128,128]{2,1,0:T(8,128)(2,1)S(1)} %get-tuple-element.256), channel_id=1, source_target_pairs={{0,96},{8,104},{16,112},{24,120},{32,64},{40,72},{48,80},{56,88},{... | collective-permute-start | bytes 393224 | tf_op jit(solution)/shard_map/ppermute | solution.py:357
  124.4 1.7 %finish.3 = (f32[32,128,128]{2,1,0:T(8,128)}, f32[8,128]{1,0:T(8,128)S(1)}) custom-call(s32[1]{0:T(128)} %bitcast.5.me_ref, s32[1]{0:T(128)S(6)} %copy.42.count_ref, s32[16,128]{1,0:T(8,128)S(1)} %get-tuple-element.487.refs_2_.table_ref, bf16[6,128,128]{2,1,0:T(8,128)(2,1)S(1)} %get-tuple-element.227.refs_0_, ...), custom_call_target="tpu_custom_call" | custom-call | tf_op jit(solution)/shard_map/finish/pallas_call | solution.py:333
  126.1 2.1 %collective-permute-done.32.refs_5_ = bf16[4,128,128]{2,1,0:T(8,128)(2,1)S(1)} collective-permute-done((bf16[4,128,128]{2,1,0:T(8,128)(2,1)S(1)}, bf16[4,128,128]{2,1,0:T(8,128)(2,1)S(1)}, u32[]{:S(2)}, u32[]{:S(2)}) %collective-permute-start.32) | collective-permute-done | bytes 131104 | tf_op jit(solution)/shard_map/ppermute | solution.py:357
  128.2 2.2 %finish.4 = (f32[32,128,128]{2,1,0:T(8,128)}, f32[8,128]{1,0:T(8,128)}) custom-call(s32[1]{0:T(128)} %bitcast.5.me_ref, s32[1]{0:T(128)S(6)} %copy.42.count_ref, s32[16,128]{1,0:T(8,128)S(1)} %get-tuple-element.487.refs_2_.table_ref, bf16[5,128,128]{2,1,0:T(8,128)(2,1)S(1)} %get-tuple-element.247.refs_0_, ...), custom_call_target="tpu_custom_call", output_to_operand_aliasing={{0}: (9, {})} | custom-call | tf_op jit(solution)/shard_map/finish/pallas_call | solution.py:333
  (76 shorter events, 23.7 us)
Async XLA Ops:
  3.5 15.4 %all-to-all-start = ((s32[8,1,128]{2,1,0:T(1,128)}), s32[8,1,128]{2,1,0:T(1,128)S(1)}, u32[]{:S(2)}, u32[]{:S(2)}) async-start(s32[8,1,128]{2,1,0:T(1,128)} %bitcast.3), calls=%async_computation | async-start | bytes 8192 | tf_op jit(solution)/shard_map/all_to_all | solution.py:377
  23.1 37.9 %all-to-all-start.1 = ((bf16[32,320,128]{2,1,0:T(8,128)(2,1)}), bf16[32,320,128]{2,1,0:T(8,128)(2,1)}, u32[]{:S(2)}, u32[]{:S(2)}) async-start(bf16[32,320,128]{2,1,0:T(8,128)(2,1)} %pack.1), calls=%async_computation.1 | async-start | bytes 5242880 | tf_op jit(solution)/shard_map/all_to_all | solution.py:379
  38.6 5.0 %collective-permute-start.12 = (bf16[48,128,128]{2,1,0:T(8,128)(2,1)S(1)}, bf16[48,128,128]{2,1,0:T(8,128)(2,1)S(1)}, u32[]{:S(2)}, u32[]{:S(2)}) collective-permute-start(bf16[48,128,128]{2,1,0:T(8,128)(2,1)S(1)} %tiles.18), channel_id=1, source_target_pairs={{0,8},{8,0},{16,24},{24,16},{32,40},{40,32},{48,56},{56,48},{64,72... | collective-permute-start | bytes 4718600 | tf_op jit(solution)/shard_map/ppermute | solution.py:357
  40.8 2.8 %copy-start.11 = (s32[8]{0:T(128)S(1)}, s32[8]{0:T(128)}, u32[]{:S(2)}) copy-start(s32[8]{0:T(128)} %constant.31.clone) | copy-start | bytes 100
  40.8 2.8 %copy-start.6 = (s32[8]{0:T(128)S(1)}, s32[8]{0:T(128)}, u32[]{:S(2)}) copy-start(s32[8]{0:T(128)} %constant.32.clone.refs_1_) | copy-start | bytes 100
  40.8 6.2 %collective-permute-start.13 = (bf16[48,128,128]{2,1,0:T(8,128)(2,1)S(1)}, bf16[48,128,128]{2,1,0:T(8,128)(2,1)S(1)}, u32[]{:S(2)}, u32[]{:S(2)}) collective-permute-start(bf16[48,128,128]{2,1,0:T(8,128)(2,1)S(1)} %tiles.19), channel_id=1, source_target_pairs={{0,8},{8,0},{16,24},{24,16},{32,40},{40,32},{48,56},{56,48},{64,72... | collective-permute-start | bytes 4718600 | tf_op jit(solution)/shard_map/ppermute | solution.py:357
  43.5 7.9 %collective-permute-start.14 = (bf16[48,128,128]{2,1,0:T(8,128)(2,1)S(1)}, bf16[48,128,128]{2,1,0:T(8,128)(2,1)S(1)}, u32[]{:S(2)}, u32[]{:S(2)}) collective-permute-start(bf16[48,128,128]{2,1,0:T(8,128)(2,1)S(1)} %tiles.20), channel_id=1, source_target_pairs={{0,8},{8,0},{16,24},{24,16},{32,40},{40,32},{48,56},{56,48},{64,72... | collective-permute-start | bytes 4718600 | tf_op jit(solution)/shard_map/ppermute | solution.py:357
  43.6 3.4 %copy-start.10 = (s32[8]{0:T(128)S(1)}, s32[8]{0:T(128)}, u32[]{:S(2)}) copy-start(s32[8]{0:T(128)} %constant.33.clone) | copy-start | bytes 100
  43.6 3.4 %copy-start.9 = (s32[8]{0:T(128)S(1)}, s32[8]{0:T(128)}, u32[]{:S(2)}) copy-start(s32[8]{0:T(128)} %constant.35.clone) | copy-start | bytes 100
  43.6 3.4 %copy-start.8 = (s32[8]{0:T(128)S(1)}, s32[8]{0:T(128)}, u32[]{:S(2)}) copy-start(s32[8]{0:T(128)} %constant.34.clone.refs_1_) | copy-start | bytes 100
  46.4 26.2 %collective-permute-start.15 = (bf16[24,128,128]{2,1,0:T(8,128)(2,1)}, bf16[24,128,128]{2,1,0:T(8,128)(2,1)}, u32[]{:S(2)}, u32[]{:S(2)}) collective-permute-start(bf16[24,128,128]{2,1,0:T(8,128)(2,1)} %get-tuple-element.211), channel_id=1, source_target_pairs={{0,16},{8,24},{16,0},{24,8},{32,48},{40,56},{48,32},{56,40},{64,80... | collective-permute-start | bytes 2359304 | tf_op jit(solution)/shard_map/ppermute | solution.py:357
  47.0 4.4 %copy-start.7 = (s32[8]{0:T(128)S(1)}, s32[8]{0:T(128)}, u32[]{:S(2)}) copy-start(s32[8]{0:T(128)} %constant.36.clone.refs_1_) | copy-start | bytes 100
  49.9 26.3 %collective-permute-start.16 = (bf16[24,128,128]{2,1,0:T(8,128)(2,1)}, bf16[24,128,128]{2,1,0:T(8,128)(2,1)}, u32[]{:S(2)}, u32[]{:S(2)}) collective-permute-start(bf16[24,128,128]{2,1,0:T(8,128)(2,1)} %get-tuple-element.215), channel_id=1, source_target_pairs={{0,32},{8,40},{16,48},{24,56},{32,0},{40,8},{48,16},{56,24},{64,96... | collective-permute-start | bytes 2359304 | tf_op jit(solution)/shard_map/ppermute | solution.py:357
  54.5 23.0 %collective-permute-start.17 = (bf16[24,128,128]{2,1,0:T(8,128)(2,1)}, bf16[24,128,128]{2,1,0:T(8,128)(2,1)S(1)}, u32[]{:S(2)}, u32[]{:S(2)}) collective-permute-start(bf16[24,128,128]{2,1,0:T(8,128)(2,1)} %get-tuple-element.218), channel_id=1, source_target_pairs={{0,96},{8,104},{16,112},{24,120},{32,64},{40,72},{48,80},{56,88},{... | collective-permute-start | bytes 2359304 | tf_op jit(solution)/shard_map/ppermute | solution.py:357
  72.3 11.2 %collective-permute-start.18 = (bf16[40,128,128]{2,1,0:T(8,128)(2,1)S(1)}, bf16[40,128,128]{2,1,0:T(8,128)(2,1)S(1)}, u32[]{:S(2)}, u32[]{:S(2)}) collective-permute-start(bf16[40,128,128]{2,1,0:T(8,128)(2,1)S(1)} %tiles.24), channel_id=1, source_target_pairs={{0,8},{8,0},{16,24},{24,16},{32,40},{40,32},{48,56},{56,48},{64,72... | collective-permute-start | bytes 3932168 | tf_op jit(solution)/shard_map/ppermute | solution.py:357
  75.8 11.0 %collective-permute-start.19 = (bf16[40,128,128]{2,1,0:T(8,128)(2,1)S(1)}, bf16[40,128,128]{2,1,0:T(8,128)(2,1)S(1)}, u32[]{:S(2)}, u32[]{:S(2)}) collective-permute-start(bf16[40,128,128]{2,1,0:T(8,128)(2,1)S(1)} %tiles.25), channel_id=1, source_target_pairs={{0,8},{8,0},{16,24},{24,16},{32,40},{40,32},{48,56},{56,48},{64,72... | collective-permute-start | bytes 3932168 | tf_op jit(solution)/shard_map/ppermute | solution.py:357
  79.4 15.6 %collective-permute-start.23 = (bf16[32,128,128]{2,1,0:T(8,128)(2,1)S(1)}, bf16[32,128,128]{2,1,0:T(8,128)(2,1)S(1)}, u32[]{:S(2)}, u32[]{:S(2)}) collective-permute-start(bf16[32,128,128]{2,1,0:T(8,128)(2,1)S(1)} %tiles.26), channel_id=1, source_target_pairs={{0,8},{8,0},{16,24},{24,16},{32,40},{40,32},{48,56},{56,48},{64,72... | collective-permute-start | bytes 3145736 | tf_op jit(solution)/shard_map/ppermute | solution.py:357
  79.7 11.9 %collective-permute-start.20 = (bf16[12,128,128]{2,1,0:T(8,128)(2,1)S(1)}, bf16[12,128,128]{2,1,0:T(8,128)(2,1)S(1)}, u32[]{:S(2)}, u32[]{:S(2)}) collective-permute-start(bf16[12,128,128]{2,1,0:T(8,128)(2,1)S(1)} %get-tuple-element.226), channel_id=1, source_target_pairs={{0,32},{8,40},{16,48},{24,56},{32,0},{40,8},{48,16},{56,24},{64,96... | collective-permute-start | bytes 1179656 | tf_op jit(solution)/shard_map/ppermute | solution.py:357
  81.3 13.5 %collective-permute-start.21 = (bf16[12,128,128]{2,1,0:T(8,128)(2,1)S(1)}, bf16[12,128,128]{2,1,0:T(8,128)(2,1)S(1)}, u32[]{:S(2)}, u32[]{:S(2)}) collective-permute-start(bf16[12,128,128]{2,1,0:T(8,128)(2,1)S(1)} %get-tuple-element.229), channel_id=1, source_target_pairs={{0,96},{8,104},{16,112},{24,120},{32,64},{40,72},{48,80},{56,88},{... | collective-permute-start | bytes 1179656 | tf_op jit(solution)/shard_map/ppermute | solution.py:357
  83.5 11.4 %collective-permute-start.22 = (bf16[12,128,128]{2,1,0:T(8,128)(2,1)S(1)}, bf16[12,128,128]{2,1,0:T(8,128)(2,1)S(1)}, u32[]{:S(2)}, u32[]{:S(2)}) collective-permute-start(bf16[12,128,128]{2,1,0:T(8,128)(2,1)S(1)} %get-tuple-element.232), channel_id=1, source_target_pairs={{0,16},{8,24},{16,0},{24,8},{32,48},{40,56},{48,32},{56,40},{64,80... | collective-permute-start | bytes 1179656 | tf_op jit(solution)/shard_map/ppermute | solution.py:357
  86.8 18.2 %collective-permute-start.24 = (bf16[20,128,128]{2,1,0:T(8,128)(2,1)S(1)}, bf16[20,128,128]{2,1,0:T(8,128)(2,1)S(1)}, u32[]{:S(2)}, u32[]{:S(2)}) collective-permute-start(bf16[20,128,128]{2,1,0:T(8,128)(2,1)S(1)} %get-tuple-element.237), channel_id=1, source_target_pairs={{0,32},{8,40},{16,48},{24,56},{32,0},{40,8},{48,16},{56,24},{64,96... | collective-permute-start | bytes 1966088 | tf_op jit(solution)/shard_map/ppermute | solution.py:357
  91.7 16.7 %collective-permute-start.25 = (bf16[20,128,128]{2,1,0:T(8,128)(2,1)S(1)}, bf16[20,128,128]{2,1,0:T(8,128)(2,1)S(1)}, u32[]{:S(2)}, u32[]{:S(2)}) collective-permute-start(bf16[20,128,128]{2,1,0:T(8,128)(2,1)S(1)} %get-tuple-element.240), channel_id=1, source_target_pairs={{0,96},{8,104},{16,112},{24,120},{32,64},{40,72},{48,80},{56,88},{... | collective-permute-start | bytes 1966088 | tf_op jit(solution)/shard_map/ppermute | solution.py:357
  96.7 13.1 %collective-permute-start.26 = (bf16[16,128,128]{2,1,0:T(8,128)(2,1)S(1)}, bf16[16,128,128]{2,1,0:T(8,128)(2,1)S(1)}, u32[]{:S(2)}, u32[]{:S(2)}) collective-permute-start(bf16[16,128,128]{2,1,0:T(8,128)(2,1)S(1)} %get-tuple-element.243), channel_id=1, source_target_pairs={{0,16},{8,24},{16,0},{24,8},{32,48},{40,56},{48,32},{56,40},{64,80... | collective-permute-start | bytes 1572872 | tf_op jit(solution)/shard_map/ppermute | solution.py:357
  105.2 10.4 %collective-permute-start.27 = (bf16[10,128,128]{2,1,0:T(8,128)(2,1)S(1)}, bf16[10,128,128]{2,1,0:T(8,128)(2,1)S(1)}, u32[]{:S(2)}, u32[]{:S(2)}) collective-permute-start(bf16[10,128,128]{2,1,0:T(8,128)(2,1)S(1)} %get-tuple-element.246), channel_id=1, source_target_pairs={{0,96},{8,104},{16,112},{24,120},{32,64},{40,72},{48,80},{56,88},{... | collective-permute-start | bytes 983048 | tf_op jit(solution)/shard_map/ppermute | solution.py:357
  108.6 10.7 %collective-permute-start.29 = (bf16[10,128,128]{2,1,0:T(8,128)(2,1)S(1)}, bf16[10,128,128]{2,1,0:T(8,128)(2,1)S(1)}, u32[]{:S(2)}, u32[]{:S(2)}) collective-permute-start(bf16[10,128,128]{2,1,0:T(8,128)(2,1)S(1)} %get-tuple-element.250), channel_id=1, source_target_pairs={{0,16},{8,24},{16,0},{24,8},{32,48},{40,56},{48,32},{56,40},{64,80... | collective-permute-start | bytes 983048 | tf_op jit(solution)/shard_map/ppermute | solution.py:357
  110.0 10.7 %collective-permute-start.31 = (bf16[8,128,128]{2,1,0:T(8,128)(2,1)S(1)}, bf16[8,128,128]{2,1,0:T(8,128)(2,1)S(1)}, u32[]{:S(2)}, u32[]{:S(2)}) collective-permute-start(bf16[8,128,128]{2,1,0:T(8,128)(2,1)S(1)} %get-tuple-element.254), channel_id=1, source_target_pairs={{0,32},{8,40},{16,48},{24,56},{32,0},{40,8},{48,16},{56,24},{64,96... | collective-permute-start | bytes 786440 | tf_op jit(solution)/shard_map/ppermute | solution.py:357
  110.2 11.8 %collective-permute-start.35 = (bf16[6,128,128]{2,1,0:T(8,128)(2,1)S(1)}, bf16[6,128,128]{2,1,0:T(8,128)(2,1)S(1)}, u32[]{:S(2)}, u32[]{:S(2)}) collective-permute-start(bf16[6,128,128]{2,1,0:T(8,128)(2,1)S(1)} %get-tuple-element.260), channel_id=1, source_target_pairs={{0,32},{8,40},{16,48},{24,56},{32,0},{40,8},{48,16},{56,24},{64,96... | collective-permute-start | bytes 589832 | tf_op jit(solution)/shard_map/ppermute | solution.py:357
  112.1 12.3 %collective-permute-start.34 = (bf16[6,128,128]{2,1,0:T(8,128)(2,1)S(1)}, bf16[6,128,128]{2,1,0:T(8,128)(2,1)S(1)}, u32[]{:S(2)}, u32[]{:S(2)}) collective-permute-start(bf16[6,128,128]{2,1,0:T(8,128)(2,1)S(1)} %get-tuple-element.259), channel_id=1, source_target_pairs={{0,16},{8,24},{16,0},{24,8},{32,48},{40,56},{48,32},{56,40},{64,80... | collective-permute-start | bytes 589832 | tf_op jit(solution)/shard_map/ppermute | solution.py:357
  115.7 8.8 %collective-permute-start.33 = (bf16[6,128,128]{2,1,0:T(8,128)(2,1)S(1)}, bf16[6,128,128]{2,1,0:T(8,128)(2,1)S(1)}, u32[]{:S(2)}, u32[]{:S(2)}) collective-permute-start(bf16[6,128,128]{2,1,0:T(8,128)(2,1)S(1)} %get-tuple-element.258), channel_id=1, source_target_pairs={{0,96},{8,104},{16,112},{24,120},{32,64},{40,72},{48,80},{56,88},{... | collective-permute-start | bytes 589832 | tf_op jit(solution)/shard_map/ppermute | solution.py:357
  119.4 6.7 %collective-permute-start.28 = (bf16[5,128,128]{2,1,0:T(8,128)(2,1)S(1)}, bf16[5,128,128]{2,1,0:T(8,128)(2,1)S(1)}, u32[]{:S(2)}, u32[]{:S(2)}) collective-permute-start(bf16[5,128,128]{2,1,0:T(8,128)(2,1)S(1)} %get-tuple-element.248), channel_id=1, source_target_pairs={{0,16},{8,24},{16,0},{24,8},{32,48},{40,56},{48,32},{56,40},{64,80... | collective-permute-start | bytes 491528 | tf_op jit(solution)/shard_map/ppermute | solution.py:357
  120.7 7.5 %collective-permute-start.30 = (bf16[5,128,128]{2,1,0:T(8,128)(2,1)S(1)}, bf16[5,128,128]{2,1,0:T(8,128)(2,1)S(1)}, u32[]{:S(2)}, u32[]{:S(2)}) collective-permute-start(bf16[5,128,128]{2,1,0:T(8,128)(2,1)S(1)} %get-tuple-element.252), channel_id=1, source_target_pairs={{0,32},{8,40},{16,48},{24,56},{32,0},{40,8},{48,16},{56,24},{64,96... | collective-permute-start | bytes 491528 | tf_op jit(solution)/shard_map/ppermute | solution.py:357
  122.0 6.2 %collective-permute-start.32 = (bf16[4,128,128]{2,1,0:T(8,128)(2,1)S(1)}, bf16[4,128,128]{2,1,0:T(8,128)(2,1)S(1)}, u32[]{:S(2)}, u32[]{:S(2)}) collective-permute-start(bf16[4,128,128]{2,1,0:T(8,128)(2,1)S(1)} %get-tuple-element.256), channel_id=1, source_target_pairs={{0,96},{8,104},{16,112},{24,120},{32,64},{40,72},{48,80},{56,88},{... | collective-permute-start | bytes 393224 | tf_op jit(solution)/shard_map/ppermute | solution.py:357
  (2 other events, 2.4 us)
